TPU v7x, 512 devices: a whole 4x4x16 slice. The times are simulated.
512 devices in a mesh: seq: 128 (over y, x, z_lo), slide: 4 (over z_hi, core).
Axes of the slice: x: 4, y: 4, z: 16 (z_hi: 2, z_lo: 8; z = z_hi * 8 + z_lo), core: 2. Of those that a mesh axis runs over, the one named last changes fastest.
Arguments:
- tiles: bfloat16 [4, 16384, 1536], P('slide', 'seq'), may hold values from -25 to 25
- counts: int32 [4, 128], P('slide', 'seq'), may hold values from 1 to 128
- w_in: bfloat16 [1536, 768], P('slide'), may hold values from -0.15625 to 0.15625
- w_qkv: bfloat16 [768, 2304], P(None, 'slide'), may hold values from -0.5 to 0.5
- w_out: bfloat16 [768, 768], P(None, 'slide'), may hold values from -0.21875 to 0.21875
- cotangent: bfloat16 [4, 16384, 768], P('slide', 'seq'), may hold values from -6 to 6
Outputs:
- slide_out: float32 [4, 16384, 768], P('slide', 'seq')
- grad_out: float32 [768, 768], P('slide')
Inputs may be any that keep to these rules, and one draw needn't show every extreme that they name: `counts`: every device holds at least one tissue tile, in its first slots.
All inputs are finite; a program needn't handle non-finite values.
Results may differ from a plain program's by a relative error of at most 0.0095.
Values may be sent and summed in bfloat16 or wider, within the bound.
No kernel may reach another device: no remote copies, remote signals or barrier semaphores. Data moves between devices by JAX's collectives and lax.ppermute only.
A program may use at most 64 MiB of HBM per device.

v0:
```python
import jax
import jax.numpy as jnp
from jax import lax
from jax.sharding import PartitionSpec as P

ENCODER_WIDTH = 768
HEADS = 16
HEAD = 48
SLIDE_DILATION = 32


def from_partner(value, axis, distance):
    mask = 2**distance
    pairs = [(source, source ^ mask) for source in range(lax.axis_size(axis))]
    return lax.ppermute(value, axis, pairs)


def fold_level(carry, query, key_matrix, value_matrix, valid_mask):
    top, total, mixed = carry
    kh = key_matrix.reshape(key_matrix.shape[0], HEADS, HEAD)
    vh = value_matrix.reshape(value_matrix.shape[0], HEADS, HEAD)
    scores = jnp.einsum("thd,khd->thk", query, kh, preferred_element_type=jnp.float32) * HEAD ** (
        -0.5
    )
    scores = jnp.where(valid_mask[None, None, :] > 0, scores, jnp.float32(-1e30))
    new_top = jnp.maximum(top, jnp.max(scores, axis=-1))
    factor = jnp.exp(top - new_top)
    weights = jnp.exp(scores - new_top[..., None])
    total = total * factor + jnp.sum(weights, axis=-1)
    part = jnp.einsum(
        "thk,khd->thd", weights.astype(jnp.bfloat16), vh, preferred_element_type=jnp.float32
    )
    mixed = mixed * factor[..., None] + part
    return (new_top, total, mixed)


def shards(tiles, counts, w_in, w_qkv, w_out, cotangent):
    rows = tiles[0]
    count = counts[0, 0]
    token_rows = rows.shape[0]
    hidden = jnp.dot(
        rows, lax.all_gather(w_in, "slide", axis=0, tiled=True), preferred_element_type=jnp.float32
    ).astype(jnp.bfloat16)
    qkv = jnp.dot(
        hidden,
        lax.all_gather(w_qkv, "slide", axis=1, tiled=True),
        preferred_element_type=jnp.float32,
    ).astype(jnp.bfloat16)
    query = qkv[:, :ENCODER_WIDTH].reshape(token_rows, HEADS, HEAD)
    key_matrix, value_matrix = (
        qkv[:, ENCODER_WIDTH : 2 * ENCODER_WIDTH],
        qkv[:, 2 * ENCODER_WIDTH :],
    )
    slot = jnp.arange(token_rows, dtype=jnp.int32)
    valid_mask = (slot < count).astype(jnp.bfloat16)
    carry = (
        jnp.full((token_rows, HEADS), -1e30, jnp.float32),
        jnp.zeros((token_rows, HEADS), jnp.float32),
        jnp.zeros((token_rows, HEADS, HEAD), jnp.float32),
    )
    carry = fold_level(carry, query, key_matrix, value_matrix, valid_mask)
    even_k, even_v, even_m = (key_matrix[0::2], value_matrix[0::2], valid_mask[0::2])
    carry = fold_level(carry, query, even_k, even_v, even_m)
    part_k, part_v, part_m = from_partner((even_k, even_v, even_m), "seq", 0)
    carry = fold_level(carry, query, part_k, part_v, part_m)
    dilated_keys = key_matrix.reshape(token_rows // SLIDE_DILATION, SLIDE_DILATION, ENCODER_WIDTH)[
        :, 0
    ]
    dilated_values = value_matrix.reshape(
        token_rows // SLIDE_DILATION, SLIDE_DILATION, ENCODER_WIDTH
    )[:, 0]
    dilated_mask = valid_mask.reshape(token_rows // SLIDE_DILATION, SLIDE_DILATION)[:, 0]
    distant_keys, distant_values, distant_mask = (
        lax.all_gather(dilated_keys, "seq", axis=0, tiled=True),
        lax.all_gather(dilated_values, "seq", axis=0, tiled=True),
        lax.all_gather(dilated_mask, "seq", axis=0, tiled=True),
    )
    far_count = distant_keys.shape[0]
    key_block = 256
    stacked = (
        distant_keys.reshape(far_count // key_block, key_block, ENCODER_WIDTH),
        distant_values.reshape(far_count // key_block, key_block, ENCODER_WIDTH),
        distant_mask.reshape(far_count // key_block, key_block),
    )

    def add_far(state, piece):
        return (fold_level(state, query, piece[0], piece[1], piece[2]), None)

    carry, _ = lax.scan(add_far, carry, stacked)
    top, total, mixed = carry
    attn = (mixed / total[..., None]).reshape(token_rows, ENCODER_WIDTH).astype(jnp.bfloat16)
    out = jnp.dot(
        attn, lax.all_gather(w_out, "slide", axis=1, tiled=True), preferred_element_type=jnp.float32
    )
    masked = jnp.where(valid_mask[:, None] > 0, attn, jnp.zeros_like(attn))
    cot = cotangent[0]
    share = ENCODER_WIDTH // lax.axis_size("slide")
    whole = lax.psum(jnp.dot(masked.T, cot, preferred_element_type=jnp.float32), ("seq", "slide"))
    grad = lax.dynamic_slice_in_dim(whole, lax.axis_index("slide") * share, share, 0)
    return (out[None], grad)


def solution(mesh):
    placed = (
        P("slide", "seq", None),
        P("slide", "seq"),
        P("slide", None),
        P(None, "slide"),
        P(None, "slide"),
        P("slide", "seq", None),
    )
    return jax.shard_map(
        shards,
        mesh=mesh,
        in_specs=placed,
        out_specs=(P("slide", "seq", None), P("slide", None)),
        check_vma=False,
    )
```

profile of v0, /device:TPU:2, one launch (start us, length us, event | category | flops | bytes accessed | tf_op | source)
XLA Modules:
  0.0 2198.7 jit_solution(17527662771240233205)
XLA Ops:
  7.2 0.7 all-gather.7.cloned.1.call-update
  8.0 0.7 all-gather.9.cloned.1.call-update
  9.5 3.8 collective-permute-start
  13.5 1.3 dynamic-slice
  15.7 528.2 %all-reduce = bf16[512]{0:T(512)(128)(2,1)S(1)} all-reduce(bf16[512]{0:T(512)(128)(2,1)S(1)} %dynamic-update-slice), channel_id=2, replica_groups=mesh['seq'=128,'slide'=4] {'seq'}, use_global_device_ids=true, to_apply=%add | all-reduce | flops 512 | bytes 2048
  543.9 4.2 convolution_convert_fusion
  548.4 0.8 copy.34
  549.2 1.9 collective-permute-start.1
  551.1 0.8 copy.46
  552.1 0.8 slice.33
  552.8 4.0 collective-permute-start.2
  556.9 524.0 %all-gather.1 = bf16[512,1,768]{2,1,0:T(2,128)(2,1)S(1)} all-gather(bf16[4,1,768]{2,1,0:T(2,128)(2,1)S(1)} %slice.40), channel_id=3, replica_groups=mesh['seq'=128,'slide'=4] {'seq'}, dimensions={0}, use_global_device_ids=true | all-gather | bytes 792576 | tf_op jit(solution)/shard_map/all_gather | solution.py:74
  1080.9 544.7 %all-gather.2 = bf16[512,1,768]{2,1,0:T(2,128)(2,1)} all-gather(bf16[4,1,768]{2,1,0:T(2,128)(2,1)S(1)} %slice.41), channel_id=4, replica_groups=mesh['seq'=128,'slide'=4] {'seq'}, dimensions={0}, use_global_device_ids=true | all-gather | bytes 792576 | tf_op jit(solution)/shard_map/all_gather | solution.py:75
  1626.1 1.1 fusion.45
  1627.2 0.8 copy.38
  1628.0 1.7 copy.48
  1629.7 1.0 copy.52
  1630.7 0.7 copy-done.1
  1631.4 1.0 copy.53
  1632.4 1.1 copy.47
  1635.0 1.1 copy.49
  1636.0 1.1 fusion.17
  1637.1 10.2 while.14
  1637.1 1.2 constant_dynamic-slice_fusion.4
  1639.8 2.5 fusion.75
  1642.2 1.2 constant_dynamic-slice_fusion.4
  1644.9 2.5 fusion.75
  1647.4 1.1 broadcast_select_fusion
  1648.4 2.8 fusion.37
  1651.3 2.5 convolution_bitcast_fusion.1
  1653.8 536.4 %all-reduce.3.cloned.1.call-done = f32[768,768]{1,0:T(8,128)} async-done(((f32[768,768]{1,0:T(8,128)}), f32[768,768]{1,0:T(8,128)}) %all-reduce.3.cloned.1.call-update) | async-done | bytes 2359312 | tf_op jit(solution)/shard_map/psum | solution.py:98
  2190.2 1.9 constant_dynamic-slice_fusion.2
  (63 shorter events, 5.8 us)
Async XLA Ops:
  7.2 536.7 %copy-start = (bf16[1,128,1536]{2,1,0:T(8,128)(2,1)S(1)}, bf16[1,128,1536]{2,1,0:T(8,128)(2,1)}, u32[]{:S(2)}) copy-start(bf16[1,128,1536]{2,1,0:T(8,128)(2,1)} %param.8) | copy-start | bytes 1179652
  7.2 536.7 %all-gather.7.cloned.1.call-start = ((), (), s32[]{:S(2)}) async-start(), calls=%async_computation | async-start | bytes 2949120 | tf_op jit(solution)/shard_map/all_gather | solution.py:42
  7.9 536.0 %all-gather.9.cloned.1.call-start = ((), (), s32[]{:S(2)}) async-start(), calls=%async_computation.1 | async-start | bytes 4423680 | tf_op jit(solution)/shard_map/all_gather | solution.py:46
  8.7 1642.6 %all-gather.11.cloned.1.call-start = ((), (), s32[]{:S(2)}) async-start(), calls=%async_computation.2 | async-start | bytes 1474560 | tf_op jit(solution)/shard_map/all_gather | solution.py:93
  9.5 534.3 %collective-permute-start = (bf16[64]{0:T(256)(128)(2,1)S(1)}, bf16[64]{0:T(256)(128)(2,1)S(1)}, u32[]{:S(2)}, u32[]{:S(2)}) collective-permute-start(bf16[64]{0:T(256)(128)(2,1)S(1)} %slice.30), channel_id=1, source_target_pairs={{0,4},{4,0},{8,12},{12,8},{16,20},{20,16},{24,28},{28,24},{32,36},... | collective-permute-start | bytes 392 | tf_op jit(solution)/shard_map/ppermute | solution.py:15
  13.4 2176.8 %all-reduce.3.cloned.1.call-start = ((), (), s32[]{:S(2)}) async-start(), calls=%async_computation.3 | async-start | bytes 4718592 | tf_op jit(solution)/shard_map/psum | solution.py:98
  549.2 1083.2 %collective-permute-start.1 = (bf16[64,768]{1,0:T(8,128)(2,1)S(1)}, bf16[64,768]{1,0:T(8,128)(2,1)}, u32[]{:S(2)}, u32[]{:S(2)}) collective-permute-start(bf16[64,768]{1,0:T(8,128)(2,1)S(1)} %slice.31), channel_id=1, source_target_pairs={{0,4},{4,0},{8,12},{12,8},{16,20},{20,16},{24,28},{28,24},{32,36},... | collective-permute-start | bytes 294920 | tf_op jit(solution)/shard_map/ppermute | solution.py:15
  552.8 1072.9 %copy-start.6 = (bf16[128,768]{0,1:T(8,128)(2,1)S(1)}, bf16[128,768]{0,1:T(8,128)(2,1)}, u32[]{:S(2)}) copy-start(bf16[128,768]{0,1:T(8,128)(2,1)} %copy.34) | copy-start | bytes 589828
  552.8 1082.2 %collective-permute-start.2 = (bf16[64,768]{1,0:T(8,128)(2,1)}, bf16[64,768]{1,0:T(8,128)(2,1)}, u32[]{:S(2)}, u32[]{:S(2)}) collective-permute-start(bf16[64,768]{1,0:T(8,128)(2,1)} %slice.33), channel_id=1, source_target_pairs={{0,4},{4,0},{8,12},{12,8},{16,20},{20,16},{24,28},{28,24},{32,36},... | collective-permute-start | bytes 294920 | tf_op jit(solution)/shard_map/ppermute | solution.py:15
  556.9 1069.2 %copy-start.5 = (bf16[64,768]{0,1:T(8,128)(2,1)S(1)}, bf16[64,768]{0,1:T(8,128)(2,1)}, u32[]{:S(2)}) copy-start(bf16[64,768]{0,1:T(8,128)(2,1)} %copy.46) | copy-start | bytes 294916
  1629.7 1.7 copy-start.1
  1631.4 2.6 copy-start.2
  1632.4 1.9 copy-start.4
  1633.8 0.9 copy-start.3
Sparse Core Ops, SparseCore 0:
  10.1 87.0 all-gather.6
  99.4 99.8 all-gather.8
  201.4 47.7 all-gather.10
  1651.4 538.8 all-reduce.2
where the time goes:
time: 2200 us
  blocking collectives  1600 us (73%)
  waiting for transfers between devices  538 us (24%)
    all_gather x1, blocking collectives, shards(): lax.all_gather(dilated_values, 'seq', axis=0, tiled=True)  545 us
    psum x1, waiting for transfers between devices, shards(): lax.psum(jnp.dot(masked.T, cot, preferred_element_type=jnp.float32), ('se...  536 us
    unnamed x1, blocking collectives  528 us
    all_gather x1, blocking collectives, shards(): lax.all_gather(dilated_keys, 'seq', axis=0, tiled=True)  524 us
  transfers between devices with their start and end apart: 7, of which 1 were waited for; matrix products, arithmetic and copies ran while one was open for 2% of the time, Pallas kernels for 0%

commit v1 on v0

v1 whole, which is shorter than its diff:
```python
import functools

import jax
import jax.numpy as jnp
from jax import lax
from jax.experimental import pallas as pl
from jax.experimental.pallas import tpu as pltpu
from jax.sharding import Mesh
from jax.sharding import PartitionSpec as P

WIDTH = 768
HEADS = 16
HEAD = 48
DIL = 32
TOK = 128
PIECE = 64
YX = ("y", "x")
NT = (((1,), (1,)), ((), ()))
NN = (((1,), (0,)), ((), ()))
BF = jnp.bfloat16
F32 = jnp.float32


def layer_kernel(
    scal,
    rows,
    even,
    partner,
    w_in,
    w_qkv,
    mate_in,
    mate_qkv,
    got,
    cross,
    w_out,
    cot,
    out,
    keep,
    send,
    near,
    far,
    marks,
    win,
    wqkv,
    hid,
    kv,
    mixed,
    attn,
    sems,
):
    count, pcount, zh, core = scal[0], scal[1], scal[2], scal[3]
    mine = zh * 2 + core
    mate = zh * 2 + 1 - core
    over = (1 - zh) * 2 + core
    over_mate = (1 - zh) * 2 + 1 - core
    moves = [
        (rows, near.at[pl.ds(0, TOK)]),
        (even, near.at[pl.ds(TOK, TOK // 2)]),
        (partner, near.at[pl.ds(TOK + TOK // 2, TOK // 2)]),
        (got.at[:, pl.ds(PIECE, 64)], far),
        (got.at[:, pl.ds(PIECE + 64, 16)], marks),
        (w_in, win.at[mine]),
        (mate_in, win.at[mate]),
        (got.at[pl.ds(0, 6), pl.ds(0, PIECE)], win.at[over]),
        (cross.at[pl.ds(0, 6)], win.at[over_mate]),
        (w_qkv, wqkv.at[mine]),
        (mate_qkv, wqkv.at[mate]),
        (got.at[pl.ds(6, 9), pl.ds(0, PIECE)], wqkv.at[over]),
        (cross.at[pl.ds(6, 9)], wqkv.at[over_mate]),
    ]
    copies = [pltpu.make_async_copy(s, d, sems.at[i]) for i, (s, d) in enumerate(moves)]
    for c in copies:
        c.start()
    for c in copies[:9]:
        c.wait()
    weight = win[...].reshape(1536, WIDTH)
    hid[pl.ds(0, 256), :] = lax.dot_general(
        near[...], weight, NN, preferred_element_type=F32
    ).astype(BF)
    left = far[:, pl.ds(0, 32), :].reshape(512, WIDTH)
    right = far[:, pl.ds(32, 32), :].reshape(512, WIDTH)
    hid[pl.ds(256, 512), :] = (
        lax.dot_general(left, weight[:WIDTH], NN, preferred_element_type=F32)
        + lax.dot_general(right, weight[WIDTH:], NN, preferred_element_type=F32)
    ).astype(BF)
    for c in copies[9:]:
        c.wait()
    kv[...] = lax.dot_general(
        wqkv[...].reshape(3 * WIDTH, WIDTH)[WIDTH:], hid[...], NT, preferred_element_type=F32
    ).astype(BF)
    seen = jnp.sum(marks[...].astype(F32), axis=(0, 1)).reshape(1, WIDTH)[:, :512]
    lane = lax.broadcasted_iota(jnp.int32, (1, 256), 1)
    offset = jnp.where(lane < TOK, lane, 2 * (lane & 63))
    limit = jnp.where(lane < TOK + TOK // 2, count, pcount)
    near_bias = jnp.where(offset < limit, F32(0), F32(-1e30))
    far_bias = jnp.where(seen > 0.5, F32(0), F32(-1e30))
    bias = jnp.concatenate([near_bias, far_bias], axis=1)
    column = lax.broadcasted_iota(jnp.int32, (TOK, TOK), 1)
    totals = jnp.ones((TOK, TOK), F32)
    own = hid[pl.ds(0, TOK), :]
    flat = wqkv[...].reshape(3 * WIDTH, WIDTH)
    for h in range(HEADS):
        q = lax.dot_general(
            own, flat[h * HEAD : (h + 1) * HEAD], NT, preferred_element_type=F32
        ).astype(BF)
        s = lax.dot_general(
            q, kv[pl.ds(h * HEAD, HEAD), :], NN, preferred_element_type=F32
        )
        s = s * F32(HEAD**-0.5) + bias
        top = jnp.max(s, axis=1, keepdims=True)
        p = jnp.exp(s - top)
        totals = jnp.where(column == h, jnp.sum(p, axis=1, keepdims=True), totals)
        mixed[pl.ds(h * HEAD, HEAD), :] = lax.dot_general(
            kv[pl.ds(WIDTH + h * HEAD, HEAD), :], p.astype(BF), NT, preferred_element_type=F32
        )
    inverse = 1.0 / totals.T
    for h in range(HEADS):
        attn[pl.ds(h * HEAD, HEAD), :] = (
            mixed[pl.ds(h * HEAD, HEAD), :] * inverse[h : h + 1, :]
        ).astype(BF)
    cotangent = cot[...]
    token = lax.broadcasted_iota(jnp.int32, (192, TOK), 1)
    for which, target in ((core, keep), (1 - core, send)):
        for half in range(2):
            start = pl.multiple_of(half * 384 + which * 192, 192)
            block = attn[pl.ds(start, 192), :]
            block = jnp.where(token < count, block, jnp.zeros_like(block))
            part = lax.dot_general(block, cotangent, NN, preferred_element_type=F32)
            for r in range(8):
                for c in range(2):
                    target[r * 2 + c, half] = part[r * 24 : r * 24 + 24, c * 384 : c * 384 + 384]
    out_t = lax.dot_general(w_out[...], attn[...], NN, preferred_element_type=F32)
    out[...] = out_t.T


def layer(*operands, interpret=False):
    any_spec = pl.BlockSpec(memory_space=pl.ANY)
    vmem = pl.BlockSpec(memory_space=pltpu.VMEM)
    part = jax.ShapeDtypeStruct((16, 2, 24, 384), F32)
    return pl.pallas_call(
        layer_kernel,
        out_shape=(jax.ShapeDtypeStruct((TOK, WIDTH), F32), part, part),
        in_specs=[pl.BlockSpec(memory_space=pltpu.SMEM)] + [any_spec] * 9 + [vmem] * 2,
        out_specs=(vmem, vmem, vmem),
        scratch_shapes=[
            pltpu.VMEM((256, 1536), BF),
            pltpu.VMEM((16, 64, WIDTH), BF),
            pltpu.VMEM((16, 16, WIDTH), BF),
            pltpu.VMEM((4, 6, PIECE, WIDTH), BF),
            pltpu.VMEM((4, 9, PIECE, WIDTH), BF),
            pltpu.VMEM((WIDTH, WIDTH), BF),
            pltpu.VMEM((2 * WIDTH, WIDTH), BF),
            pltpu.VMEM((WIDTH, TOK), F32),
            pltpu.VMEM((WIDTH, TOK), BF),
            pltpu.SemaphoreType.DMA((13,)),
        ],
        compiler_params=pltpu.CompilerParams(vmem_limit_bytes=48 * 1024 * 1024),
        interpret=interpret,
    )(*operands)


def spread(block, axes, size):
    return lax.all_to_all(
        jnp.broadcast_to(block[None], (size,) + block.shape), axes, 0, 0, tiled=True
    )


def swap(value, axis):
    return lax.ppermute(value, axis, [(0, 1), (1, 0)])


def shards(tiles, counts, w_in, w_qkv, w_out, cotangent):
    rows = tiles[0]
    count = counts[0, 0]
    yx = lax.axis_index("y") * 4 + lax.axis_index("x")
    zl, zh, core = lax.axis_index("zl"), lax.axis_index("zh"), lax.axis_index("core")
    w_in = w_in.reshape(6, PIECE, WIDTH)
    w_qkv = w_qkv.T.reshape(9, PIECE, WIDTH)
    piece = jnp.where(
        yx < 6,
        lax.dynamic_index_in_dim(w_in, jnp.minimum(yx, 5), 0, False),
        lax.dynamic_index_in_dim(w_qkv, jnp.clip(yx - 6, 0, 8), 0, False),
    )
    piece = swap(piece, "zh")
    even = rows[0::2]
    partner = lax.ppermute(even, "zl", [(i, i ^ 1) for i in range(8)])
    mate_in, mate_qkv = swap(w_in, "core"), swap(w_qkv, "core")
    out_w = lax.all_gather(w_out.T, ("zh", "core"), axis=0, tiled=True)
    distant = rows[0::DIL]
    lane = lax.broadcasted_iota(jnp.int32, (1, WIDTH), 1)
    local = lane - (yx * 32 + zl * 4)
    mark = (local >= 0) & (local < 4) & (local * DIL < count)
    mark = jnp.where(lane == 512, count.astype(BF), mark.astype(BF))
    block = jnp.concatenate(
        [distant[:, :WIDTH], distant[:, WIDTH:], mark, jnp.zeros((7, WIDTH), BF)], axis=0
    )
    line = spread(block, "zl", 8)
    pcount = lax.dynamic_slice(line, (zl ^ 1, 8, 512), (1, 1, 1))[0, 0, 0].astype(jnp.int32)
    payload = jnp.concatenate(
        [
            piece,
            line[:, 0:4].reshape(32, WIDTH),
            line[:, 4:8].reshape(32, WIDTH),
            line[:, 8],
            jnp.zeros((8, WIDTH), BF),
        ],
        axis=0,
    )
    got = spread(payload, YX, 16)
    cross = swap(got[:15, :PIECE], "core")
    scal = jnp.stack([count, pcount, zh, core]).astype(jnp.int32)
    out, keep, send = layer(
        scal, rows, even, partner, w_in, w_qkv, mate_in, mate_qkv, got, cross, out_w, cotangent[0]
    )
    pair = (keep + swap(send, "core")).astype(BF)
    plane = lax.all_to_all(pair, YX, 0, 0, tiled=True)
    plane = jnp.sum(plane.astype(F32), axis=0).astype(BF)
    column = jnp.broadcast_to(plane[:, None], (2, 8, 24, 384)).reshape(16, 24, 384)
    column = lax.all_to_all(column, ("zh", "zl"), 0, 0, tiled=True)
    total = jnp.sum(column.astype(F32), axis=0)
    whole = spread(total, YX, 16)
    grad = whole.reshape(8, 2, 24, 384).transpose(0, 2, 1, 3).reshape(192, WIDTH)
    return (out[None], grad)


def solution(mesh):
    fine = Mesh(mesh.devices.reshape(4, 4, 8, 2, 2), ("y", "x", "zl", "zh", "core"))
    seq, slide = ("y", "x", "zl"), ("zh", "core")
    placed = (
        P(slide, seq, None),
        P(slide, seq),
        P(slide, None),
        P(None, slide),
        P(None, slide),
        P(slide, seq, None),
    )
    return jax.shard_map(
        shards,
        mesh=fine,
        in_specs=placed,
        out_specs=(P(slide, seq, None), P(slide, None)),
        check_vma=False,
    )
```

time: 2200 us -> 217 us (0.10)
  the two profiles are of different devices: /device:TPU:2 before, /device:TPU:32 now
where the time goes in v1:
time: 217 us; the launch traced here: 216 us
  blocking collectives  70.6 us (33%)
  waiting for transfers between devices  60.2 us (28%)
  starting transfers between devices  41.2 us (19%)
  Pallas kernels  16.9 us (8%)
  between operations  15.6 us (7%)
  local copies, waits for them, and re-layouts  10.4 us (5%)
    all_to_all x2, waiting for transfers between devices, spread(): lax.all_to_all(jnp.broadcast_to(block[None], (size,) + block.shape), axes...  44.3 us
    all_to_all x1, blocking collectives, shards(): column = lax.all_to_all(column, ('zh', 'zl'), 0, 0, tiled=True)  40.2 us
    all_to_all x2, starting transfers between devices, spread(): lax.all_to_all(jnp.broadcast_to(block[None], (size,) + block.shape), axes...  19.7 us
    pallas_call x1, Pallas kernels, layer(): pl.pallas_call(layer_kernel, out_shape=(jax.ShapeDtypeStruct((TOK, WIDTH)...  16.9 us
    ppermute x5, starting transfers between devices, swap(): return lax.ppermute(value, axis, [(0, 1), (1, 0)])  16.4 us
    all_to_all x1, blocking collectives, shards(): plane = lax.all_to_all(pair, YX, 0, 0, tiled=True)  16.1 us
    all_to_all x1, blocking collectives, spread(): lax.all_to_all(jnp.broadcast_to(block[None], (size,) + block.shape), axes...  14.3 us
    ppermute x5, waiting for transfers between devices, swap(): return lax.ppermute(value, axis, [(0, 1), (1, 0)])  11.5 us
  transfers between devices with their start and end apart: 9, of which 4 were waited for; matrix products, arithmetic and copies ran while one was open for 2% of the time, Pallas kernels for 0%

profile of v1, /device:TPU:32, one launch (start us, length us, event | category | flops | bytes accessed | tf_op | source)
XLA Modules:
  0.0 216.4 jit_solution(7963103906282135127)
XLA Ops:
  7.8 1.0 slice.24
  8.9 0.1 pad.7.clone
  9.0 0.1 maximum_maximum_fusion
  9.1 0.7 broadcast_in_dim.20
  9.8 12.6 %all-to-all-start = ((bf16[8,16,768]{2,1,0:T(8,128)(2,1)}), bf16[8,16,768]{2,1,0:T(8,128)(2,1)S(1)}, u32[]{:S(2)}, u32[]{:S(2)}) async-start(bf16[8,16,768]{2,1,0:T(8,128)(2,1)} %broadcast_in_dim.20), calls=%async_computation | async-start | bytes 393216 | tf_op jit(solution)/shard_map/all_to_all | solution.py:163
  22.4 1.0 select_bitcast_fusion
  23.3 8.2 %collective-permute-start.3 = (bf16[64,768]{1,0:T(8,128)(2,1)S(1)}, bf16[64,768]{1,0:T(8,128)(2,1)S(1)}, u32[]{:S(2)}, u32[]{:S(2)}) collective-permute-start(bf16[64,768]{1,0:T(8,128)(2,1)S(1)} %select_bitcast_fusion), channel_id=1, source_target_pairs={{0,2},{2,0},{1,3},{3,1},{4,6},{6,4},{5,7},{7,5},{8,10},{10,8},{9,1... | collective-permute-start | bytes 294920 | tf_op jit(solution)/shard_map/ppermute | solution.py:169
  31.6 8.5 %collective-permute-done.3 = bf16[64,768]{1,0:T(8,128)(2,1)S(1)} collective-permute-done((bf16[64,768]{1,0:T(8,128)(2,1)S(1)}, bf16[64,768]{1,0:T(8,128)(2,1)S(1)}, u32[]{:S(2)}, u32[]{:S(2)}) %collective-permute-start.3) | collective-permute-done | bytes 98336 | tf_op jit(solution)/shard_map/ppermute | solution.py:169
  40.3 2.0 broadcast_in_dim.41
  42.3 7.1 %all-to-all-start.1 = ((bf16[16,144,768]{2,1,0:T(8,128)(2,1)}), bf16[16,144,768]{2,1,0:T(8,128)(2,1)}, u32[]{:S(2)}, u32[]{:S(2)}) async-start(bf16[16,144,768]{2,1,0:T(8,128)(2,1)} %broadcast_in_dim.41), calls=%async_computation.1 | async-start | bytes 7077888 | tf_op jit(solution)/shard_map/all_to_all | solution.py:163
  49.4 0.7 all-gather.2.cloned.1.call-update
  50.2 44.3 %all-to-all-done.1.got = bf16[16,144,768]{2,1,0:T(8,128)(2,1)} async-done(((bf16[16,144,768]{2,1,0:T(8,128)(2,1)}), bf16[16,144,768]{2,1,0:T(8,128)(2,1)}, u32[]{:S(2)}, u32[]{:S(2)}) %all-to-all-start.1) | async-done | bytes 3538976 | tf_op jit(solution)/shard_map/all_to_all | solution.py:163
  94.5 2.7 %slice.37 = bf16[15,64,768]{2,1,0:T(8,128)(2,1)} slice(bf16[16,144,768]{2,1,0:T(8,128)(2,1)} %all-to-all-done.1.got), slice={[0:15], [0:64], [0:768]} | slice | bytes 2949120 | tf_op jit(solution)/shard_map/slice | solution.py:210
  97.1 1.9 collective-permute-start.4
  99.1 2.4 %collective-permute-start.2 = (bf16[9,64,768]{2,1,0:T(8,128)(2,1)S(1)}, bf16[9,64,768]{2,1,0:T(8,128)(2,1)S(1)}, u32[]{:S(2)}, u32[]{:S(2)}) collective-permute-start(bf16[9,64,768]{2,1,0:T(8,128)(2,1)S(1)} %bitcast.31), channel_id=1, source_target_pairs={{0,1},{1,0},{2,3},{3,2},{4,5},{5,4},{6,7},{7,6},{8,9},{9,8},{10,11... | collective-permute-start | bytes 2654216 | tf_op jit(solution)/shard_map/ppermute | solution.py:169
  101.5 1.9 collective-permute-start.1
  103.4 0.4 slice.27.even
  103.8 5.1 %collective-permute-start = (bf16[64,1536]{1,0:T(8,128)(2,1)S(1)}, bf16[64,1536]{1,0:T(8,128)(2,1)}, u32[]{:S(2)}, u32[]{:S(2)}) collective-permute-start(bf16[64,1536]{1,0:T(8,128)(2,1)S(1)} %slice.27.even), channel_id=1, source_target_pairs={{0,4},{4,0},{8,12},{12,8},{16,20},{20,16},{24,28},{28,24},{1,5},{5... | collective-permute-start | bytes 589832 | tf_op jit(solution)/shard_map/ppermute | solution.py:186
  108.9 1.2 constant_dynamic-slice_fusion
  110.8 0.1 pad_add_fusion.scal
  110.9 3.7 %collective-permute-done.partner = bf16[64,1536]{1,0:T(8,128)(2,1)} collective-permute-done((bf16[64,1536]{1,0:T(8,128)(2,1)S(1)}, bf16[64,1536]{1,0:T(8,128)(2,1)}, u32[]{:S(2)}, u32[]{:S(2)}) %collective-permute-start) | collective-permute-done | bytes 196640 | tf_op jit(solution)/shard_map/ppermute | solution.py:186
  114.6 0.9 copy-done.3
  115.5 16.9 %shard_map.77 = (f32[128,768]{1,0:T(8,128)}, f32[16,2,24,384]{3,2,1,0:T(8,128)S(1)}, f32[16,2,24,384]{3,2,1,0:T(8,128)}) custom-call(s32[4]{0:T(128)S(1)} %pad_add_fusion.scal, bf16[128,1536]{1,0:T(8,128)(2,1)S(1)} %bitcast.35, bf16[64,1536]{1,0:T(8,128)(2,1)S(1)} %slice.27.even, bf16[64,1536]{1,0:T(8,128)(2,1)} %collective-permute-done.partner, ...), custom_call_target="tpu_custom_call" | custom-call | tf_op jit(solution)/shard_map/pallas_call | solution.py:140
  132.4 1.9 collective-permute-start.5
  134.3 3.0 %collective-permute-done.5 = f32[16,2,24,384]{3,2,1,0:T(8,128)S(1)} collective-permute-done((f32[16,2,24,384]{3,2,1,0:T(8,128)}, f32[16,2,24,384]{3,2,1,0:T(8,128)S(1)}, u32[]{:S(2)}, u32[]{:S(2)}) %collective-permute-start.5) | collective-permute-done | bytes 1179680 | tf_op jit(solution)/shard_map/ppermute | solution.py:169
  137.4 0.2 add_convert_fusion
  137.5 16.1 %all_to_all.25 = bf16[16,2,24,384]{3,2,1,0:T(8,128)(2,1)S(1)} all-to-all(bf16[16,2,24,384]{3,2,1,0:T(8,128)(2,1)S(1)} %add_convert_fusion), channel_id=1, replica_groups=mesh['y'=4,'x'=4,'zl'=8,'zh'=2,'core'=2] {'y','x'}, dimensions={0} | all-to-all | bytes 1179648 | tf_op jit(solution)/shard_map/all_to_all | solution.py:216
  153.6 0.1 reduce_sum.21
  153.7 40.2 %all_to_all.26 = bf16[16,24,384]{2,1,0:T(8,128)(2,1)S(1)} all-to-all(bf16[16,24,384]{2,1,0:T(8,128)(2,1)S(1)} %bitcast.42), channel_id=1, replica_groups=mesh['y'=4,'x'=4,'zl'=8,'zh'=2,'core'=2] {'zh','zl'}, dimensions={0} | all-to-all | bytes 589824 | tf_op jit(solution)/shard_map/all_to_all | solution.py:219
  194.1 14.3 %all_to_all.27 = f32[16,24,384]{2,1,0:T(8,128)S(1)} all-to-all(f32[16,24,384]{2,1,0:T(8,128)S(1)} %broadcast_in_dim.44), channel_id=1, replica_groups=mesh['y'=4,'x'=4,'zl'=8,'zh'=2,'core'=2] {'y','x'}, dimensions={0} | all-to-all | bytes 1179648 | tf_op jit(solution)/shard_map/all_to_all | solution.py:163
  208.4 0.3 copy.16
  208.7 0.9 copy.18
  (30 shorter events, 0.4 us)
Async XLA Ops:
  9.8 30.3 %all-to-all-start = ((bf16[8,16,768]{2,1,0:T(8,128)(2,1)}), bf16[8,16,768]{2,1,0:T(8,128)(2,1)S(1)}, u32[]{:S(2)}, u32[]{:S(2)}) async-start(bf16[8,16,768]{2,1,0:T(8,128)(2,1)} %broadcast_in_dim.20), calls=%async_computation | async-start | bytes 393216 | tf_op jit(solution)/shard_map/all_to_all | solution.py:163
  23.3 16.7 %collective-permute-start.3 = (bf16[64,768]{1,0:T(8,128)(2,1)S(1)}, bf16[64,768]{1,0:T(8,128)(2,1)S(1)}, u32[]{:S(2)}, u32[]{:S(2)}) collective-permute-start(bf16[64,768]{1,0:T(8,128)(2,1)S(1)} %select_bitcast_fusion), channel_id=1, source_target_pairs={{0,2},{2,0},{1,3},{3,1},{4,6},{6,4},{5,7},{7,5},{8,10},{10,8},{9,1... | collective-permute-start | bytes 294920 | tf_op jit(solution)/shard_map/ppermute | solution.py:169
  40.1 2.2 %copy-start.4 = (bf16[8,16,768]{2,1,0:T(8,128)(2,1)}, bf16[8,16,768]{2,1,0:T(8,128)(2,1)S(1)}, u32[]{:S(2)}) copy-start(bf16[8,16,768]{2,1,0:T(8,128)(2,1)S(1)} %all-to-all-done) | copy-start | bytes 589828
  42.3 52.2 %all-to-all-start.1 = ((bf16[16,144,768]{2,1,0:T(8,128)(2,1)}), bf16[16,144,768]{2,1,0:T(8,128)(2,1)}, u32[]{:S(2)}, u32[]{:S(2)}) async-start(bf16[16,144,768]{2,1,0:T(8,128)(2,1)} %broadcast_in_dim.41), calls=%async_computation.1 | async-start | bytes 7077888 | tf_op jit(solution)/shard_map/all_to_all | solution.py:163
  49.4 65.2 %all-gather.2.cloned.1.call-start = ((), (), s32[]{:S(2)}) async-start(), calls=%async_computation.5 | async-start | bytes 1474560 | tf_op jit(solution)/shard_map/all_gather | solution.py:188
  50.1 48.9 %copy-start = (bf16[768,576]{0,1:T(8,128)(2,1)S(1)}, bf16[768,576]{0,1:T(8,128)(2,1)}, u32[]{:S(2)}) copy-start(bf16[768,576]{0,1:T(8,128)(2,1)} %param.9) | copy-start | bytes 2654212
  50.1 51.3 %copy-start.2 = (bf16[384,768]{1,0:T(8,128)(2,1)S(1)}, bf16[384,768]{1,0:T(8,128)(2,1)}, u32[]{:S(2)}) copy-start(bf16[384,768]{1,0:T(8,128)(2,1)} %param.8) | copy-start | bytes 1769476
  50.1 53.3 %copy-start.1 = (bf16[1,128,1536]{2,1,0:T(8,128)(2,1)S(1)}, bf16[1,128,1536]{2,1,0:T(8,128)(2,1)}, u32[]{:S(2)}) copy-start(bf16[1,128,1536]{2,1,0:T(8,128)(2,1)} %param.6) | copy-start | bytes 1179652
  97.1 17.5 %collective-permute-start.4 = (bf16[15,64,768]{2,1,0:T(8,128)(2,1)}, bf16[15,64,768]{2,1,0:T(8,128)(2,1)}, u32[]{:S(2)}, u32[]{:S(2)}) collective-permute-start(bf16[15,64,768]{2,1,0:T(8,128)(2,1)} %slice.37), channel_id=1, source_target_pairs={{0,1},{1,0},{2,3},{3,2},{4,5},{5,4},{6,7},{7,6},{8,9},{9,8},{10,11... | collective-permute-start | bytes 4423688 | tf_op jit(solution)/shard_map/ppermute | solution.py:169
  99.1 15.5 %collective-permute-start.2 = (bf16[9,64,768]{2,1,0:T(8,128)(2,1)S(1)}, bf16[9,64,768]{2,1,0:T(8,128)(2,1)S(1)}, u32[]{:S(2)}, u32[]{:S(2)}) collective-permute-start(bf16[9,64,768]{2,1,0:T(8,128)(2,1)S(1)} %bitcast.31), channel_id=1, source_target_pairs={{0,1},{1,0},{2,3},{3,2},{4,5},{5,4},{6,7},{7,6},{8,9},{9,8},{10,11... | collective-permute-start | bytes 2654216 | tf_op jit(solution)/shard_map/ppermute | solution.py:169
  101.5 13.1 %collective-permute-start.1 = (bf16[6,64,768]{2,1,0:T(8,128)(2,1)S(1)}, bf16[6,64,768]{2,1,0:T(8,128)(2,1)S(1)}, u32[]{:S(2)}, u32[]{:S(2)}) collective-permute-start(bf16[6,64,768]{2,1,0:T(8,128)(2,1)S(1)} %bitcast.37), channel_id=1, source_target_pairs={{0,1},{1,0},{2,3},{3,2},{4,5},{5,4},{6,7},{7,6},{8,9},{9,8},{10,11... | collective-permute-start | bytes 1769480 | tf_op jit(solution)/shard_map/ppermute | solution.py:169
  103.8 10.7 %collective-permute-start = (bf16[64,1536]{1,0:T(8,128)(2,1)S(1)}, bf16[64,1536]{1,0:T(8,128)(2,1)}, u32[]{:S(2)}, u32[]{:S(2)}) collective-permute-start(bf16[64,1536]{1,0:T(8,128)(2,1)S(1)} %slice.27.even), channel_id=1, source_target_pairs={{0,4},{4,0},{8,12},{12,8},{16,20},{20,16},{24,28},{28,24},{1,5},{5... | collective-permute-start | bytes 589832 | tf_op jit(solution)/shard_map/ppermute | solution.py:186
  114.6 0.9 copy-start.3
  132.4 5.0 %collective-permute-start.5 = (f32[16,2,24,384]{3,2,1,0:T(8,128)}, f32[16,2,24,384]{3,2,1,0:T(8,128)S(1)}, u32[]{:S(2)}, u32[]{:S(2)}) collective-permute-start(f32[16,2,24,384]{3,2,1,0:T(8,128)} %get-tuple-element.7), channel_id=1, source_target_pairs={{0,1},{1,0},{2,3},{3,2},{4,5},{5,4},{6,7},{7,6},{8,9},{9,8},{10,11... | collective-permute-start | bytes 3538952 | tf_op jit(solution)/shard_map/ppermute | solution.py:169
Sparse Core Ops, SparseCore 0:
  52.3 54.7 all-gather.1

commit v2 on v1

v2 whole, which is shorter than its diff:
```python
import jax
import jax.numpy as jnp
from jax import lax
from jax.experimental import pallas as pl
from jax.experimental.pallas import tpu as pltpu
from jax.sharding import Mesh
from jax.sharding import PartitionSpec as P

WIDTH = 768
TILE = 1536
HEADS = 16
HEAD = 48
DIL = 32
TOK = 128
FAR = 512
PACK = 1152
YX = ("y", "x")
NT = (((1,), (1,)), ((), ()))
NN = (((1,), (0,)), ((), ()))
BF = jnp.bfloat16
F32 = jnp.float32
MARK = 64.0
LOW = -1e30
VMEM_BYTES = 56 * 1024 * 1024


def dot(a, b, dims):
    return lax.dot_general(a, b, dims, preferred_element_type=F32)


def weight_moves(scal, packs, win, wqkv):
    zh, core = scal[1], scal[2]
    places = (zh * 2 + core, zh * 2 + 1 - core, (1 - zh) * 2 + core, (1 - zh) * 2 + 1 - core)
    first = [(p.at[pl.ds(0, 384)], win.at[s]) for p, s in zip(packs, places)]
    second = [(p.at[pl.ds(384, 576)], wqkv.at[s]) for p, s in zip(packs, places)]
    return first, second


def key_bias(block):
    lane = lax.broadcasted_iota(jnp.int32, (16, TOK), 1)
    pick = jnp.where(lane == 0, F32(1), F32(0)).astype(BF)
    return jnp.where(dot(pick, block[:, :TOK], NT)[0:1] > MARK / 2, F32(LOW), F32(0))


def attend(query, kv, bias, mixed):
    column = lax.broadcasted_iota(jnp.int32, (TOK, TOK), 1)
    tops = jnp.zeros((TOK, TOK), F32)
    totals = jnp.ones((TOK, TOK), F32)
    for h in range(HEADS):
        s = dot(query(h), kv[pl.ds(h * HEAD, HEAD), :], NN) * F32(HEAD**-0.5) + bias
        top = jnp.max(s, axis=1, keepdims=True)
        p = jnp.exp(s - top)
        tops = jnp.where(column == h, top, tops)
        totals = jnp.where(column == h, jnp.sum(p, axis=1, keepdims=True), totals)
        mixed[pl.ds(h * HEAD, HEAD), :] = dot(
            kv[pl.ds(WIDTH + h * HEAD, HEAD), :], p.astype(BF), NT
        )
    return tops.T, totals.T


def near_kernel(
    scal, rows, even, partner, own, mate, got, cross, query, mixed, tops, totals, near, win, wqkv, hid, kv, sems
):
    first, second = weight_moves(scal, (own, mate, got, cross), win, wqkv)
    moves = [
        (rows, near.at[pl.ds(0, TOK)]),
        (even, near.at[pl.ds(TOK, TOK // 2)]),
        (partner, near.at[pl.ds(TOK + TOK // 2, TOK // 2)]),
    ]
    moves = moves + first + second
    copies = [pltpu.make_async_copy(s, d, sems.at[i]) for i, (s, d) in enumerate(moves)]
    for c in copies:
        c.start()
    for c in copies[:7]:
        c.wait()
    hid[...] = dot(near[...], win[...].reshape(TILE, WIDTH), NN).astype(BF)
    for c in copies[7:]:
        c.wait()
    flat = wqkv[...].reshape(3 * WIDTH, WIDTH)
    kv[...] = dot(flat[WIDTH:], hid[...], NT).astype(BF)
    own_hid = hid[pl.ds(0, TOK), :]
    for h in range(HEADS):
        query[h] = dot(own_hid, flat[h * HEAD : (h + 1) * HEAD], NT).astype(BF)
    lane = lax.broadcasted_iota(jnp.int32, (1, 192), 1)
    offset = jnp.where(lane < TOK, lane, 2 * (lane - TOK))
    mine = jnp.where(offset < scal[0], F32(0), F32(LOW))
    bias = jnp.concatenate([mine, key_bias(near[pl.ds(192, 64), :])], axis=1)
    tops[...], totals[...] = attend(lambda h: query[h], kv, bias, mixed)


def far_kernel(
    scal,
    rows,
    query,
    near_mixed,
    near_tops,
    near_totals,
    cot,
    own,
    mate,
    got,
    cross,
    out,
    keep,
    send,
    far,
    win,
    wqkv,
    wout,
    hid,
    kv,
    mixed,
    attn,
    sems,
):
    first, second = weight_moves(scal, (own, mate, got, cross), win, wqkv)
    zh, core = scal[1], scal[2]
    places = (zh * 2 + core, zh * 2 + 1 - core, (1 - zh) * 2 + core, (1 - zh) * 2 + 1 - core)
    last = [(p.at[pl.ds(960, 192)], wout.at[s]) for p, s in zip((own, mate, got, cross), places)]
    moves = [(rows, far)] + first + second + last
    copies = [pltpu.make_async_copy(s, d, sems.at[i]) for i, (s, d) in enumerate(moves)]
    for c in copies:
        c.start()
    for c in copies[:5]:
        c.wait()
    left = far[:, pl.ds(0, 32), :].reshape(FAR, WIDTH)
    right = far[:, pl.ds(32, 32), :].reshape(FAR, WIDTH)
    weight = win[...].reshape(TILE, WIDTH)
    hid[...] = (dot(left, weight[:WIDTH], NN) + dot(right, weight[WIDTH:], NN)).astype(BF)
    for c in copies[5:]:
        c.wait()
    kv[...] = dot(wqkv[...].reshape(3 * WIDTH, WIDTH)[WIDTH:], hid[...], NT).astype(BF)
    far_tops, far_totals = attend(lambda h: query[h], kv, key_bias(left), mixed)
    top = jnp.maximum(near_tops[...], far_tops)
    near_scale, far_scale = jnp.exp(near_tops[...] - top), jnp.exp(far_tops - top)
    inverse = 1.0 / (near_totals[...] * near_scale + far_totals * far_scale)
    near_scale, far_scale = near_scale * inverse, far_scale * inverse
    for h in range(HEADS):
        at = pl.ds(h * HEAD, HEAD)
        attn[at, :] = (
            near_mixed[at, :] * near_scale[h : h + 1, :] + mixed[at, :] * far_scale[h : h + 1, :]
        ).astype(BF)
    cotangent = cot[...]
    token = lax.broadcasted_iota(jnp.int32, (192, TOK), 1)
    for which, target in ((core, keep), (1 - core, send)):
        for half in range(2):
            start = pl.multiple_of(half * 384 + which * 192, 192)
            block = attn[pl.ds(start, 192), :]
            block = jnp.where(token < scal[0], block, jnp.zeros_like(block))
            part = dot(block, cotangent, NN)
            for r in range(8):
                for c in range(2):
                    target[r * 2 + c, half] = part[r * 24 : r * 24 + 24, c * 384 : c * 384 + 384]
    out[...] = dot(wout[...].reshape(WIDTH, WIDTH), attn[...], NN).T


ANY = pl.BlockSpec(memory_space=pl.ANY)
VMEM = pl.BlockSpec(memory_space=pltpu.VMEM)
SMEM = pl.BlockSpec(memory_space=pltpu.SMEM)
PARAMS = pltpu.CompilerParams(vmem_limit_bytes=VMEM_BYTES)


def near_call(*operands, interpret=False):
    state = jax.ShapeDtypeStruct((TOK, TOK), F32)
    return pl.pallas_call(
        near_kernel,
        out_shape=(
            jax.ShapeDtypeStruct((HEADS, TOK, HEAD), BF),
            jax.ShapeDtypeStruct((WIDTH, TOK), F32),
            state,
            state,
        ),
        in_specs=[SMEM] + [ANY] * 7,
        out_specs=(VMEM,) * 4,
        scratch_shapes=[
            pltpu.VMEM((256, TILE), BF),
            pltpu.VMEM((4, 384, WIDTH), BF),
            pltpu.VMEM((4, 576, WIDTH), BF),
            pltpu.VMEM((256, WIDTH), BF),
            pltpu.VMEM((2 * WIDTH, 256), BF),
            pltpu.SemaphoreType.DMA((11,)),
        ],
        compiler_params=PARAMS,
        cost_estimate=pl.CostEstimate(
            flops=2_000_000_000, bytes_accessed=12_000_000, transcendentals=600_000
        ),
        interpret=interpret,
    )(*operands)


def far_call(*operands, interpret=False):
    part = jax.ShapeDtypeStruct((16, 2, 24, 384), F32)
    return pl.pallas_call(
        far_kernel,
        out_shape=(jax.ShapeDtypeStruct((TOK, WIDTH), F32), part, part),
        in_specs=[SMEM, ANY] + [VMEM] * 5 + [ANY] * 4,
        out_specs=(VMEM,) * 3,
        scratch_shapes=[
            pltpu.VMEM((16, 64, WIDTH), BF),
            pltpu.VMEM((4, 384, WIDTH), BF),
            pltpu.VMEM((4, 576, WIDTH), BF),
            pltpu.VMEM((4, 192, WIDTH), BF),
            pltpu.VMEM((FAR, WIDTH), BF),
            pltpu.VMEM((2 * WIDTH, FAR), BF),
            pltpu.VMEM((WIDTH, TOK), F32),
            pltpu.VMEM((WIDTH, TOK), BF),
            pltpu.SemaphoreType.DMA((13,)),
        ],
        compiler_params=PARAMS,
        cost_estimate=pl.CostEstimate(
            flops=3_000_000_000, bytes_accessed=16_000_000, transcendentals=1_000_000
        ),
        interpret=interpret,
    )(*operands)


def spread(block, axes, size):
    return lax.all_to_all(
        jnp.broadcast_to(block[None], (size,) + block.shape), axes, 0, 0, tiled=True
    )


def swap(value, axis):
    return lax.ppermute(value, axis, [(0, 1), (1, 0)])


def marked(rows, offsets, count):
    lane = lax.broadcasted_iota(jnp.int32, rows.shape, 1)
    mark = jnp.where(lane == 0, BF(MARK), BF(0))
    return jnp.where((offsets < count)[:, None], rows, mark)


def shards(tiles, counts, w_in, w_qkv, w_out, cotangent):
    rows = tiles[0]
    count = counts[0, 0]
    yx = lax.axis_index("y") * 4 + lax.axis_index("x")
    zh, core = lax.axis_index("zh"), lax.axis_index("core")
    own = jnp.concatenate([w_in, w_qkv.T, w_out.T], axis=0)
    piece = swap(lax.dynamic_slice(own, (yx * (PACK // 16), 0), (PACK // 16, WIDTH)), "zh")
    distant = marked(rows[0::DIL], jnp.arange(4) * DIL, count)
    line = spread(jnp.concatenate([distant[:, :WIDTH], distant[:, WIDTH:]], axis=0), "zl", 8)
    mate = swap(own, "core")
    even = rows[0::2]
    partner = lax.ppermute(
        marked(even, jnp.arange(TOK // 2) * 2, count), "zl", [(i, i ^ 1) for i in range(8)]
    )
    piece, line, mate, partner = lax.optimization_barrier((piece, line, mate, partner))
    got = spread(piece, YX, 16).reshape(PACK, WIDTH)
    far_rows = jnp.concatenate(
        [line[:, :4].reshape(32, WIDTH), line[:, 4:].reshape(32, WIDTH)], axis=0
    )
    far = spread(far_rows, YX, 16)
    cross = swap(got, "core")
    scal = jnp.stack([count, zh, core]).astype(jnp.int32)
    packs = (own, mate, got, cross)
    state = near_call(scal, rows, even, partner, *packs)
    out, keep, send = far_call(scal, far, *state, cotangent[0], *packs)
    pair = (keep + swap(send, "core")).astype(BF)
    plane = lax.all_to_all(pair, YX, 0, 0, tiled=True)
    plane = jnp.sum(plane.astype(F32), axis=0).astype(BF)
    column = jnp.broadcast_to(plane[:, None], (2, 8, 24, 384)).reshape(16, 24, 384)
    column = lax.all_to_all(column, ("zh", "zl"), 0, 0, tiled=True)
    total = jnp.sum(column.astype(F32), axis=0)
    whole = spread(total, YX, 16)
    grad = whole.reshape(8, 2, 24, 384).transpose(0, 2, 1, 3).reshape(192, WIDTH)
    return (out[None], grad)


def solution(mesh):
    fine = Mesh(mesh.devices.reshape(4, 4, 8, 2, 2), ("y", "x", "zl", "zh", "core"))
    seq, slide = ("y", "x", "zl"), ("zh", "core")
    placed = (
        P(slide, seq, None),
        P(slide, seq),
        P(slide, None),
        P(None, slide),
        P(None, slide),
        P(slide, seq, None),
    )
    return jax.shard_map(
        shards,
        mesh=fine,
        in_specs=placed,
        out_specs=(P(slide, seq, None), P(slide, None)),
        check_vma=False,
    )
```

time: 217 us -> 204 us (0.940)
  waiting for transfers between devices: 60.2 us -> 31.1 us
  blocking collectives: 70.6 us -> 94.8 us
  between operations: 15.6 us -> 1.45 us
  starting transfers between devices: 41.2 us -> 32.9 us
  local copies, waits for them, and re-layouts: 10.4 us -> 15.5 us
  other arithmetic: 1.42 us -> 6.38 us
  Pallas kernels: 16.9 us -> 20.8 us
    all_to_all x1 -> x2, blocking collectives: 14.3 us -> 43.3 us  [spread(): lax.all_to_all(jnp.broadcast_to(block[None], (size,) + block.shape), axes...]
    all_to_all x2, waiting for transfers between devices: 44.3 us -> 18.2 us  [spread(): lax.all_to_all(jnp.broadcast_to(block[None], (size,) + block.shape), axes...]
    all_to_all x1, blocking collectives: 40.2 us -> 36.1 us  [shards(): column = lax.all_to_all(column, ('zh', 'zl'), 0, 0, tiled=True)]
    pallas_call x1 -> x2, Pallas kernels: 16.9 us -> 20.8 us  [the longest x1 13.4 us: far_call(): pl.pallas_call(far_kernel, out_shape=(jax.ShapeDtypeStruct((TOK, WIDTH),...]
    ppermute x1, waiting for transfers between devices: 3.71 us -> 0.01 us  [shards(): lax.ppermute(marked(even, jnp.arange(TOK // 2) * 2, count), 'zl', [(i, i...]
    ppermute x1, starting transfers between devices: 5.08 us -> 1.91 us  [shards(): lax.ppermute(marked(even, jnp.arange(TOK // 2) * 2, count), 'zl', [(i, i...]
    reshape x2, local copies, waits for them, and re-layouts: 0.04 us -> 2.88 us  [the longest x1 1.44 us: shards(): line[:, :4].reshape(32, WIDTH)]
    all_to_all x2, starting transfers between devices: 19.7 us -> 17 us  [spread(): lax.all_to_all(jnp.broadcast_to(block[None], (size,) + block.shape), axes...]
  transfers between devices with their start and end apart: 9 -> 7, of which waited for: 4 -> 3; matrix products, arithmetic and copies ran while one was open for 2% -> 7% of each run, Pallas kernels for 0% -> 4%
where the time goes in v2:
time: 204 us; the launch traced here: 203 us
  blocking collectives  94.8 us (46%)
  starting transfers between devices  32.9 us (16%)
  waiting for transfers between devices  31.1 us (15%)
  Pallas kernels  20.8 us (10%)
  local copies, waits for them, and re-layouts  15.5 us (8%)
  other arithmetic  6.38 us (3%)
    all_to_all x2, blocking collectives, spread(): lax.all_to_all(jnp.broadcast_to(block[None], (size,) + block.shape), axes...  43.3 us
    all_to_all x1, blocking collectives, shards(): column = lax.all_to_all(column, ('zh', 'zl'), 0, 0, tiled=True)  36.1 us
    all_to_all x2, waiting for transfers between devices, spread(): lax.all_to_all(jnp.broadcast_to(block[None], (size,) + block.shape), axes...  18.2 us
    all_to_all x2, starting transfers between devices, spread(): lax.all_to_all(jnp.broadcast_to(block[None], (size,) + block.shape), axes...  17 us
    all_to_all x1, blocking collectives, shards(): plane = lax.all_to_all(pair, YX, 0, 0, tiled=True)  15.4 us
    ppermute x4, starting transfers between devices, swap(): return lax.ppermute(value, axis, [(0, 1), (1, 0)])  14 us
    pallas_call x1, Pallas kernels, far_call(): pl.pallas_call(far_kernel, out_shape=(jax.ShapeDtypeStruct((TOK, WIDTH),...  13.4 us
    ppermute x4, waiting for transfers between devices, swap(): return lax.ppermute(value, axis, [(0, 1), (1, 0)])  12.9 us
  transfers between devices with their start and end apart: 7, of which 3 were waited for; matrix products, arithmetic and copies ran while one was open for 7% of the time, Pallas kernels for 4%

profile of v2, /device:TPU:32, one launch (start us, length us, event | category | flops | bytes accessed | tf_op | source)
XLA Modules:
  0.0 203.0 jit_solution(9752470431565751600)
XLA Ops:
  0.6 1.5 pad_maximum_fusion.own
  2.2 1.9 collective-permute-start.1
  4.8 1.0 slice.18
  5.9 0.6 broadcast_in_dim.66
  6.6 12.6 %all-to-all-start = ((bf16[8,8,768]{2,1,0:T(8,128)(2,1)}), bf16[8,8,768]{2,1,0:T(8,128)(2,1)}, u32[]{:S(2)}, u32[]{:S(2)}) async-start(bf16[8,8,768]{2,1,0:T(8,128)(2,1)} %broadcast_in_dim.66), calls=%async_computation | async-start | bytes 196608 | tf_op jit(solution)/shard_map/all_to_all | solution.py:218
  19.2 2.6 %slice.21.even = bf16[64,1536]{1,0:T(8,128)(2,1)} slice(bf16[128,1536]{1,0:T(8,128)(2,1)} %bitcast.27), slice={[0:128:2], [0:1536:1]} | slice | bytes 393216 | tf_op jit(solution)/shard_map/slice | solution.py:243
  21.8 1.7 broadcast_select_fusion
  23.5 1.9 collective-permute-start.2
  25.4 8.2 %collective-permute-start = (bf16[72,768]{1,0:T(8,128)(2,1)S(1)}, bf16[72,768]{1,0:T(8,128)(2,1)S(1)}, u32[]{:S(2)}, u32[]{:S(2)}) collective-permute-start(bf16[72,768]{1,0:T(8,128)(2,1)S(1)} %constant_dynamic-slice_fusion), channel_id=1, source_target_pairs={{0,2},{2,0},{1,3},{3,1},{4,6},{6,4},{5,7},{7,5},{8,10},{10,8},{9,1... | collective-permute-start | bytes 331784 | tf_op jit(solution)/shard_map/ppermute | solution.py:224
  33.7 9.8 %collective-permute-done = bf16[72,768]{1,0:T(8,128)(2,1)S(1)} collective-permute-done((bf16[72,768]{1,0:T(8,128)(2,1)S(1)}, bf16[72,768]{1,0:T(8,128)(2,1)S(1)}, u32[]{:S(2)}, u32[]{:S(2)}) %collective-permute-start) | collective-permute-done | bytes 110624 | tf_op jit(solution)/shard_map/ppermute | solution.py:224
  44.2 1.2 copy-done.2
  45.4 1.0 broadcast_in_dim.69
  46.4 28.5 %all_to_all.30 = bf16[16,72,768]{2,1,0:T(8,128)(2,1)S(1)} all-to-all(bf16[16,72,768]{2,1,0:T(8,128)(2,1)S(1)} %broadcast_in_dim.69), channel_id=1, replica_groups=mesh['y'=4,'x'=4,'zl'=8,'zh'=2,'core'=2] {'y','x'}, dimensions={0} | all-to-all | bytes 3538944 | tf_op jit(solution)/shard_map/all_to_all | solution.py:218
  74.9 1.9 collective-permute-start.3
  76.8 1.7 fusion.1
  78.4 1.4 reshape.37
  79.9 1.4 reshape.38
  81.3 0.8 pad_maximum_fusion.1
  82.1 1.4 broadcast_in_dim.68
  83.5 4.4 %all-to-all-start.1 = ((bf16[16,64,768]{2,1,0:T(8,128)(2,1)}), bf16[16,64,768]{2,1,0:T(8,128)(2,1)}, u32[]{:S(2)}, u32[]{:S(2)}) async-start(bf16[16,64,768]{2,1,0:T(8,128)(2,1)} %broadcast_in_dim.68), calls=%async_computation.1 | async-start | bytes 3145728 | tf_op jit(solution)/shard_map/all_to_all | solution.py:218
  87.9 0.6 pad_add_fusion.scal
  88.6 1.3 copy-done.3
  89.9 7.4 %shard_map.77 = (bf16[16,128,48]{2,1,0:T(8,128)(2,1)}, f32[768,128]{1,0:T(8,128)}, f32[128,128]{1,0:T(8,128)}, f32[128,128]{1,0:T(8,128)}) custom-call(s32[3]{0:T(128)} %pad_add_fusion.scal, bf16[128,1536]{1,0:T(8,128)(2,1)} %bitcast.28, bf16[64,1536]{1,0:T(8,128)(2,1)} %slice.21.even, bf16[64,1536]{1,0:T(8,128)(2,1)} %collective-permute-done.2.partner, ...), custom_call_target="tpu_custom_call" | custom-call | flops 2000000000 | bytes 12000000 | tf_op jit(solution)/shard_map/pallas_call | solution.py:165
  97.3 18.2 %all-to-all-done.1.rows = bf16[16,64,768]{2,1,0:T(8,128)(2,1)} async-done(((bf16[16,64,768]{2,1,0:T(8,128)(2,1)}), bf16[16,64,768]{2,1,0:T(8,128)(2,1)}, u32[]{:S(2)}, u32[]{:S(2)}) %all-to-all-start.1) | async-done | bytes 1572896 | tf_op jit(solution)/shard_map/all_to_all | solution.py:218
  115.5 13.4 %shard_map.78 = (f32[128,768]{1,0:T(8,128)}, f32[16,2,24,384]{3,2,1,0:T(8,128)}, f32[16,2,24,384]{3,2,1,0:T(8,128)}) custom-call(s32[3]{0:T(128)} %pad_add_fusion.scal, bf16[16,64,768]{2,1,0:T(8,128)(2,1)} %all-to-all-done.1.rows, bf16[16,128,48]{2,1,0:T(8,128)(2,1)} %get-tuple-element.17.query, f32[768,128]{1,0:T(8,128)} %get-tuple-element.18.near_mixed, ...), custom_call_target="tpu_custom_call" | custom-call | flops 3000000000 | bytes 16000000 | tf_op jit(solution)/shard_map/pallas_call | solution.py:193
  128.8 1.9 collective-permute-start.4
  130.8 3.0 %collective-permute-done.4 = f32[16,2,24,384]{3,2,1,0:T(8,128)S(1)} collective-permute-done((f32[16,2,24,384]{3,2,1,0:T(8,128)}, f32[16,2,24,384]{3,2,1,0:T(8,128)S(1)}, u32[]{:S(2)}, u32[]{:S(2)}) %collective-permute-start.4) | collective-permute-done | bytes 1179680 | tf_op jit(solution)/shard_map/ppermute | solution.py:224
  133.8 1.4 add_convert_fusion
  135.2 15.4 %all_to_all.31 = bf16[16,2,24,384]{3,2,1,0:T(8,128)(2,1)S(1)} all-to-all(bf16[16,2,24,384]{3,2,1,0:T(8,128)(2,1)S(1)} %add_convert_fusion), channel_id=1, replica_groups=mesh['y'=4,'x'=4,'zl'=8,'zh'=2,'core'=2] {'y','x'}, dimensions={0} | all-to-all | bytes 1179648 | tf_op jit(solution)/shard_map/all_to_all | solution.py:259
  150.8 36.1 %all_to_all.32 = bf16[16,24,384]{2,1,0:T(8,128)(2,1)S(1)} all-to-all(bf16[16,24,384]{2,1,0:T(8,128)(2,1)S(1)} %bitcast.25), channel_id=1, replica_groups=mesh['y'=4,'x'=4,'zl'=8,'zh'=2,'core'=2] {'zh','zl'}, dimensions={0} | all-to-all | bytes 589824 | tf_op jit(solution)/shard_map/all_to_all | solution.py:262
  187.0 14.8 %all_to_all.33 = f32[16,24,384]{2,1,0:T(8,128)S(1)} all-to-all(f32[16,24,384]{2,1,0:T(8,128)S(1)} %broadcast_in_dim.72), channel_id=1, replica_groups=mesh['y'=4,'x'=4,'zl'=8,'zh'=2,'core'=2] {'y','x'}, dimensions={0} | all-to-all | bytes 1179648 | tf_op jit(solution)/shard_map/all_to_all | solution.py:218
  202.1 0.9 copy.10
  (24 shorter events, 1.3 us)
Async XLA Ops:
  2.2 72.7 %copy-start = (bf16[1152,768]{1,0:T(8,128)(2,1)}, bf16[1152,768]{1,0:T(8,128)(2,1)S(1)}, u32[]{:S(2)}) copy-start(bf16[1152,768]{1,0:T(8,128)(2,1)S(1)} %pad_maximum_fusion.own) | copy-start | bytes 5308420
  2.2 42.0 %collective-permute-start.1 = (bf16[1152,768]{1,0:T(8,128)(2,1)S(1)}, bf16[1152,768]{1,0:T(8,128)(2,1)S(1)}, u32[]{:S(2)}, u32[]{:S(2)}) collective-permute-start(bf16[1152,768]{1,0:T(8,128)(2,1)S(1)} %pad_maximum_fusion.own), channel_id=1, source_target_pairs={{0,1},{1,0},{2,3},{3,2},{4,5},{5,4},{6,7},{7,6},{8,9},{9,8},{10,11... | collective-permute-start | bytes 5308424 | tf_op jit(solution)/shard_map/ppermute | solution.py:224
  6.6 37.6 %all-to-all-start = ((bf16[8,8,768]{2,1,0:T(8,128)(2,1)}), bf16[8,8,768]{2,1,0:T(8,128)(2,1)}, u32[]{:S(2)}, u32[]{:S(2)}) async-start(bf16[8,8,768]{2,1,0:T(8,128)(2,1)} %broadcast_in_dim.66), calls=%async_computation | async-start | bytes 196608 | tf_op jit(solution)/shard_map/all_to_all | solution.py:218
  23.5 20.7 %collective-permute-start.2 = (bf16[64,1536]{1,0:T(8,128)(2,1)}, bf16[64,1536]{1,0:T(8,128)(2,1)}, u32[]{:S(2)}, u32[]{:S(2)}) collective-permute-start(bf16[64,1536]{1,0:T(8,128)(2,1)} %broadcast_select_fusion), channel_id=1, source_target_pairs={{0,4},{4,0},{8,12},{12,8},{16,20},{20,16},{24,28},{28,24},{1,5},{5... | collective-permute-start | bytes 589832 | tf_op jit(solution)/shard_map/ppermute | solution.py:244
  25.4 18.1 %collective-permute-start = (bf16[72,768]{1,0:T(8,128)(2,1)S(1)}, bf16[72,768]{1,0:T(8,128)(2,1)S(1)}, u32[]{:S(2)}, u32[]{:S(2)}) collective-permute-start(bf16[72,768]{1,0:T(8,128)(2,1)S(1)} %constant_dynamic-slice_fusion), channel_id=1, source_target_pairs={{0,2},{2,0},{1,3},{3,1},{4,6},{6,4},{5,7},{7,5},{8,10},{10,8},{9,1... | collective-permute-start | bytes 331784 | tf_op jit(solution)/shard_map/ppermute | solution.py:224
  43.5 0.6 copy-start.4
  44.2 1.2 copy-start.2
  74.9 8.7 %copy-start.1 = (bf16[16,72,768]{2,1,0:T(8,128)(2,1)}, bf16[16,72,768]{2,1,0:T(8,128)(2,1)S(1)}, u32[]{:S(2)}) copy-start(bf16[16,72,768]{2,1,0:T(8,128)(2,1)S(1)} %all_to_all.30) | copy-start | bytes 5308420
  74.9 13.7 %collective-permute-start.3 = (bf16[1152,768]{1,0:T(8,128)(2,1)S(1)}, bf16[1152,768]{1,0:T(8,128)(2,1)S(1)}, u32[]{:S(2)}, u32[]{:S(2)}) collective-permute-start(bf16[1152,768]{1,0:T(8,128)(2,1)S(1)} %bitcast.20), channel_id=1, source_target_pairs={{0,1},{1,0},{2,3},{3,2},{4,5},{5,4},{6,7},{7,6},{8,9},{9,8},{10,11... | collective-permute-start | bytes 5308424 | tf_op jit(solution)/shard_map/ppermute | solution.py:224
  83.5 32.0 %all-to-all-start.1 = ((bf16[16,64,768]{2,1,0:T(8,128)(2,1)}), bf16[16,64,768]{2,1,0:T(8,128)(2,1)}, u32[]{:S(2)}, u32[]{:S(2)}) async-start(bf16[16,64,768]{2,1,0:T(8,128)(2,1)} %broadcast_in_dim.68), calls=%async_computation.1 | async-start | bytes 3145728 | tf_op jit(solution)/shard_map/all_to_all | solution.py:218
  88.6 1.3 copy-start.3
  128.8 5.0 %collective-permute-start.4 = (f32[16,2,24,384]{3,2,1,0:T(8,128)}, f32[16,2,24,384]{3,2,1,0:T(8,128)S(1)}, u32[]{:S(2)}, u32[]{:S(2)}) collective-permute-start(f32[16,2,24,384]{3,2,1,0:T(8,128)} %get-tuple-element.23), channel_id=1, source_target_pairs={{0,1},{1,0},{2,3},{3,2},{4,5},{5,4},{6,7},{7,6},{8,9},{9,8},{10,11... | collective-permute-start | bytes 3538952 | tf_op jit(solution)/shard_map/ppermute | solution.py:224

commit v3 on v2

v3 whole, which is shorter than its diff:
```python
import jax
import jax.numpy as jnp
from jax import lax
from jax.experimental import pallas as pl
from jax.experimental.pallas import tpu as pltpu
from jax.sharding import Mesh
from jax.sharding import PartitionSpec as P

WIDTH = 768
TILE = 1536
HEADS = 16
HEAD = 48
DIL = 32
TOK = 128
FAR = 512
PACK = 1152
YX = ("y", "x")
ZL = ("zm", "zn")
NT = (((1,), (1,)), ((), ()))
NN = (((1,), (0,)), ((), ()))
BF = jnp.bfloat16
F32 = jnp.float32
MARK = 64.0
LOW = -1e30
LOG2 = 0.6931471805599453


def dot(a, b, dims):
    return lax.dot_general(a, b, dims, preferred_element_type=F32)


def weight_moves(scal, packs, win, wqkv):
    zh, core = scal[1], scal[2]
    places = (zh * 2 + core, zh * 2 + 1 - core, (1 - zh) * 2 + core, (1 - zh) * 2 + 1 - core)
    first = [(p.at[pl.ds(0, 384)], win.at[s]) for p, s in zip(packs, places)]
    second = [(p.at[pl.ds(384, 576)], wqkv.at[s]) for p, s in zip(packs, places)]
    return first, second


def key_bias(block):
    lane = lax.broadcasted_iota(jnp.int32, (16, TOK), 1)
    pick = jnp.where(lane == 0, F32(1), F32(0)).astype(BF)
    return jnp.where(dot(pick, block[:, :TOK], NT)[0:1] > MARK / 2, F32(LOW), F32(0))


def attend(query, kv, bias, mixed):
    column = lax.broadcasted_iota(jnp.int32, (TOK, TOK), 1)
    tops = jnp.zeros((TOK, TOK), F32)
    totals = jnp.ones((TOK, TOK), F32)
    for h in range(HEADS):
        s = dot(query(h), kv[pl.ds(h * HEAD, HEAD), :], NN) * F32(HEAD**-0.5) + bias
        top = jnp.max(s, axis=1, keepdims=True)
        p = jnp.exp(s - top)
        tops = jnp.where(column == h, top, tops)
        totals = jnp.where(column == h, jnp.sum(p, axis=1, keepdims=True), totals)
        mixed[pl.ds(h * HEAD, HEAD), :] = dot(
            kv[pl.ds(WIDTH + h * HEAD, HEAD), :], p.astype(BF), NT
        )
    return tops.T, totals.T


def near_kernel(
    scal, rows, partner, own, mate, got, cross, query, mixed, tops, totals, near, win, wqkv, hid, kv, sems
):
    first, second = weight_moves(scal, (own, mate, got, cross), win, wqkv)
    moves = [
        (rows, near.at[pl.ds(0, TOK)]),
        (partner, near.at[pl.ds(TOK, TOK // 2)]),
    ]
    moves = moves + first + second
    copies = [pltpu.make_async_copy(s, d, sems.at[i]) for i, (s, d) in enumerate(moves)]
    for c in copies:
        c.start()
    near[pl.ds(192, 64), :] = jnp.zeros((64, TILE), BF)
    for c in copies[:6]:
        c.wait()
    hid[...] = dot(near[...], win[...].reshape(TILE, WIDTH), NN).astype(BF)
    for c in copies[6:]:
        c.wait()
    flat = wqkv[...].reshape(3 * WIDTH, WIDTH)
    kv[...] = dot(flat[WIDTH:], hid[...], NT).astype(BF)
    own_hid = hid[pl.ds(0, TOK), :]
    for h in range(HEADS):
        query[h] = dot(own_hid, flat[h * HEAD : (h + 1) * HEAD], NT).astype(BF)
    lane = lax.broadcasted_iota(jnp.int32, (1, TOK), 1)
    twice = jnp.where(lane & 1 == 0, F32(LOG2), F32(0))
    bias = jnp.concatenate(
        [
            jnp.where(lane < scal[0], twice, F32(LOW)),
            key_bias(near[pl.ds(TOK, 64), :]),
            jnp.full((1, 64), LOW, F32),
        ],
        axis=1,
    )
    tops[...], totals[...] = attend(lambda h: query[h], kv, bias, mixed)


def far_kernel(
    scal,
    far,
    query,
    near_mixed,
    near_tops,
    near_totals,
    cot,
    own,
    mate,
    got,
    cross,
    over_rest,
    cross_rest,
    out,
    keep,
    send,
    win,
    wqkv,
    wout,
    hid,
    kv,
    mixed,
    attn,
    sems,
):
    zh, core = scal[1], scal[2]
    first, second = weight_moves(scal, (own, mate, got, cross), win, wqkv)
    places = (zh * 2 + core, zh * 2 + 1 - core, (1 - zh) * 2 + core, (1 - zh) * 2 + 1 - core)
    last = [(p.at[pl.ds(960, 192)], wout.at[s]) for p, s in zip((own, mate), places[:2])]
    for p, rest, s in zip((got, cross), (over_rest, cross_rest), places[2:]):
        last.append((p.at[pl.ds(960, 64)], wout.at[s, pl.ds(0, 64)]))
        last.append((rest, wout.at[s, pl.ds(64, 128)]))
    moves = first + second + last
    copies = [pltpu.make_async_copy(s, d, sems.at[i]) for i, (s, d) in enumerate(moves)]
    for c in copies:
        c.start()
    for c in copies[:4]:
        c.wait()
    left = far[:, pl.ds(0, 32), :].reshape(FAR, WIDTH)
    right = far[:, pl.ds(32, 32), :].reshape(FAR, WIDTH)
    weight = win[...].reshape(TILE, WIDTH)
    hid[...] = (dot(left, weight[:WIDTH], NN) + dot(right, weight[WIDTH:], NN)).astype(BF)
    for c in copies[4:8]:
        c.wait()
    kv[...] = dot(wqkv[...].reshape(3 * WIDTH, WIDTH)[WIDTH:], hid[...], NT).astype(BF)
    far_tops, far_totals = attend(lambda h: query[h], kv, key_bias(left), mixed)
    top = jnp.maximum(near_tops[...], far_tops)
    near_scale, far_scale = jnp.exp(near_tops[...] - top), jnp.exp(far_tops - top)
    inverse = 1.0 / (near_totals[...] * near_scale + far_totals * far_scale)
    near_scale, far_scale = near_scale * inverse, far_scale * inverse
    for h in range(HEADS):
        at = pl.ds(h * HEAD, HEAD)
        attn[at, :] = (
            near_mixed[at, :] * near_scale[h : h + 1, :] + mixed[at, :] * far_scale[h : h + 1, :]
        ).astype(BF)
    cotangent = cot[...]
    token = lax.broadcasted_iota(jnp.int32, (192, TOK), 1)
    for which, target in ((core, keep), (1 - core, send)):
        for half in range(2):
            start = pl.multiple_of(half * 384 + which * 192, 192)
            block = attn[pl.ds(start, 192), :]
            block = jnp.where(token < scal[0], block, jnp.zeros_like(block))
            part = dot(block, cotangent, NN)
            for r in range(8):
                for c in range(2):
                    target[r * 2 + c, half] = part[r * 24 : r * 24 + 24, c * 384 : c * 384 + 384].astype(
                        target.dtype
                    )
    for c in copies[8:]:
        c.wait()
    out[...] = dot(wout[...].reshape(WIDTH, WIDTH), attn[...], NN).T


ANY = pl.BlockSpec(memory_space=pl.ANY)
VMEM = pl.BlockSpec(memory_space=pltpu.VMEM)
SMEM = pl.BlockSpec(memory_space=pltpu.SMEM)


def room(mebibytes):
    return pltpu.CompilerParams(vmem_limit_bytes=mebibytes * 1024 * 1024)


def prepare_kernel(scal, rows, w_in, w_qkv, w_out, own, ahead, even, sixteen, sems):
    count, zh, at = scal[0], scal[1], scal[3]
    moves = [
        (w_in, own.at[pl.ds(0, 384)]),
        (w_qkv, own.at[pl.ds(384, 576)]),
        (w_out, own.at[pl.ds(960, 192)]),
    ]
    copies = [pltpu.make_async_copy(s, d, sems.at[i]) for i, (s, d) in enumerate(moves)]
    for c in copies:
        c.start()
    block = at // 16

    def fetch(source, first):
        start = pl.multiple_of((block - first) * 16, 16)
        copy = pltpu.make_async_copy(source.at[pl.ds(start, 16)], sixteen, sems.at[3])
        copy.start()
        copy.wait()

    @pl.when(block < 24)
    def _():
        fetch(w_in, 0)

    @pl.when((block >= 24) & (block < 60))
    def _():
        fetch(w_qkv, 24)

    @pl.when(block >= 60)
    def _():
        fetch(w_out, 60)

    wide = sixteen[...].astype(F32)
    eight = jnp.where(at - block * 16 > 0, wide[8:16], wide[0:8])
    lane = lax.broadcasted_iota(jnp.int32, (1, TILE), 1)
    mark = jnp.where(lane == 0, F32(MARK), F32(0))
    distant = jnp.concatenate(
        [
            jnp.where(DIL * j < count, rows[pl.ds(DIL * j, 16), :].astype(F32)[0:1], mark)
            for j in range(4)
        ],
        axis=0,
    )
    far = jnp.concatenate([distant[:, :WIDTH], distant[:, WIDTH:]], axis=0)
    for half in range(2):
        value = jnp.where(zh == half, far, eight)
        ahead[half] = jnp.concatenate([value] * 8, axis=0).astype(BF)
    row = lax.broadcasted_iota(jnp.int32, (TOK // 2, TOK), 0)
    source = lax.broadcasted_iota(jnp.int32, (TOK // 2, TOK), 1)
    pick = jnp.where((source == 2 * row) & (source < count), F32(1), F32(0)).astype(BF)
    marks = jnp.where(
        2 * lax.broadcasted_iota(jnp.int32, (TOK // 2, TILE), 0) < count, F32(0), mark
    )
    even[...] = (dot(pick, rows[...], NN) + marks).astype(BF)
    for c in copies:
        c.wait()


def prepare_call(*operands, interpret=False):
    return pl.pallas_call(
        prepare_kernel,
        out_shape=(
            jax.ShapeDtypeStruct((PACK, WIDTH), BF),
            jax.ShapeDtypeStruct((2, 64, WIDTH), BF),
            jax.ShapeDtypeStruct((TOK // 2, TILE), BF),
        ),
        in_specs=[SMEM, VMEM] + [ANY] * 3,
        out_specs=(ANY, VMEM, VMEM),
        scratch_shapes=[pltpu.VMEM((16, WIDTH), BF), pltpu.SemaphoreType.DMA((4,))],
        compiler_params=room(62),
        interpret=interpret,
    )(*operands)


def split_kernel(scal, line, pieces, rows):
    zh = scal[1]
    piece = line[1 - zh]
    target = lax.broadcasted_iota(jnp.int32, (64, 64), 0)
    source = lax.broadcasted_iota(jnp.int32, (64, 64), 1)
    origin = (target & 31) // 4 * 8 + target // 32 * 4 + (target & 3)
    pick = jnp.where(source == origin, F32(1), F32(0)).astype(BF)
    ordered = dot(pick, line[zh], NN).astype(BF)
    for i in range(16):
        pieces[i] = piece
        rows[i] = ordered


def split_call(*operands, interpret=False):
    payload = jax.ShapeDtypeStruct((16, 64, WIDTH), BF)
    return pl.pallas_call(
        split_kernel,
        out_shape=(payload, payload),
        in_specs=[SMEM, VMEM],
        out_specs=(VMEM, VMEM),
        compiler_params=room(16),
        interpret=interpret,
    )(*operands)


def near_call(*operands, interpret=False):
    state = jax.ShapeDtypeStruct((TOK, TOK), F32)
    return pl.pallas_call(
        near_kernel,
        out_shape=(
            jax.ShapeDtypeStruct((HEADS, TOK, HEAD), BF),
            jax.ShapeDtypeStruct((WIDTH, TOK), F32),
            state,
            state,
        ),
        in_specs=[SMEM] + [ANY] * 6,
        out_specs=(VMEM,) * 4,
        scratch_shapes=[
            pltpu.VMEM((256, TILE), BF),
            pltpu.VMEM((4, 384, WIDTH), BF),
            pltpu.VMEM((4, 576, WIDTH), BF),
            pltpu.VMEM((256, WIDTH), BF),
            pltpu.VMEM((2 * WIDTH, 256), BF),
            pltpu.SemaphoreType.DMA((10,)),
        ],
        compiler_params=room(62),
        cost_estimate=pl.CostEstimate(
            flops=2_000_000_000, bytes_accessed=12_000_000, transcendentals=600_000
        ),
        interpret=interpret,
    )(*operands)


def far_call(*operands, interpret=False):
    part = jax.ShapeDtypeStruct((16, 2, 24, 384), F32)
    sent = jax.ShapeDtypeStruct((16, 2, 24, 384), BF)
    return pl.pallas_call(
        far_kernel,
        out_shape=(jax.ShapeDtypeStruct((TOK, WIDTH), F32), part, sent),
        in_specs=[SMEM] + [VMEM] * 6 + [ANY] * 6,
        out_specs=(VMEM,) * 3,
        scratch_shapes=[
            pltpu.VMEM((4, 384, WIDTH), BF),
            pltpu.VMEM((4, 576, WIDTH), BF),
            pltpu.VMEM((4, 192, WIDTH), BF),
            pltpu.VMEM((FAR, WIDTH), BF),
            pltpu.VMEM((2 * WIDTH, FAR), BF),
            pltpu.VMEM((WIDTH, TOK), F32),
            pltpu.VMEM((WIDTH, TOK), BF),
            pltpu.SemaphoreType.DMA((14,)),
        ],
        compiler_params=room(60),
        cost_estimate=pl.CostEstimate(
            flops=3_000_000_000, bytes_accessed=16_000_000, transcendentals=1_000_000
        ),
        interpret=interpret,
    )(*operands)


def spread(block, axes, size):
    return lax.all_to_all(
        jnp.broadcast_to(block[None], (size,) + block.shape), axes, 0, 0, tiled=True
    )


def swap(value, axis):
    return lax.ppermute(value, axis, [(0, 1), (1, 0)])


def shards(tiles, counts, w_in, w_qkv, w_out, cotangent):
    rows = tiles[0]
    count = counts[0, 0]
    yx = lax.axis_index("y") * 4 + lax.axis_index("x")
    zl = lax.axis_index("zm") * 4 + lax.axis_index("zn")
    zh, core = lax.axis_index("zh"), lax.axis_index("core")
    w_out = w_out.T
    scal = jnp.stack([count, zh, core, yx * 64 + zl * 8]).astype(jnp.int32)
    own, ahead, even = prepare_call(scal, rows, w_in, w_qkv.T, w_out)
    line = lax.all_to_all(ahead.reshape(16, 8, WIDTH), ("zh",) + ZL, 0, 0, tiled=True)
    line = line.reshape(2, 64, WIDTH)
    mate = swap(own, "core")
    partner = lax.ppermute(even, "zn", [(i, i ^ 1) for i in range(4)])
    line, mate, partner = lax.optimization_barrier((line, mate, partner))
    pieces, far_rows = split_call(scal, line)
    got = lax.all_to_all(pieces, YX, 0, 0, tiled=True).reshape(1024, WIDTH)
    over_rest = swap(w_out[64:], "zh")
    got, over_rest, far_rows = lax.optimization_barrier((got, over_rest, far_rows))
    far = lax.all_to_all(far_rows, YX, 0, 0, tiled=True)
    cross, cross_rest = swap(got, "core"), swap(over_rest, "core")
    packs = (own, mate, got, cross)
    state = near_call(scal, rows, partner, *packs)
    out, keep, send = far_call(
        scal, far, *state, cotangent[0], *packs, over_rest, cross_rest
    )
    pair = (keep + swap(send, "core").astype(F32)).astype(BF)
    plane = lax.all_to_all(pair, YX, 0, 0, tiled=True)
    plane = jnp.sum(plane.astype(F32), axis=0).astype(BF)
    near_z = spread(plane, "zn", 4)
    near_z = jnp.sum(near_z.astype(F32), axis=0).astype(BF)
    column = jnp.broadcast_to(near_z[:, None], (2, 2, 24, 384)).reshape(4, 24, 384)
    column = lax.all_to_all(column, ("zh", "zm"), 0, 0, tiled=True)
    total = jnp.sum(column.astype(F32), axis=0)
    whole = spread(total, YX, 16)
    grad = whole.reshape(8, 2, 24, 384).transpose(0, 2, 1, 3).reshape(192, WIDTH)
    return (out[None], grad)


def solution(mesh):
    fine = Mesh(mesh.devices.reshape(4, 4, 2, 4, 2, 2), ("y", "x", "zm", "zn", "zh", "core"))
    seq, slide = YX + ZL, ("zh", "core")
    placed = (
        P(slide, seq, None),
        P(slide, seq),
        P(slide, None),
        P(None, slide),
        P(None, slide),
        P(slide, seq, None),
    )
    return jax.shard_map(
        shards,
        mesh=fine,
        in_specs=placed,
        out_specs=(P(slide, seq, None), P(slide, None)),
        check_vma=False,
    )
```

time: 204 us -> 248 us (1.22)
  Pallas kernels: 20.8 us -> 79.7 us
  blocking collectives: 94.8 us -> 59.4 us
  waiting for transfers between devices: 31.1 us -> 52.9 us
  starting transfers between devices: 32.9 us -> 48.7 us
  local copies, waits for them, and re-layouts: 15.5 us -> 2.42 us
  other arithmetic: 6.38 us -> 2.13 us
    pallas_call x0 -> x2, Pallas kernels: none -> 58.9 us  [the longest x1 56.5 us: prepare_call(): pl.pallas_call(prepare_kernel, out_shape=(jax.ShapeDtypeStruct((PACK, WID...]
    all_to_all x2, blocking collectives: 43.3 us -> 22.1 us  [spread(): lax.all_to_all(jnp.broadcast_to(block[None], (size,) + block.shape), axes...]
    all_to_all x1, blocking collectives: 36.1 us -> 21.9 us  [shards(): column = lax.all_to_all(column, ('zh', 'zm'), 0, 0, tiled=True)]
    all_to_all x2 -> x3, starting transfers between devices: 17 us -> 29.4 us  [the longest x1 15.2 us: shards(): lax.all_to_all(ahead.reshape(16, 8, WIDTH), ('zh',) + ZL, 0, 0, tiled=True)]
    ppermute x1, waiting for transfers between devices: 0.01 us -> 12.2 us  [shards(): partner = lax.ppermute(even, 'zn', [(i, i ^ 1) for i in range(4)])]
    ppermute x4 -> x5, waiting for transfers between devices: 12.9 us -> 22.1 us  [swap(): return lax.ppermute(value, axis, [(0, 1), (1, 0)])]
    slice x4 -> x1, local copies, waits for them, and re-layouts: 5.29 us -> 0.01 us  [shards(): over_rest = swap(w_out[64:], 'zh')]
    ppermute x4 -> x5, starting transfers between devices: 14 us -> 17.3 us  [swap(): return lax.ppermute(value, axis, [(0, 1), (1, 0)])]
  transfers between devices with their start and end apart: 7 -> 9, of which waited for: 3 -> 5; matrix products, arithmetic and copies ran while one was open for 7% -> 0% of each run, Pallas kernels for 4% -> 3%
where the time goes in v3:
time: 248 us; the launch traced here: 247 us
  Pallas kernels  79.7 us (32%)
  blocking collectives  59.4 us (24%)
  waiting for transfers between devices  52.9 us (21%)
  starting transfers between devices  48.7 us (20%)
    pallas_call x1, Pallas kernels, prepare_call(): pl.pallas_call(prepare_kernel, out_shape=(jax.ShapeDtypeStruct((PACK, WID...  56.5 us
    ppermute x5, waiting for transfers between devices, swap(): return lax.ppermute(value, axis, [(0, 1), (1, 0)])  22.1 us
    all_to_all x2, blocking collectives, spread(): lax.all_to_all(jnp.broadcast_to(block[None], (size,) + block.shape), axes...  22.1 us
    all_to_all x1, blocking collectives, shards(): column = lax.all_to_all(column, ('zh', 'zm'), 0, 0, tiled=True)  21.9 us
    ppermute x5, starting transfers between devices, swap(): return lax.ppermute(value, axis, [(0, 1), (1, 0)])  17.3 us
    all_to_all x1, waiting for transfers between devices, shards(): far = lax.all_to_all(far_rows, YX, 0, 0, tiled=True)  15.9 us
    all_to_all x1, blocking collectives, shards(): plane = lax.all_to_all(pair, YX, 0, 0, tiled=True)  15.4 us
    all_to_all x1, starting transfers between devices, shards(): lax.all_to_all(ahead.reshape(16, 8, WIDTH), ('zh',) + ZL, 0, 0, tiled=True)  15.2 us
  transfers between devices with their start and end apart: 9, of which 5 were waited for; matrix products, arithmetic and copies ran while one was open for 0% of the time, Pallas kernels for 3%

profile of v3, /device:TPU:32, one launch (start us, length us, event | category | flops | bytes accessed | tf_op | source)
XLA Modules:
  0.0 246.8 jit_solution(3952091121538170352)
XLA Ops:
  1.3 0.6 pad_add_fusion.scal
  1.9 56.5 %shard_map.77 = (bf16[1152,768]{1,0:T(8,128)(2,1)}, bf16[2,64,768]{2,1,0:T(8,128)(2,1)}, bf16[64,1536]{1,0:T(8,128)(2,1)}) custom-call(s32[4]{0:T(128)} %pad_add_fusion.scal, bf16[128,1536]{1,0:T(8,128)(2,1)} %bitcast.30, bf16[384,768]{1,0:T(8,128)(2,1)} %w_in.1, bf16[576,768]{1,0:T(8,128)(2,1)} %bitcast.26, bf16[192,768]{1,0:T(8,128)(2,1)} %bitcast.27), custom_call_target="tpu_custom_call" | custom-call | tf_op jit(solution)/shard_map/pallas_call | solution.py:238
  58.4 1.9 collective-permute-start
  60.3 15.2 %all-to-all-start = ((bf16[16,8,768]{2,1,0:T(8,128)(2,1)}), bf16[16,8,768]{2,1,0:T(8,128)(2,1)S(1)}, u32[]{:S(2)}, u32[]{:S(2)}) async-start(bf16[16,8,768]{2,1,0:T(8,128)(2,1)} %bitcast.33), calls=%async_computation | async-start | bytes 393216 | tf_op jit(solution)/shard_map/all_to_all | solution.py:351
  75.5 2.0 collective-permute-start.1
  77.6 12.2 %collective-permute-done.1.partner = bf16[64,1536]{1,0:T(8,128)(2,1)S(1)} collective-permute-done((bf16[64,1536]{1,0:T(8,128)(2,1)}, bf16[64,1536]{1,0:T(8,128)(2,1)S(1)}, u32[]{:S(2)}, u32[]{:S(2)}) %collective-permute-start.1) | collective-permute-done | bytes 196640 | tf_op jit(solution)/shard_map/ppermute | solution.py:354
  89.8 2.6 %all-to-all-done = bf16[16,8,768]{2,1,0:T(8,128)(2,1)S(1)} async-done(((bf16[16,8,768]{2,1,0:T(8,128)(2,1)}), bf16[16,8,768]{2,1,0:T(8,128)(2,1)S(1)}, u32[]{:S(2)}, u32[]{:S(2)}) %all-to-all-start) | async-done | bytes 196640 | tf_op jit(solution)/shard_map/all_to_all | solution.py:351
  92.4 0.0 collective-permute-done.mate
  92.4 2.4 shard_map.78
  94.8 7.2 %all-to-all-start.1 = ((bf16[16,64,768]{2,1,0:T(8,128)(2,1)}), bf16[16,64,768]{2,1,0:T(8,128)(2,1)S(1)}, u32[]{:S(2)}, u32[]{:S(2)}) async-start(bf16[16,64,768]{2,1,0:T(8,128)(2,1)} %get-tuple-element.24), calls=%async_computation.1 | async-start | bytes 3145728 | tf_op jit(solution)/shard_map/all_to_all | solution.py:357
  102.0 9.5 %collective-permute-start.2 = (bf16[128,768]{1,0:T(8,128)(2,1)S(1)}, bf16[128,768]{1,0:T(8,128)(2,1)S(1)}, u32[]{:S(2)}, u32[]{:S(2)}) collective-permute-start(bf16[128,768]{1,0:T(8,128)(2,1)S(1)} %slice.4), channel_id=1, source_target_pairs={{0,2},{2,0},{1,3},{3,1},{4,6},{6,4},{5,7},{7,5},{8,10},{10,8},{9,1... | collective-permute-start | bytes 589832 | tf_op jit(solution)/shard_map/ppermute | solution.py:339
  111.5 19.9 %collective-permute-done.2.over_rest = bf16[128,768]{1,0:T(8,128)(2,1)S(1)} collective-permute-done((bf16[128,768]{1,0:T(8,128)(2,1)S(1)}, bf16[128,768]{1,0:T(8,128)(2,1)S(1)}, u32[]{:S(2)}, u32[]{:S(2)}) %collective-permute-start.2) | collective-permute-done | bytes 196640 | tf_op jit(solution)/shard_map/ppermute | solution.py:339
  131.4 0.0 all-to-all-done.1
  131.5 1.9 collective-permute-start.3
  133.4 7.0 %all-to-all-start.2 = ((bf16[16,64,768]{2,1,0:T(8,128)(2,1)}), bf16[16,64,768]{2,1,0:T(8,128)(2,1)}, u32[]{:S(2)}, u32[]{:S(2)}) async-start(bf16[16,64,768]{2,1,0:T(8,128)(2,1)} %get-tuple-element.26), calls=%async_computation.2 | async-start | bytes 3145728 | tf_op jit(solution)/shard_map/all_to_all | solution.py:360
  140.4 2.1 collective-permute-start.4
  142.5 0.0 collective-permute-done.3.cross
  142.5 1.2 copy-done.4
  143.7 7.3 %shard_map.79 = (bf16[16,128,48]{2,1,0:T(8,128)(2,1)}, f32[768,128]{1,0:T(8,128)}, f32[128,128]{1,0:T(8,128)}, f32[128,128]{1,0:T(8,128)}) custom-call(s32[4]{0:T(128)} %pad_add_fusion.scal, bf16[128,1536]{1,0:T(8,128)(2,1)} %bitcast.31, bf16[64,1536]{1,0:T(8,128)(2,1)} %copy-done.5, bf16[1152,768]{1,0:T(8,128)(2,1)} %get-tuple-element.21.own, ...), custom_call_target="tpu_custom_call" | custom-call | flops 2000000000 | bytes 12000000 | tf_op jit(solution)/shard_map/pallas_call | solution.py:280
  151.0 0.0 collective-permute-done.4.cross_rest
  151.0 15.9 %all-to-all-done.2.far = bf16[16,64,768]{2,1,0:T(8,128)(2,1)} async-done(((bf16[16,64,768]{2,1,0:T(8,128)(2,1)}), bf16[16,64,768]{2,1,0:T(8,128)(2,1)}, u32[]{:S(2)}, u32[]{:S(2)}) %all-to-all-start.2) | async-done | bytes 1572896 | tf_op jit(solution)/shard_map/all_to_all | solution.py:360
  167.0 13.5 %shard_map.80 = (f32[128,768]{1,0:T(8,128)}, f32[16,2,24,384]{3,2,1,0:T(8,128)}, bf16[16,2,24,384]{3,2,1,0:T(8,128)(2,1)}) custom-call(s32[4]{0:T(128)} %pad_add_fusion.scal, bf16[16,64,768]{2,1,0:T(8,128)(2,1)} %all-to-all-done.2.far, bf16[16,128,48]{2,1,0:T(8,128)(2,1)} %get-tuple-element.30.query, f32[768,128]{1,0:T(8,128)} %get-tuple-element.31.near_mixed, ...), custom_call_target="tpu_custom_call" | custom-call | flops 3000000000 | bytes 16000000 | tf_op jit(solution)/shard_map/pallas_call | solution.py:309
  180.5 1.9 collective-permute-start.5
  182.4 2.2 collective-permute-done.5
  184.6 1.4 add_convert_fusion
  186.0 15.4 %all_to_all.35 = bf16[16,2,24,384]{3,2,1,0:T(8,128)(2,1)S(1)} all-to-all(bf16[16,2,24,384]{3,2,1,0:T(8,128)(2,1)S(1)} %add_convert_fusion), channel_id=1, replica_groups=mesh['y'=4,'x'=4,'zm'=2,'zn'=4,'zh'=2,'core'=2] {'y','x'}, dimensions={0} | all-to-all | bytes 1179648 | tf_op jit(solution)/shard_map/all_to_all | solution.py:368
  201.4 0.1 reduce_sum.33
  201.5 8.4 %all_to_all.36 = bf16[4,2,24,384]{3,2,1,0:T(8,128)(2,1)S(1)} all-to-all(bf16[4,2,24,384]{3,2,1,0:T(8,128)(2,1)S(1)} %broadcast_in_dim.9), channel_id=1, replica_groups=mesh['y'=4,'x'=4,'zm'=2,'zn'=4,'zh'=2,'core'=2] {'zn'}, dimensions={0} | all-to-all | bytes 294912 | tf_op jit(solution)/shard_map/all_to_all | solution.py:333
  210.0 21.9 %all_to_all.37 = bf16[4,24,384]{2,1,0:T(8,128)(2,1)S(1)} all-to-all(bf16[4,24,384]{2,1,0:T(8,128)(2,1)S(1)} %bitcast.32), channel_id=1, replica_groups=mesh['y'=4,'x'=4,'zm'=2,'zn'=4,'zh'=2,'core'=2] {'zh','zm'}, dimensions={0} | all-to-all | bytes 147456 | tf_op jit(solution)/shard_map/all_to_all | solution.py:373
  232.0 13.7 %all_to_all.38 = f32[16,24,384]{2,1,0:T(8,128)S(1)} all-to-all(f32[16,24,384]{2,1,0:T(8,128)S(1)} %broadcast_in_dim.11), channel_id=1, replica_groups=mesh['y'=4,'x'=4,'zm'=2,'zn'=4,'zh'=2,'core'=2] {'y','x'}, dimensions={0} | all-to-all | bytes 1179648 | tf_op jit(solution)/shard_map/all_to_all | solution.py:333
  245.6 0.3 copy.9
  245.9 0.9 copy.10
  (21 shorter events, 0.1 us)
Async XLA Ops:
  1.9 90.5 %copy-start = (s32[4]{0:T(128)S(1)}, s32[4]{0:T(128)}, u32[]{:S(2)}) copy-start(s32[4]{0:T(128)} %pad_add_fusion.scal) | copy-start | bytes 52
  58.4 34.0 %collective-permute-start = (bf16[1152,768]{1,0:T(8,128)(2,1)}, bf16[1152,768]{1,0:T(8,128)(2,1)S(1)}, u32[]{:S(2)}, u32[]{:S(2)}) collective-permute-start(bf16[1152,768]{1,0:T(8,128)(2,1)} %get-tuple-element.21.own), channel_id=1, source_target_pairs={{0,1},{1,0},{2,3},{3,2},{4,5},{5,4},{6,7},{7,6},{8,9},{9,8},{10,11... | collective-permute-start | bytes 5308424 | tf_op jit(solution)/shard_map/ppermute | solution.py:339
  60.3 32.1 %all-to-all-start = ((bf16[16,8,768]{2,1,0:T(8,128)(2,1)}), bf16[16,8,768]{2,1,0:T(8,128)(2,1)S(1)}, u32[]{:S(2)}, u32[]{:S(2)}) async-start(bf16[16,8,768]{2,1,0:T(8,128)(2,1)} %bitcast.33), calls=%async_computation | async-start | bytes 393216 | tf_op jit(solution)/shard_map/all_to_all | solution.py:351
  75.5 14.2 %collective-permute-start.1 = (bf16[64,1536]{1,0:T(8,128)(2,1)}, bf16[64,1536]{1,0:T(8,128)(2,1)S(1)}, u32[]{:S(2)}, u32[]{:S(2)}) collective-permute-start(bf16[64,1536]{1,0:T(8,128)(2,1)} %get-tuple-element.22), channel_id=1, source_target_pairs={{0,4},{4,0},{8,12},{12,8},{1,5},{5,1},{9,13},{13,9},{2,6},{6,2},{1... | collective-permute-start | bytes 589832 | tf_op jit(solution)/shard_map/ppermute | solution.py:354
  89.8 5.1 %copy-start.5 = (bf16[64,1536]{1,0:T(8,128)(2,1)}, bf16[64,1536]{1,0:T(8,128)(2,1)S(1)}, u32[]{:S(2)}) copy-start(bf16[64,1536]{1,0:T(8,128)(2,1)S(1)} %collective-permute-done.1.partner) | copy-start | bytes 589828
  92.4 2.4 copy-start.3
  94.8 7.2 %copy-start.2 = (bf16[768,192]{0,1:T(8,128)(2,1)S(1)}, bf16[768,192]{0,1:T(8,128)(2,1)}, u32[]{:S(2)}) copy-start(bf16[768,192]{0,1:T(8,128)(2,1)} %param.10) | copy-start | bytes 884740
  94.8 36.6 %all-to-all-start.1 = ((bf16[16,64,768]{2,1,0:T(8,128)(2,1)}), bf16[16,64,768]{2,1,0:T(8,128)(2,1)S(1)}, u32[]{:S(2)}, u32[]{:S(2)}) async-start(bf16[16,64,768]{2,1,0:T(8,128)(2,1)} %get-tuple-element.24), calls=%async_computation.1 | async-start | bytes 3145728 | tf_op jit(solution)/shard_map/all_to_all | solution.py:357
  102.0 29.4 %collective-permute-start.2 = (bf16[128,768]{1,0:T(8,128)(2,1)S(1)}, bf16[128,768]{1,0:T(8,128)(2,1)S(1)}, u32[]{:S(2)}, u32[]{:S(2)}) collective-permute-start(bf16[128,768]{1,0:T(8,128)(2,1)S(1)} %slice.4), channel_id=1, source_target_pairs={{0,2},{2,0},{1,3},{3,1},{4,6},{6,4},{5,7},{7,5},{8,10},{10,8},{9,1... | collective-permute-start | bytes 589832 | tf_op jit(solution)/shard_map/ppermute | solution.py:339
  131.4 8.9 %copy-start.6 = (bf16[128,768]{1,0:T(8,128)(2,1)}, bf16[128,768]{1,0:T(8,128)(2,1)S(1)}, u32[]{:S(2)}) copy-start(bf16[128,768]{1,0:T(8,128)(2,1)S(1)} %collective-permute-done.2.over_rest) | copy-start | bytes 589828
  131.4 1.9 copy-start.1
  131.5 11.0 %collective-permute-start.3 = (bf16[1024,768]{1,0:T(8,128)(2,1)S(1)}, bf16[1024,768]{1,0:T(8,128)(2,1)S(1)}, u32[]{:S(2)}, u32[]{:S(2)}) collective-permute-start(bf16[1024,768]{1,0:T(8,128)(2,1)S(1)} %bitcast.23), channel_id=1, source_target_pairs={{0,1},{1,0},{2,3},{3,2},{4,5},{5,4},{6,7},{7,6},{8,9},{9,8},{10,11... | collective-permute-start | bytes 4718600 | tf_op jit(solution)/shard_map/ppermute | solution.py:339
  133.4 33.6 %all-to-all-start.2 = ((bf16[16,64,768]{2,1,0:T(8,128)(2,1)}), bf16[16,64,768]{2,1,0:T(8,128)(2,1)}, u32[]{:S(2)}, u32[]{:S(2)}) async-start(bf16[16,64,768]{2,1,0:T(8,128)(2,1)} %get-tuple-element.26), calls=%async_computation.2 | async-start | bytes 3145728 | tf_op jit(solution)/shard_map/all_to_all | solution.py:360
  140.4 10.6 %collective-permute-start.4 = (bf16[128,768]{1,0:T(8,128)(2,1)S(1)}, bf16[128,768]{1,0:T(8,128)(2,1)S(1)}, u32[]{:S(2)}, u32[]{:S(2)}) collective-permute-start(bf16[128,768]{1,0:T(8,128)(2,1)S(1)} %collective-permute-done.2.over_rest), channel_id=1, source_target_pairs={{0,1},{1,0},{2,3},{3,2},{4,5},{5,4},{6,7},{7,6},{8,9},{9,8},{10,11... | collective-permute-start | bytes 589832 | tf_op jit(solution)/shard_map/ppermute | solution.py:339
  142.5 1.2 copy-start.4
  151.0 16.0 %copy-start.7 = (bf16[128,768]{1,0:T(8,128)(2,1)}, bf16[128,768]{1,0:T(8,128)(2,1)S(1)}, u32[]{:S(2)}) copy-start(bf16[128,768]{1,0:T(8,128)(2,1)S(1)} %collective-permute-done.4.cross_rest) | copy-start | bytes 589828
  180.5 4.1 %collective-permute-start.5 = (bf16[16,2,24,384]{3,2,1,0:T(8,128)(2,1)}, bf16[16,2,24,384]{3,2,1,0:T(8,128)(2,1)S(1)}, u32[]{:S(2)}, u32[]{:S(2)}) collective-permute-start(bf16[16,2,24,384]{3,2,1,0:T(8,128)(2,1)} %get-tuple-element.37), channel_id=1, source_target_pairs={{0,1},{1,0},{2,3},{3,2},{4,5},{5,4},{6,7},{7,6},{8,9},{9,8},{10,11... | collective-permute-start | bytes 1769480 | tf_op jit(solution)/shard_map/ppermute | solution.py:339

commit v4 on v3

v4 whole, which is shorter than its diff:
```python
import jax
import jax.numpy as jnp
from jax import lax
from jax.experimental import pallas as pl
from jax.experimental.pallas import tpu as pltpu
from jax.sharding import Mesh
from jax.sharding import PartitionSpec as P

WIDTH = 768
TILE = 1536
HEADS = 16
HEAD = 48
DIL = 32
TOK = 128
FAR = 512
PACK = 1152
YX = ("y", "x")
Z = ("zh", "zl")
NT = (((1,), (1,)), ((), ()))
NN = (((1,), (0,)), ((), ()))
BF = jnp.bfloat16
F32 = jnp.float32
MARK = 64.0
LOW = -1e30
LOG2 = 0.6931471805599453


def dot(a, b, dims):
    return lax.dot_general(a, b, dims, preferred_element_type=F32)


def key_bias(block):
    lane = lax.broadcasted_iota(jnp.int32, (16, TOK), 1)
    pick = jnp.where(lane == 0, F32(1), F32(0)).astype(BF)
    return jnp.where(dot(pick, block[:, :TOK], NT)[0:1] > MARK / 2, F32(LOW), F32(0))


def layer_kernel(
    scal,
    rows,
    partner,
    own,
    mate,
    got,
    cross,
    over_rest,
    cross_rest,
    cot,
    out,
    keep,
    send,
    near,
    far,
    win,
    wqkv,
    wout,
    hid,
    kv,
    mixed,
    attn,
    sems,
):
    count, zh, core = scal[0], scal[1], scal[2]
    mine, other = zh * 2 + core, zh * 2 + 1 - core
    over, over_other = (1 - zh) * 2 + core, (1 - zh) * 2 + 1 - core
    arrived = got.at[:, pl.ds(0, 64)]
    moves = [
        (own.at[pl.ds(0, 6)], win.at[mine]),
        (mate.at[pl.ds(0, 6)], win.at[other]),
        (arrived.at[pl.ds(0, 6)], win.at[over]),
        (cross.at[pl.ds(0, 6)], win.at[over_other]),
        (rows, near.at[pl.ds(0, TOK)]),
        (partner, near.at[pl.ds(TOK, TOK // 2)]),
        (got.at[:, pl.ds(64, 64)], far),
        (own.at[pl.ds(6, 9)], wqkv.at[mine]),
        (mate.at[pl.ds(6, 9)], wqkv.at[other]),
        (arrived.at[pl.ds(6, 9)], wqkv.at[over]),
        (cross.at[pl.ds(6, 9)], wqkv.at[over_other]),
        (own.at[pl.ds(15, 3)], wout.at[mine]),
        (mate.at[pl.ds(15, 3)], wout.at[other]),
        (arrived.at[15], wout.at[over, 0]),
        (cross.at[15], wout.at[over_other, 0]),
        (over_rest, wout.at[over, pl.ds(1, 2)]),
        (cross_rest, wout.at[over_other, pl.ds(1, 2)]),
    ]
    copies = [pltpu.make_async_copy(s, d, sems.at[i]) for i, (s, d) in enumerate(moves)]
    for c in copies:
        c.start()
    near[pl.ds(192, 64), :] = jnp.zeros((64, TILE), BF)
    lane = lax.broadcasted_iota(jnp.int32, (1, TOK), 1)
    twice = jnp.where(lane & 1 == 0, F32(LOG2), F32(0))
    for c in copies[:7]:
        c.wait()
    left = far[:, pl.ds(0, 32), :].reshape(FAR, WIDTH)
    right = far[:, pl.ds(32, 32), :].reshape(FAR, WIDTH)
    weight = win[...].reshape(TILE, WIDTH)
    hid[pl.ds(0, 256), :] = dot(near[...], weight, NN).astype(BF)
    hid[pl.ds(256, FAR), :] = (
        dot(left, weight[:WIDTH], NN) + dot(right, weight[WIDTH:], NN)
    ).astype(BF)
    bias = jnp.concatenate(
        [
            jnp.where(lane < count, twice, F32(LOW)),
            key_bias(near[pl.ds(TOK, 64), :]),
            jnp.full((1, 64), LOW, F32),
            key_bias(left),
        ],
        axis=1,
    )
    for c in copies[7:11]:
        c.wait()
    flat = wqkv[...].reshape(3 * WIDTH, WIDTH)
    kv[...] = dot(flat[WIDTH:], hid[...], NT).astype(BF)
    own_hid = hid[pl.ds(0, TOK), :]
    column = lax.broadcasted_iota(jnp.int32, (TOK, TOK), 1)
    totals = jnp.ones((TOK, TOK), F32)
    for h in range(HEADS):
        q = dot(own_hid, flat[h * HEAD : (h + 1) * HEAD], NT).astype(BF)
        s = dot(q, kv[pl.ds(h * HEAD, HEAD), :], NN) * F32(HEAD**-0.5) + bias
        p = jnp.exp(s - jnp.max(s, axis=1, keepdims=True))
        totals = jnp.where(column == h, jnp.sum(p, axis=1, keepdims=True), totals)
        mixed[pl.ds(h * HEAD, HEAD), :] = dot(
            kv[pl.ds(WIDTH + h * HEAD, HEAD), :], p.astype(BF), NT
        )
    inverse = 1.0 / totals.T
    for h in range(HEADS):
        at = pl.ds(h * HEAD, HEAD)
        attn[at, :] = (mixed[at, :] * inverse[h : h + 1, :]).astype(BF)
    cotangent = cot[...]
    token = lax.broadcasted_iota(jnp.int32, (192, TOK), 1)
    for which, target in ((core, keep), (1 - core, send)):
        for half in range(2):
            start = pl.multiple_of(half * 384 + which * 192, 192)
            block = attn[pl.ds(start, 192), :]
            block = jnp.where(token < count, block, jnp.zeros_like(block))
            part = dot(block, cotangent, NN)
            for r in range(8):
                for c in range(2):
                    target[r * 2 + c, half] = part[r * 24 : r * 24 + 24, c * 384 : c * 384 + 384].astype(
                        target.dtype
                    )
    for c in copies[11:]:
        c.wait()
    out[...] = dot(wout[...].reshape(WIDTH, WIDTH), attn[...], NN).T


ANY = pl.BlockSpec(memory_space=pl.ANY)
VMEM = pl.BlockSpec(memory_space=pltpu.VMEM)
SMEM = pl.BlockSpec(memory_space=pltpu.SMEM)


def room(mebibytes):
    return pltpu.CompilerParams(vmem_limit_bytes=mebibytes * 1024 * 1024)


def prepare_kernel(scal, rows, w_in, w_qkv, w_out, own, ahead, even, sems):
    count, zh, at = scal[0], scal[1], scal[3]
    moves = [
        (w_in, own.at[pl.ds(0, 384)]),
        (w_qkv, own.at[pl.ds(384, 576)]),
        (w_out, own.at[pl.ds(960, 192)]),
    ]
    copies = [pltpu.make_async_copy(s, d, sems.at[i]) for i, (s, d) in enumerate(moves)]
    for c in copies:
        c.start()
    lane = lax.broadcasted_iota(jnp.int32, (1, TILE), 1)
    mark = jnp.where(lane == 0, F32(MARK), F32(0))
    distant = jnp.concatenate(
        [
            jnp.where(DIL * j < count, rows[pl.ds(DIL * j, 16), :].astype(F32)[0:1], mark)
            for j in range(4)
        ],
        axis=0,
    )
    row = lax.broadcasted_iota(jnp.int32, (TOK // 2, TOK), 0)
    source = lax.broadcasted_iota(jnp.int32, (TOK // 2, TOK), 1)
    pick = jnp.where((source == 2 * row) & (source < count), F32(1), F32(0)).astype(BF)
    marks = jnp.where(
        2 * lax.broadcasted_iota(jnp.int32, (TOK // 2, TILE), 0) < count, F32(0), mark
    )
    even[...] = (dot(pick, rows[...], NN) + marks).astype(BF)
    for c in copies:
        c.wait()
    start = pl.multiple_of(at // 16 * 16, 16)
    wide = own[pl.ds(start, 16), :].astype(F32)
    eight = jnp.where(at > start, wide[8:16], wide[0:8])
    far = jnp.concatenate([distant[:, :WIDTH], distant[:, WIDTH:]], axis=0)
    for half in range(2):
        value = jnp.where(zh == half, far, eight)
        ahead[half] = jnp.concatenate([value] * 8, axis=0).astype(BF)


def prepare_call(*operands, interpret=False):
    return pl.pallas_call(
        prepare_kernel,
        out_shape=(
            jax.ShapeDtypeStruct((PACK, WIDTH), BF),
            jax.ShapeDtypeStruct((2, 64, WIDTH), BF),
            jax.ShapeDtypeStruct((TOK // 2, TILE), BF),
        ),
        in_specs=[SMEM, VMEM] + [ANY] * 3,
        out_specs=(VMEM, VMEM, VMEM),
        scratch_shapes=[pltpu.SemaphoreType.DMA((3,))],
        compiler_params=room(62),
        interpret=interpret,
    )(*operands)


def split_kernel(scal, line, payload):
    zh = scal[1]
    piece = line[1 - zh]
    target = lax.broadcasted_iota(jnp.int32, (64, 64), 0)
    source = lax.broadcasted_iota(jnp.int32, (64, 64), 1)
    origin = (target & 31) // 4 * 8 + target // 32 * 4 + (target & 3)
    pick = jnp.where(source == origin, F32(1), F32(0)).astype(BF)
    ordered = dot(pick, line[zh], NN).astype(BF)
    both = jnp.concatenate([piece, ordered], axis=0)
    for i in range(16):
        payload[i] = both


def split_call(*operands, interpret=False):
    return pl.pallas_call(
        split_kernel,
        out_shape=jax.ShapeDtypeStruct((16, 128, WIDTH), BF),
        in_specs=[SMEM, VMEM],
        out_specs=VMEM,
        compiler_params=room(16),
        interpret=interpret,
    )(*operands)


def layer_call(*operands, interpret=False):
    part = jax.ShapeDtypeStruct((16, 2, 24, 384), F32)
    sent = jax.ShapeDtypeStruct((16, 2, 24, 384), BF)
    return pl.pallas_call(
        layer_kernel,
        out_shape=(jax.ShapeDtypeStruct((TOK, WIDTH), F32), part, sent),
        in_specs=[SMEM] + [ANY] * 8 + [VMEM],
        out_specs=(VMEM,) * 3,
        scratch_shapes=[
            pltpu.VMEM((256, TILE), BF),
            pltpu.VMEM((16, 64, WIDTH), BF),
            pltpu.VMEM((4, 6, 64, WIDTH), BF),
            pltpu.VMEM((4, 9, 64, WIDTH), BF),
            pltpu.VMEM((4, 3, 64, WIDTH), BF),
            pltpu.VMEM((WIDTH, WIDTH), BF),
            pltpu.VMEM((2 * WIDTH, WIDTH), BF),
            pltpu.VMEM((WIDTH, TOK), F32),
            pltpu.VMEM((WIDTH, TOK), BF),
            pltpu.SemaphoreType.DMA((17,)),
        ],
        compiler_params=room(62),
        interpret=interpret,
    )(*operands)


def spread(block, axes, size):
    return lax.all_to_all(
        jnp.broadcast_to(block[None], (size,) + block.shape), axes, 0, 0, tiled=True
    )


def swap(value, axis):
    return lax.ppermute(value, axis, [(0, 1), (1, 0)])


def shards(tiles, counts, w_in, w_qkv, w_out, cotangent):
    rows = tiles[0]
    count = counts[0, 0]
    yx = lax.axis_index("y") * 4 + lax.axis_index("x")
    zl = lax.axis_index("zl")
    zh, core = lax.axis_index("zh"), lax.axis_index("core")
    w_out = w_out.T
    scal = jnp.stack([count, zh, core, yx * 64 + zl * 8]).astype(jnp.int32)
    own, ahead, even = prepare_call(scal, rows, w_in, w_qkv.T, w_out)
    line = lax.all_to_all(ahead.reshape(16, 8, WIDTH), Z, 0, 0, tiled=True)
    mate = swap(own, "core")
    line, mate, even = lax.optimization_barrier((line.reshape(2, 64, WIDTH), mate, even))
    partner = lax.ppermute(even, "zl", [(i, i ^ 1) for i in range(8)])
    over_rest = swap(w_out[64:], "zh")
    got = lax.all_to_all(split_call(scal, line), YX, 0, 0, tiled=True)
    cross_rest = swap(over_rest, "core")
    got, over_rest, cross_rest, partner = lax.optimization_barrier(
        (got, over_rest, cross_rest, partner)
    )
    cross = swap(got[:, :64], "core")
    out, keep, send = layer_call(
        scal,
        rows,
        partner,
        own.reshape(18, 64, WIDTH),
        mate.reshape(18, 64, WIDTH),
        got,
        cross,
        over_rest.reshape(2, 64, WIDTH),
        cross_rest.reshape(2, 64, WIDTH),
        cotangent[0],
    )
    pair = (keep + swap(send, "core").astype(F32)).astype(BF)
    plane = lax.all_to_all(pair, YX, 0, 0, tiled=True)
    plane = jnp.sum(plane.astype(F32), axis=0).astype(BF)
    column = jnp.broadcast_to(plane[:, None], (2, 8, 24, 384)).reshape(16, 24, 384)
    column = lax.all_to_all(column, Z, 0, 0, tiled=True)
    total = jnp.sum(column.astype(F32), axis=0)
    whole = spread(total, YX, 16)
    grad = whole.reshape(8, 2, 24, 384).transpose(0, 2, 1, 3).reshape(192, WIDTH)
    return (out[None], grad)


def solution(mesh):
    fine = Mesh(mesh.devices.reshape(4, 4, 8, 2, 2), ("y", "x", "zl", "zh", "core"))
    seq, slide = YX + ("zl",), ("zh", "core")
    placed = (
        P(slide, seq, None),
        P(slide, seq),
        P(slide, None),
        P(None, slide),
        P(None, slide),
        P(slide, seq, None),
    )
    return jax.shard_map(
        shards,
        mesh=fine,
        in_specs=placed,
        out_specs=(P(slide, seq, None), P(slide, None)),
        check_vma=False,
    )
```

time: 248 us -> 183 us (0.74)
  Pallas kernels: 79.7 us -> 23.2 us
  blocking collectives: 59.4 us -> 88 us
  starting transfers between devices: 48.7 us -> 22.2 us
  waiting for transfers between devices: 52.9 us -> 42.9 us
    pallas_call x1, Pallas kernels: 56.5 us -> 3.77 us  [prepare_call(): pl.pallas_call(prepare_kernel, out_shape=(jax.ShapeDtypeStruct((PACK, WID...]
    all_to_all x1 -> x2, blocking collectives: 21.9 us -> 57.7 us  [the longest x1 31.8 us: shards(): line = lax.all_to_all(ahead.reshape(16, 8, WIDTH), Z, 0, 0, tiled=True)]
    all_to_all x3 -> x1, starting transfers between devices: 29.4 us -> 7.17 us  [shards(): got = lax.all_to_all(split_call(scal, line), YX, 0, 0, tiled=True)]
    all_to_all x3 -> x1, waiting for transfers between devices: 18.6 us -> 8.58 us  [shards(): got = lax.all_to_all(split_call(scal, line), YX, 0, 0, tiled=True)]
    all_to_all x2 -> x1, blocking collectives: 22.1 us -> 14.3 us  [spread(): lax.all_to_all(jnp.broadcast_to(block[None], (size,) + block.shape), axes...]
    ppermute x5, waiting for transfers between devices: 22.1 us -> 26.8 us  [swap(): return lax.ppermute(value, axis, [(0, 1), (1, 0)])]
    ppermute x1, waiting for transfers between devices: 12.2 us -> 7.57 us  [shards(): partner = lax.ppermute(even, 'zl', [(i, i ^ 1) for i in range(8)])]
    ppermute x5, starting transfers between devices: 17.3 us -> 13.1 us  [swap(): return lax.ppermute(value, axis, [(0, 1), (1, 0)])]
  transfers between devices with their start and end apart: 9 -> 7, of which waited for: 5 -> 5; matrix products, arithmetic and copies ran while one was open for 0% -> 0% of each run, Pallas kernels for 3% -> 0%
where the time goes in v4:
time: 183 us
  blocking collectives  88 us (48%)
  waiting for transfers between devices  42.9 us (23%)
  Pallas kernels  23.2 us (13%)
  starting transfers between devices  22.2 us (12%)
  local copies, waits for them, and re-layouts  2.88 us (2%)
  other arithmetic  2.18 us (1%)
    all_to_all x1, blocking collectives, shards(): line = lax.all_to_all(ahead.reshape(16, 8, WIDTH), Z, 0, 0, tiled=True)  31.8 us
    ppermute x5, waiting for transfers between devices, swap(): return lax.ppermute(value, axis, [(0, 1), (1, 0)])  26.8 us
    all_to_all x1, blocking collectives, shards(): column = lax.all_to_all(column, Z, 0, 0, tiled=True)  25.8 us
    pallas_call x1, Pallas kernels, layer_call(): pl.pallas_call(layer_kernel, out_shape=(jax.ShapeDtypeStruct((TOK, WIDTH)...  16.9 us
    all_to_all x1, blocking collectives, shards(): plane = lax.all_to_all(pair, YX, 0, 0, tiled=True)  16.1 us
    all_to_all x1, blocking collectives, spread(): lax.all_to_all(jnp.broadcast_to(block[None], (size,) + block.shape), axes...  14.3 us
    ppermute x5, starting transfers between devices, swap(): return lax.ppermute(value, axis, [(0, 1), (1, 0)])  13.1 us
    all_to_all x1, waiting for transfers between devices, shards(): got = lax.all_to_all(split_call(scal, line), YX, 0, 0, tiled=True)  8.58 us
  transfers between devices with their start and end apart: 7, of which 5 were waited for; matrix products, arithmetic and copies ran while one was open for 0% of the time, Pallas kernels for 0%

profile of v4, /device:TPU:32, one launch (start us, length us, event | category | flops | bytes accessed | tf_op | source)
XLA Modules:
  0.0 182.8 jit_solution(8219440543384838369)
XLA Ops:
  1.3 0.7 pad_add_fusion.scal
  1.9 3.8 %shard_map.77 = (bf16[1152,768]{1,0:T(8,128)(2,1)}, bf16[2,64,768]{2,1,0:T(8,128)(2,1)}, bf16[64,1536]{1,0:T(8,128)(2,1)}) custom-call(s32[4]{0:T(128)} %pad_add_fusion.scal, bf16[128,1536]{1,0:T(8,128)(2,1)} %bitcast.27, bf16[384,768]{1,0:T(8,128)(2,1)} %w_in.1, bf16[576,768]{1,0:T(8,128)(2,1)} %bitcast.30, bf16[192,768]{1,0:T(8,128)(2,1)} %bitcast.31), custom_call_target="tpu_custom_call" | custom-call | tf_op jit(solution)/shard_map/pallas_call | solution.py:194
  5.7 1.9 %collective-permute-start = (bf16[1152,768]{1,0:T(8,128)(2,1)}, bf16[1152,768]{1,0:T(8,128)(2,1)}, u32[]{:S(2)}, u32[]{:S(2)}) collective-permute-start(bf16[1152,768]{1,0:T(8,128)(2,1)} %get-tuple-element.16), channel_id=1, source_target_pairs={{0,1},{1,0},{2,3},{3,2},{4,5},{5,4},{6,7},{7,6},{8,9},{9,8},{10,11... | collective-permute-start | bytes 5308424 | tf_op jit(solution)/shard_map/ppermute | solution.py:265
  7.7 31.8 %all_to_all.25 = bf16[16,8,768]{2,1,0:T(8,128)(2,1)S(1)} all-to-all(bf16[16,8,768]{2,1,0:T(8,128)(2,1)} %bitcast.34), channel_id=1, replica_groups=mesh['y'=4,'x'=4,'zl'=8,'zh'=2,'core'=2] {'zh','zl'}, dimensions={0} | all-to-all | bytes 393216 | tf_op jit(solution)/shard_map/all_to_all | solution.py:277
  39.5 0.0 collective-permute-done
  39.5 0.0 copy-done
  39.5 2.5 %shard_map.78 = bf16[16,128,768]{2,1,0:T(8,128)(2,1)} custom-call(s32[4]{0:T(128)S(1)} %copy-done, bf16[2,64,768]{2,1,0:T(8,128)(2,1)S(1)} %bitcast.23), custom_call_target="tpu_custom_call" | custom-call | tf_op jit(solution)/shard_map/pallas_call | solution.py:223
  42.0 7.2 %all-to-all-start.1 = ((bf16[16,128,768]{2,1,0:T(8,128)(2,1)}), bf16[16,128,768]{2,1,0:T(8,128)(2,1)S(1)}, u32[]{:S(2)}, u32[]{:S(2)}) async-start(bf16[16,128,768]{2,1,0:T(8,128)(2,1)} %shard_map.78), calls=%async_computation.1 | async-start | bytes 6291456 | tf_op jit(solution)/shard_map/all_to_all | solution.py:282
  49.2 0.0 copy-done.2
  49.3 5.3 %collective-permute-start.1 = (bf16[128,768]{1,0:T(8,128)(2,1)S(1)}, bf16[128,768]{1,0:T(8,128)(2,1)S(1)}, u32[]{:S(2)}, u32[]{:S(2)}) collective-permute-start(bf16[128,768]{1,0:T(8,128)(2,1)S(1)} %slice.8), channel_id=1, source_target_pairs={{0,2},{2,0},{1,3},{3,1},{4,6},{6,4},{5,7},{7,5},{8,10},{10,8},{9,1... | collective-permute-start | bytes 589832 | tf_op jit(solution)/shard_map/ppermute | solution.py:265
  54.5 21.2 %collective-permute-done.1 = bf16[128,768]{1,0:T(8,128)(2,1)S(1)} collective-permute-done((bf16[128,768]{1,0:T(8,128)(2,1)S(1)}, bf16[128,768]{1,0:T(8,128)(2,1)S(1)}, u32[]{:S(2)}, u32[]{:S(2)}) %collective-permute-start.1) | collective-permute-done | bytes 196640 | tf_op jit(solution)/shard_map/ppermute | solution.py:265
  75.8 1.9 %collective-permute-start.2 = (bf16[128,768]{1,0:T(8,128)(2,1)S(1)}, bf16[128,768]{1,0:T(8,128)(2,1)S(1)}, u32[]{:S(2)}, u32[]{:S(2)}) collective-permute-start(bf16[128,768]{1,0:T(8,128)(2,1)S(1)} %collective-permute-done.1), channel_id=1, source_target_pairs={{0,1},{1,0},{2,3},{3,2},{4,5},{5,4},{6,7},{7,6},{8,9},{9,8},{10,11... | collective-permute-start | bytes 589832 | tf_op jit(solution)/shard_map/ppermute | solution.py:265
  77.7 1.9 %collective-permute-start.3 = (bf16[64,1536]{1,0:T(8,128)(2,1)}, bf16[64,1536]{1,0:T(8,128)(2,1)}, u32[]{:S(2)}, u32[]{:S(2)}) collective-permute-start(bf16[64,1536]{1,0:T(8,128)(2,1)} %get-tuple-element.19), channel_id=1, source_target_pairs={{0,4},{4,0},{8,12},{12,8},{16,20},{20,16},{24,28},{28,24},{1,5},{5... | collective-permute-start | bytes 589832 | tf_op jit(solution)/shard_map/ppermute | solution.py:280
  79.6 0.0 collective-permute-done.2
  79.6 0.0 copy-start.4
  79.6 7.6 %collective-permute-done.3.partner = bf16[64,1536]{1,0:T(8,128)(2,1)} collective-permute-done((bf16[64,1536]{1,0:T(8,128)(2,1)}, bf16[64,1536]{1,0:T(8,128)(2,1)}, u32[]{:S(2)}, u32[]{:S(2)}) %collective-permute-start.3) | collective-permute-done | bytes 196640 | tf_op jit(solution)/shard_map/ppermute | solution.py:280
  87.2 8.6 %all-to-all-done.1.got = bf16[16,128,768]{2,1,0:T(8,128)(2,1)S(1)} async-done(((bf16[16,128,768]{2,1,0:T(8,128)(2,1)}), bf16[16,128,768]{2,1,0:T(8,128)(2,1)S(1)}, u32[]{:S(2)}, u32[]{:S(2)}) %all-to-all-start.1) | async-done | bytes 3145760 | tf_op jit(solution)/shard_map/all_to_all | solution.py:282
  95.8 0.1 slice.7
  95.9 1.5 copy-done.1
  97.4 1.9 %collective-permute-start.4 = (bf16[16,64,768]{2,1,0:T(8,128)(2,1)S(1)}, bf16[16,64,768]{2,1,0:T(8,128)(2,1)}, u32[]{:S(2)}, u32[]{:S(2)}) collective-permute-start(bf16[16,64,768]{2,1,0:T(8,128)(2,1)S(1)} %slice.7), channel_id=1, source_target_pairs={{0,1},{1,0},{2,3},{3,2},{4,5},{5,4},{6,7},{7,6},{8,9},{9,8},{10,11... | collective-permute-start | bytes 4718600 | tf_op jit(solution)/shard_map/ppermute | solution.py:265
  99.3 3.5 %collective-permute-done.4.cross = bf16[16,64,768]{2,1,0:T(8,128)(2,1)} collective-permute-done((bf16[16,64,768]{2,1,0:T(8,128)(2,1)S(1)}, bf16[16,64,768]{2,1,0:T(8,128)(2,1)}, u32[]{:S(2)}, u32[]{:S(2)}) %collective-permute-start.4) | collective-permute-done | bytes 1572896 | tf_op jit(solution)/shard_map/ppermute | solution.py:265
  102.9 0.0 copy-done.3
  102.9 16.9 %shard_map.79 = (f32[128,768]{1,0:T(8,128)}, f32[16,2,24,384]{3,2,1,0:T(8,128)}, bf16[16,2,24,384]{3,2,1,0:T(8,128)(2,1)}) custom-call(s32[4]{0:T(128)} %pad_add_fusion.scal, bf16[128,1536]{1,0:T(8,128)(2,1)} %bitcast.28, bf16[64,1536]{1,0:T(8,128)(2,1)} %collective-permute-done.3.partner, bf16[18,64,768]{2,1,0:T(8,128)(2,1)} %bitcast.26, ...), custom_call_target="tpu_custom_call" | custom-call | tf_op jit(solution)/shard_map/pallas_call | solution.py:236
  119.8 2.1 %collective-permute-start.5 = (bf16[16,2,24,384]{3,2,1,0:T(8,128)(2,1)}, bf16[16,2,24,384]{3,2,1,0:T(8,128)(2,1)S(1)}, u32[]{:S(2)}, u32[]{:S(2)}) collective-permute-start(bf16[16,2,24,384]{3,2,1,0:T(8,128)(2,1)} %get-tuple-element.27), channel_id=1, source_target_pairs={{0,1},{1,0},{2,3},{3,2},{4,5},{5,4},{6,7},{7,6},{8,9},{9,8},{10,11... | collective-permute-start | bytes 1769480 | tf_op jit(solution)/shard_map/ppermute | solution.py:265
  121.8 2.0 %collective-permute-done.5 = bf16[16,2,24,384]{3,2,1,0:T(8,128)(2,1)S(1)} collective-permute-done((bf16[16,2,24,384]{3,2,1,0:T(8,128)(2,1)}, bf16[16,2,24,384]{3,2,1,0:T(8,128)(2,1)S(1)}, u32[]{:S(2)}, u32[]{:S(2)}) %collective-permute-start.5) | collective-permute-done | bytes 589856 | tf_op jit(solution)/shard_map/ppermute | solution.py:265
  123.9 1.4 add_convert_fusion
  125.3 16.1 %all_to_all.26 = bf16[16,2,24,384]{3,2,1,0:T(8,128)(2,1)S(1)} all-to-all(bf16[16,2,24,384]{3,2,1,0:T(8,128)(2,1)S(1)} %add_convert_fusion), channel_id=1, replica_groups=mesh['y'=4,'x'=4,'zl'=8,'zh'=2,'core'=2] {'y','x'}, dimensions={0} | all-to-all | bytes 1179648 | tf_op jit(solution)/shard_map/all_to_all | solution.py:301
  141.3 0.1 reduce_sum.21
  141.4 25.8 %all_to_all.27 = bf16[16,24,384]{2,1,0:T(8,128)(2,1)S(1)} all-to-all(bf16[16,24,384]{2,1,0:T(8,128)(2,1)S(1)} %bitcast.29), channel_id=1, replica_groups=mesh['y'=4,'x'=4,'zl'=8,'zh'=2,'core'=2] {'zh','zl'}, dimensions={0} | all-to-all | bytes 589824 | tf_op jit(solution)/shard_map/all_to_all | solution.py:304
  167.4 14.3 %all_to_all.28 = f32[16,24,384]{2,1,0:T(8,128)S(1)} all-to-all(f32[16,24,384]{2,1,0:T(8,128)S(1)} %broadcast_in_dim.8), channel_id=1, replica_groups=mesh['y'=4,'x'=4,'zl'=8,'zh'=2,'core'=2] {'y','x'}, dimensions={0} | all-to-all | bytes 1179648 | tf_op jit(solution)/shard_map/all_to_all | solution.py:259
  181.6 0.3 copy.9
  182.0 0.9 copy.10
  (9 shorter events, 0.1 us)
Async XLA Ops:
  1.9 37.6 %copy-start = (s32[4]{0:T(128)S(1)}, s32[4]{0:T(128)}, u32[]{:S(2)}) copy-start(s32[4]{0:T(128)} %pad_add_fusion.scal) | copy-start | bytes 52
  5.7 33.8 %collective-permute-start = (bf16[1152,768]{1,0:T(8,128)(2,1)}, bf16[1152,768]{1,0:T(8,128)(2,1)}, u32[]{:S(2)}, u32[]{:S(2)}) collective-permute-start(bf16[1152,768]{1,0:T(8,128)(2,1)} %get-tuple-element.16), channel_id=1, source_target_pairs={{0,1},{1,0},{2,3},{3,2},{4,5},{5,4},{6,7},{7,6},{8,9},{9,8},{10,11... | collective-permute-start | bytes 5308424 | tf_op jit(solution)/shard_map/ppermute | solution.py:265
  42.0 7.2 %copy-start.2 = (bf16[768,192]{0,1:T(8,128)(2,1)S(1)}, bf16[768,192]{0,1:T(8,128)(2,1)}, u32[]{:S(2)}) copy-start(bf16[768,192]{0,1:T(8,128)(2,1)} %param.10) | copy-start | bytes 884740
  42.0 53.7 %all-to-all-start.1 = ((bf16[16,128,768]{2,1,0:T(8,128)(2,1)}), bf16[16,128,768]{2,1,0:T(8,128)(2,1)S(1)}, u32[]{:S(2)}, u32[]{:S(2)}) async-start(bf16[16,128,768]{2,1,0:T(8,128)(2,1)} %shard_map.78), calls=%async_computation.1 | async-start | bytes 6291456 | tf_op jit(solution)/shard_map/all_to_all | solution.py:282
  49.3 26.5 %collective-permute-start.1 = (bf16[128,768]{1,0:T(8,128)(2,1)S(1)}, bf16[128,768]{1,0:T(8,128)(2,1)S(1)}, u32[]{:S(2)}, u32[]{:S(2)}) collective-permute-start(bf16[128,768]{1,0:T(8,128)(2,1)S(1)} %slice.8), channel_id=1, source_target_pairs={{0,2},{2,0},{1,3},{3,1},{4,6},{6,4},{5,7},{7,5},{8,10},{10,8},{9,1... | collective-permute-start | bytes 589832 | tf_op jit(solution)/shard_map/ppermute | solution.py:265
  75.8 27.1 %copy-start.3 = (bf16[128,768]{1,0:T(8,128)(2,1)}, bf16[128,768]{1,0:T(8,128)(2,1)S(1)}, u32[]{:S(2)}) copy-start(bf16[128,768]{1,0:T(8,128)(2,1)S(1)} %collective-permute-done.1) | copy-start | bytes 589828
  75.8 3.8 %collective-permute-start.2 = (bf16[128,768]{1,0:T(8,128)(2,1)S(1)}, bf16[128,768]{1,0:T(8,128)(2,1)S(1)}, u32[]{:S(2)}, u32[]{:S(2)}) collective-permute-start(bf16[128,768]{1,0:T(8,128)(2,1)S(1)} %collective-permute-done.1), channel_id=1, source_target_pairs={{0,1},{1,0},{2,3},{3,2},{4,5},{5,4},{6,7},{7,6},{8,9},{9,8},{10,11... | collective-permute-start | bytes 589832 | tf_op jit(solution)/shard_map/ppermute | solution.py:265
  77.7 9.5 %collective-permute-start.3 = (bf16[64,1536]{1,0:T(8,128)(2,1)}, bf16[64,1536]{1,0:T(8,128)(2,1)}, u32[]{:S(2)}, u32[]{:S(2)}) collective-permute-start(bf16[64,1536]{1,0:T(8,128)(2,1)} %get-tuple-element.19), channel_id=1, source_target_pairs={{0,4},{4,0},{8,12},{12,8},{16,20},{20,16},{24,28},{28,24},{1,5},{5... | collective-permute-start | bytes 589832 | tf_op jit(solution)/shard_map/ppermute | solution.py:280
  79.6 23.2 %copy-start.4 = (bf16[128,768]{1,0:T(8,128)(2,1)}, bf16[128,768]{1,0:T(8,128)(2,1)S(1)}, u32[]{:S(2)}) copy-start(bf16[128,768]{1,0:T(8,128)(2,1)S(1)} %collective-permute-done.2) | copy-start | bytes 589828
  95.8 1.6 copy-start.1
  97.4 5.4 %collective-permute-start.4 = (bf16[16,64,768]{2,1,0:T(8,128)(2,1)S(1)}, bf16[16,64,768]{2,1,0:T(8,128)(2,1)}, u32[]{:S(2)}, u32[]{:S(2)}) collective-permute-start(bf16[16,64,768]{2,1,0:T(8,128)(2,1)S(1)} %slice.7), channel_id=1, source_target_pairs={{0,1},{1,0},{2,3},{3,2},{4,5},{5,4},{6,7},{7,6},{8,9},{9,8},{10,11... | collective-permute-start | bytes 4718600 | tf_op jit(solution)/shard_map/ppermute | solution.py:265
  119.8 4.1 %collective-permute-start.5 = (bf16[16,2,24,384]{3,2,1,0:T(8,128)(2,1)}, bf16[16,2,24,384]{3,2,1,0:T(8,128)(2,1)S(1)}, u32[]{:S(2)}, u32[]{:S(2)}) collective-permute-start(bf16[16,2,24,384]{3,2,1,0:T(8,128)(2,1)} %get-tuple-element.27), channel_id=1, source_target_pairs={{0,1},{1,0},{2,3},{3,2},{4,5},{5,4},{6,7},{7,6},{8,9},{9,8},{10,11... | collective-permute-start | bytes 1769480 | tf_op jit(solution)/shard_map/ppermute | solution.py:265

commit v5 on v4

--- a/solution.py
+++ b/solution.py
@@ -22,7 +22,7 @@
 F32 = jnp.float32
 MARK = 64.0
 LOW = -1e30
-LOG2 = 0.6931471805599453
+SCALE = HEAD**-0.5 / 0.6931471805599453
 
 
 def dot(a, b, dims):
@@ -49,14 +49,12 @@
     out,
     keep,
     send,
-    near,
-    far,
+    given,
     win,
     wqkv,
     wout,
     hid,
     kv,
-    mixed,
     attn,
     sems,
 ):
@@ -69,9 +67,10 @@
         (mate.at[pl.ds(0, 6)], win.at[other]),
         (arrived.at[pl.ds(0, 6)], win.at[over]),
         (cross.at[pl.ds(0, 6)], win.at[over_other]),
-        (rows, near.at[pl.ds(0, TOK)]),
-        (partner, near.at[pl.ds(TOK, TOK // 2)]),
-        (got.at[:, pl.ds(64, 64)], far),
+        (rows, given.at[pl.ds(0, 4)]),
+        (partner, given.at[pl.ds(4, 2)]),
+        (got.at[:, pl.ds(64, 32)], given.at[pl.ds(8, 16), :, pl.ds(0, WIDTH)]),
+        (got.at[:, pl.ds(96, 32)], given.at[pl.ds(8, 16), :, pl.ds(WIDTH, WIDTH)]),
         (own.at[pl.ds(6, 9)], wqkv.at[mine]),
         (mate.at[pl.ds(6, 9)], wqkv.at[other]),
         (arrived.at[pl.ds(6, 9)], wqkv.at[over]),
@@ -86,46 +85,34 @@
     copies = [pltpu.make_async_copy(s, d, sems.at[i]) for i, (s, d) in enumerate(moves)]
     for c in copies:
         c.start()
-    near[pl.ds(192, 64), :] = jnp.zeros((64, TILE), BF)
+    given[pl.ds(6, 2)] = jnp.zeros((2, 32, TILE), BF)
     lane = lax.broadcasted_iota(jnp.int32, (1, TOK), 1)
-    twice = jnp.where(lane & 1 == 0, F32(LOG2), F32(0))
-    for c in copies[:7]:
+    twice = jnp.where(lane & 1 == 0, F32(1), F32(0))
+    for c in copies[:8]:
         c.wait()
-    left = far[:, pl.ds(0, 32), :].reshape(FAR, WIDTH)
-    right = far[:, pl.ds(32, 32), :].reshape(FAR, WIDTH)
-    weight = win[...].reshape(TILE, WIDTH)
-    hid[pl.ds(0, 256), :] = dot(near[...], weight, NN).astype(BF)
-    hid[pl.ds(256, FAR), :] = (
-        dot(left, weight[:WIDTH], NN) + dot(right, weight[WIDTH:], NN)
-    ).astype(BF)
+    keys = given[...].reshape(WIDTH, TILE)
+    hid[...] = dot(keys, win[...].reshape(TILE, WIDTH), NN).astype(BF)
     bias = jnp.concatenate(
         [
             jnp.where(lane < count, twice, F32(LOW)),
-            key_bias(near[pl.ds(TOK, 64), :]),
+            key_bias(keys[TOK : TOK + 64]),
             jnp.full((1, 64), LOW, F32),
-            key_bias(left),
+            key_bias(keys[256:]),
         ],
         axis=1,
     )
-    for c in copies[7:11]:
+    for c in copies[8:12]:
         c.wait()
     flat = wqkv[...].reshape(3 * WIDTH, WIDTH)
     kv[...] = dot(flat[WIDTH:], hid[...], NT).astype(BF)
     own_hid = hid[pl.ds(0, TOK), :]
-    column = lax.broadcasted_iota(jnp.int32, (TOK, TOK), 1)
-    totals = jnp.ones((TOK, TOK), F32)
     for h in range(HEADS):
         q = dot(own_hid, flat[h * HEAD : (h + 1) * HEAD], NT).astype(BF)
-        s = dot(q, kv[pl.ds(h * HEAD, HEAD), :], NN) * F32(HEAD**-0.5) + bias
-        p = jnp.exp(s - jnp.max(s, axis=1, keepdims=True))
-        totals = jnp.where(column == h, jnp.sum(p, axis=1, keepdims=True), totals)
-        mixed[pl.ds(h * HEAD, HEAD), :] = dot(
-            kv[pl.ds(WIDTH + h * HEAD, HEAD), :], p.astype(BF), NT
-        )
-    inverse = 1.0 / totals.T
-    for h in range(HEADS):
-        at = pl.ds(h * HEAD, HEAD)
-        attn[at, :] = (mixed[at, :] * inverse[h : h + 1, :]).astype(BF)
+        s = dot(q, kv[pl.ds(h * HEAD, HEAD), :], NN) * F32(SCALE) + bias
+        p = jnp.exp2(s - jnp.max(s, axis=1, keepdims=True))
+        o = dot(p.astype(BF), kv[pl.ds(WIDTH + h * HEAD, HEAD), :], NT)
+        o = o / jnp.sum(p, axis=1, keepdims=True)
+        attn[pl.ds(h * HEAD, HEAD), :] = o.T.astype(BF)
     cotangent = cot[...]
     token = lax.broadcasted_iota(jnp.int32, (192, TOK), 1)
     for which, target in ((core, keep), (1 - core, send)):
@@ -139,7 +126,7 @@
                     target[r * 2 + c, half] = part[r * 24 : r * 24 + 24, c * 384 : c * 384 + 384].astype(
                         target.dtype
                     )
-    for c in copies[11:]:
+    for c in copies[12:]:
         c.wait()
     out[...] = dot(wout[...].reshape(WIDTH, WIDTH), attn[...], NN).T
 
@@ -153,7 +140,7 @@
     return pltpu.CompilerParams(vmem_limit_bytes=mebibytes * 1024 * 1024)
 
 
-def prepare_kernel(scal, rows, w_in, w_qkv, w_out, own, ahead, even, sems):
+def prepare_kernel(scal, rows, w_in, w_qkv, w_out, own, ahead, even, tail, sems):
     count, zh, at = scal[0], scal[1], scal[3]
     moves = [
         (w_in, own.at[pl.ds(0, 384)]),
@@ -184,6 +171,11 @@
     start = pl.multiple_of(at // 16 * 16, 16)
     wide = own[pl.ds(start, 16), :].astype(F32)
     eight = jnp.where(at > start, wide[8:16], wide[0:8])
+    first = 8 * (at // 64)
+    start = pl.multiple_of(1024 + first // 16 * 16, 16)
+    wide = own[pl.ds(start, 16), :].astype(F32)
+    last = jnp.where(first % 16 > 0, wide[8:16], wide[0:8])
+    tail[...] = jnp.concatenate([last, last], axis=0).astype(BF)
     far = jnp.concatenate([distant[:, :WIDTH], distant[:, WIDTH:]], axis=0)
     for half in range(2):
         value = jnp.where(zh == half, far, eight)
@@ -197,16 +189,17 @@
             jax.ShapeDtypeStruct((PACK, WIDTH), BF),
             jax.ShapeDtypeStruct((2, 64, WIDTH), BF),
             jax.ShapeDtypeStruct((TOK // 2, TILE), BF),
+            jax.ShapeDtypeStruct((16, WIDTH), BF),
         ),
         in_specs=[SMEM, VMEM] + [ANY] * 3,
-        out_specs=(VMEM, VMEM, VMEM),
+        out_specs=(VMEM,) * 4,
         scratch_shapes=[pltpu.SemaphoreType.DMA((3,))],
         compiler_params=room(62),
         interpret=interpret,
     )(*operands)
 
 
-def split_kernel(scal, line, payload):
+def split_kernel(scal, line, tail, payload):
     zh = scal[1]
     piece = line[1 - zh]
     target = lax.broadcasted_iota(jnp.int32, (64, 64), 0)
@@ -214,7 +207,9 @@
     origin = (target & 31) // 4 * 8 + target // 32 * 4 + (target & 3)
     pick = jnp.where(source == origin, F32(1), F32(0)).astype(BF)
     ordered = dot(pick, line[zh], NN).astype(BF)
-    both = jnp.concatenate([piece, ordered], axis=0)
+    both = jnp.concatenate(
+        [piece.astype(F32), ordered.astype(F32), tail[...].astype(F32)[0:8]], axis=0
+    ).astype(BF)
     for i in range(16):
         payload[i] = both
 
@@ -222,8 +217,8 @@
 def split_call(*operands, interpret=False):
     return pl.pallas_call(
         split_kernel,
-        out_shape=jax.ShapeDtypeStruct((16, 128, WIDTH), BF),
-        in_specs=[SMEM, VMEM],
+        out_shape=jax.ShapeDtypeStruct((16, 136, WIDTH), BF),
+        in_specs=[SMEM, VMEM, VMEM],
         out_specs=VMEM,
         compiler_params=room(16),
         interpret=interpret,
@@ -239,16 +234,14 @@
         in_specs=[SMEM] + [ANY] * 8 + [VMEM],
         out_specs=(VMEM,) * 3,
         scratch_shapes=[
-            pltpu.VMEM((256, TILE), BF),
-            pltpu.VMEM((16, 64, WIDTH), BF),
+            pltpu.VMEM((24, 32, TILE), BF),
             pltpu.VMEM((4, 6, 64, WIDTH), BF),
             pltpu.VMEM((4, 9, 64, WIDTH), BF),
             pltpu.VMEM((4, 3, 64, WIDTH), BF),
             pltpu.VMEM((WIDTH, WIDTH), BF),
             pltpu.VMEM((2 * WIDTH, WIDTH), BF),
-            pltpu.VMEM((WIDTH, TOK), F32),
             pltpu.VMEM((WIDTH, TOK), BF),
-            pltpu.SemaphoreType.DMA((17,)),
+            pltpu.SemaphoreType.DMA((18,)),
         ],
         compiler_params=room(62),
         interpret=interpret,
@@ -273,22 +266,21 @@
     zh, core = lax.axis_index("zh"), lax.axis_index("core")
     w_out = w_out.T
     scal = jnp.stack([count, zh, core, yx * 64 + zl * 8]).astype(jnp.int32)
-    own, ahead, even = prepare_call(scal, rows, w_in, w_qkv.T, w_out)
+    own, ahead, even, tail = prepare_call(scal, rows, w_in, w_qkv.T, w_out)
     line = lax.all_to_all(ahead.reshape(16, 8, WIDTH), Z, 0, 0, tiled=True)
     mate = swap(own, "core")
-    line, mate, even = lax.optimization_barrier((line.reshape(2, 64, WIDTH), mate, even))
+    tail = swap(tail, "zh")
     partner = lax.ppermute(even, "zl", [(i, i ^ 1) for i in range(8)])
-    over_rest = swap(w_out[64:], "zh")
-    got = lax.all_to_all(split_call(scal, line), YX, 0, 0, tiled=True)
-    cross_rest = swap(over_rest, "core")
-    got, over_rest, cross_rest, partner = lax.optimization_barrier(
-        (got, over_rest, cross_rest, partner)
-    )
-    cross = swap(got[:, :64], "core")
+    line, mate, tail, partner = lax.optimization_barrier(
+        (line.reshape(2, 64, WIDTH), mate, tail, partner)
+    )
+    got = lax.all_to_all(split_call(scal, line, tail), YX, 0, 0, tiled=True)
+    over_rest = got[:, 128:].reshape(128, WIDTH)
+    cross, cross_rest = swap(got[:, :64], "core"), swap(over_rest, "core")
     out, keep, send = layer_call(
         scal,
-        rows,
-        partner,
+        rows.reshape(4, 32, TILE),
+        partner.reshape(2, 32, TILE),
         own.reshape(18, 64, WIDTH),
         mate.reshape(18, 64, WIDTH),
         got,
@@ -303,7 +295,7 @@
     column = jnp.broadcast_to(plane[:, None], (2, 8, 24, 384)).reshape(16, 24, 384)
     column = lax.all_to_all(column, Z, 0, 0, tiled=True)
     total = jnp.sum(column.astype(F32), axis=0)
-    whole = spread(total, YX, 16)
+    whole = spread(total.astype(BF), YX, 16).astype(F32)
     grad = whole.reshape(8, 2, 24, 384).transpose(0, 2, 1, 3).reshape(192, WIDTH)
     return (out[None], grad)
 

time: 183 us -> 180 us (0.984)
  the two profiles are of different devices: /device:TPU:32 before, /device:TPU:64 now
where the time goes in v5:
time: 180 us; the launch traced here: 179 us
  blocking collectives  102 us (57%)
  starting transfers between devices  36 us (20%)
  Pallas kernels  20.9 us (12%)
  waiting for transfers between devices  12.6 us (7%)
  local copies, waits for them, and re-layouts  3.74 us (2%)
  other arithmetic  2.15 us (1%)
    all_to_all x1, blocking collectives, shards(): got = lax.all_to_all(split_call(scal, line, tail), YX, 0, 0, tiled=True)  48.1 us
    all_to_all x1, blocking collectives, shards(): column = lax.all_to_all(column, Z, 0, 0, tiled=True)  26.4 us
    ppermute x5, starting transfers between devices, swap(): return lax.ppermute(value, axis, [(0, 1), (1, 0)])  17.9 us
    pallas_call x1, Pallas kernels, layer_call(): pl.pallas_call(layer_kernel, out_shape=(jax.ShapeDtypeStruct((TOK, WIDTH)...  16.3 us
    all_to_all x1, blocking collectives, shards(): plane = lax.all_to_all(pair, YX, 0, 0, tiled=True)  15.8 us
    all_to_all x1, starting transfers between devices, shards(): line = lax.all_to_all(ahead.reshape(16, 8, WIDTH), Z, 0, 0, tiled=True)  14.8 us
    ppermute x5, waiting for transfers between devices, swap(): return lax.ppermute(value, axis, [(0, 1), (1, 0)])  12.6 us
    all_to_all x1, blocking collectives, spread(): lax.all_to_all(jnp.broadcast_to(block[None], (size,) + block.shape), axes...  12.1 us
  transfers between devices with their start and end apart: 7, of which 3 were waited for; matrix products, arithmetic and copies ran while one was open for 0% of the time, Pallas kernels for 0%

profile of v5, /device:TPU:64, one launch (start us, length us, event | category | flops | bytes accessed | tf_op | source)
XLA Modules:
  0.0 179.4 jit_solution(6016705684863921923)
XLA Ops:
  1.3 0.6 pad_add_fusion.scal
  1.9 3.8 %shard_map.77 = (bf16[1152,768]{1,0:T(8,128)(2,1)}, bf16[2,64,768]{2,1,0:T(8,128)(2,1)}, bf16[64,1536]{1,0:T(8,128)(2,1)}, bf16[16,768]{1,0:T(8,128)(2,1)}) custom-call(s32[4]{0:T(128)} %pad_add_fusion.scal, bf16[128,1536]{1,0:T(8,128)(2,1)} %bitcast.32, bf16[384,768]{1,0:T(8,128)(2,1)} %w_in.1, bf16[576,768]{1,0:T(8,128)(2,1)} %bitcast.36, ...), custom_call_target="tpu_custom_call" | custom-call | tf_op jit(solution)/shard_map/pallas_call | solution.py:186
  5.7 1.9 %collective-permute-start = (bf16[1152,768]{1,0:T(8,128)(2,1)}, bf16[1152,768]{1,0:T(8,128)(2,1)S(1)}, u32[]{:S(2)}, u32[]{:S(2)}) collective-permute-start(bf16[1152,768]{1,0:T(8,128)(2,1)} %get-tuple-element.14), channel_id=1, source_target_pairs={{0,1},{1,0},{2,3},{3,2},{4,5},{5,4},{6,7},{7,6},{8,9},{9,8},{10,11... | collective-permute-start | bytes 5308424 | tf_op jit(solution)/shard_map/ppermute | solution.py:258
  7.6 14.8 %all-to-all-start = ((bf16[16,8,768]{2,1,0:T(8,128)(2,1)}), bf16[16,8,768]{2,1,0:T(8,128)(2,1)S(1)}, u32[]{:S(2)}, u32[]{:S(2)}) async-start(bf16[16,8,768]{2,1,0:T(8,128)(2,1)} %bitcast.40), calls=%async_computation | async-start | bytes 393216 | tf_op jit(solution)/shard_map/all_to_all | solution.py:270
  22.4 3.4 %collective-permute-start.2 = (bf16[64,1536]{1,0:T(8,128)(2,1)}, bf16[64,1536]{1,0:T(8,128)(2,1)S(1)}, u32[]{:S(2)}, u32[]{:S(2)}) collective-permute-start(bf16[64,1536]{1,0:T(8,128)(2,1)} %get-tuple-element.16), channel_id=1, source_target_pairs={{0,4},{4,0},{8,12},{12,8},{16,20},{20,16},{24,28},{28,24},{1,5},{5... | collective-permute-start | bytes 589832 | tf_op jit(solution)/shard_map/ppermute | solution.py:273
  25.7 9.4 %collective-permute-start.1 = (bf16[16,768]{1,0:T(8,128)(2,1)}, bf16[16,768]{1,0:T(8,128)(2,1)S(1)}, u32[]{:S(2)}, u32[]{:S(2)}) collective-permute-start(bf16[16,768]{1,0:T(8,128)(2,1)} %get-tuple-element.15), channel_id=1, source_target_pairs={{0,2},{2,0},{1,3},{3,1},{4,6},{6,4},{5,7},{7,5},{8,10},{10,8},{9,1... | collective-permute-start | bytes 73736 | tf_op jit(solution)/shard_map/ppermute | solution.py:258
  35.1 9.8 %collective-permute-done.1.tail = bf16[16,768]{1,0:T(8,128)(2,1)S(1)} collective-permute-done((bf16[16,768]{1,0:T(8,128)(2,1)}, bf16[16,768]{1,0:T(8,128)(2,1)S(1)}, u32[]{:S(2)}, u32[]{:S(2)}) %collective-permute-start.1) | collective-permute-done | bytes 24608 | tf_op jit(solution)/shard_map/ppermute | solution.py:258
  44.9 0.0 collective-permute-done.2
  44.9 0.0 all-to-all-done
  44.9 0.0 collective-permute-done
  44.9 0.8 shard_map.78
  45.8 0.4 copy-done.2
  46.2 48.1 %all_to_all.25.got = bf16[16,136,768]{2,1,0:T(8,128)(2,1)S(1)} all-to-all(bf16[16,136,768]{2,1,0:T(8,128)(2,1)S(1)} %shard_map.78), channel_id=1, replica_groups=mesh['y'=4,'x'=4,'zl'=8,'zh'=2,'core'=2] {'y','x'}, dimensions={0} | all-to-all | bytes 6684672 | tf_op jit(solution)/shard_map/all_to_all | solution.py:277
  94.3 0.1 slice.8
  94.5 1.9 %collective-permute-start.3 = (bf16[16,64,768]{2,1,0:T(8,128)(2,1)S(1)}, bf16[16,64,768]{2,1,0:T(8,128)(2,1)S(1)}, u32[]{:S(2)}, u32[]{:S(2)}) collective-permute-start(bf16[16,64,768]{2,1,0:T(8,128)(2,1)S(1)} %slice.8), channel_id=1, source_target_pairs={{0,1},{1,0},{2,3},{3,2},{4,5},{5,4},{6,7},{7,6},{8,9},{9,8},{10,11... | collective-permute-start | bytes 4718600 | tf_op jit(solution)/shard_map/ppermute | solution.py:258
  96.4 0.7 slice_bitcast_fusion
  97.1 0.0 copy-done.1
  97.1 2.4 %collective-permute-start.4 = (bf16[128,768]{1,0:T(8,128)(2,1)S(1)}, bf16[128,768]{1,0:T(8,128)(2,1)S(1)}, u32[]{:S(2)}, u32[]{:S(2)}) collective-permute-start(bf16[128,768]{1,0:T(8,128)(2,1)S(1)} %get-tuple-element.24), channel_id=1, source_target_pairs={{0,1},{1,0},{2,3},{3,2},{4,5},{5,4},{6,7},{7,6},{8,9},{9,8},{10,11... | collective-permute-start | bytes 589832 | tf_op jit(solution)/shard_map/ppermute | solution.py:258
  99.5 1.0 collective-permute-done.4
  100.6 0.0 collective-permute-done.3.cross
  100.6 0.7 copy-done.5
  101.2 0.6 copy-done.3
  101.8 16.3 %shard_map.79 = (f32[128,768]{1,0:T(8,128)}, f32[16,2,24,384]{3,2,1,0:T(8,128)}, bf16[16,2,24,384]{3,2,1,0:T(8,128)(2,1)}) custom-call(s32[4]{0:T(128)} %pad_add_fusion.scal, bf16[4,32,1536]{2,1,0:T(8,128)(2,1)} %bitcast.33, bf16[2,32,1536]{2,1,0:T(8,128)(2,1)} %bitcast.42, bf16[18,64,768]{2,1,0:T(8,128)(2,1)} %bitcast.30, bf16[18,64,768]{2,1,0:T(8,128)(2,1)} %bitcast.31, ...), custom_call_target="tpu_custom_call" | custom-call | tf_op jit(solution)/shard_map/pallas_call | solution.py:231
  118.1 2.3 %collective-permute-start.5 = (bf16[16,2,24,384]{3,2,1,0:T(8,128)(2,1)}, bf16[16,2,24,384]{3,2,1,0:T(8,128)(2,1)S(1)}, u32[]{:S(2)}, u32[]{:S(2)}) collective-permute-start(bf16[16,2,24,384]{3,2,1,0:T(8,128)(2,1)} %get-tuple-element.23), channel_id=1, source_target_pairs={{0,1},{1,0},{2,3},{3,2},{4,5},{5,4},{6,7},{7,6},{8,9},{9,8},{10,11... | collective-permute-start | bytes 1769480 | tf_op jit(solution)/shard_map/ppermute | solution.py:258
  120.4 1.8 %collective-permute-done.5 = bf16[16,2,24,384]{3,2,1,0:T(8,128)(2,1)S(1)} collective-permute-done((bf16[16,2,24,384]{3,2,1,0:T(8,128)(2,1)}, bf16[16,2,24,384]{3,2,1,0:T(8,128)(2,1)S(1)}, u32[]{:S(2)}, u32[]{:S(2)}) %collective-permute-start.5) | collective-permute-done | bytes 589856 | tf_op jit(solution)/shard_map/ppermute | solution.py:258
  122.2 1.4 add_convert_fusion
  123.6 15.8 %all_to_all.26 = bf16[16,2,24,384]{3,2,1,0:T(8,128)(2,1)S(1)} all-to-all(bf16[16,2,24,384]{3,2,1,0:T(8,128)(2,1)S(1)} %add_convert_fusion), channel_id=1, replica_groups=mesh['y'=4,'x'=4,'zl'=8,'zh'=2,'core'=2] {'y','x'}, dimensions={0} | all-to-all | bytes 1179648 | tf_op jit(solution)/shard_map/all_to_all | solution.py:293
  139.4 0.1 reduce_sum.24
  139.5 26.4 %all_to_all.27 = bf16[16,24,384]{2,1,0:T(8,128)(2,1)S(1)} all-to-all(bf16[16,24,384]{2,1,0:T(8,128)(2,1)S(1)} %bitcast.35), channel_id=1, replica_groups=mesh['y'=4,'x'=4,'zl'=8,'zh'=2,'core'=2] {'zh','zl'}, dimensions={0} | all-to-all | bytes 589824 | tf_op jit(solution)/shard_map/all_to_all | solution.py:296
  166.0 12.1 %all_to_all.28 = bf16[16,24,384]{2,1,0:T(8,128)(2,1)S(1)} all-to-all(bf16[16,24,384]{2,1,0:T(8,128)(2,1)S(1)} %broadcast_in_dim.8), channel_id=1, replica_groups=mesh['y'=4,'x'=4,'zl'=8,'zh'=2,'core'=2] {'y','x'}, dimensions={0} | all-to-all | bytes 589824 | tf_op jit(solution)/shard_map/all_to_all | solution.py:252
  178.2 0.3 copy.9
  178.5 0.9 copy.10
  (12 shorter events, 0.2 us)
Async XLA Ops:
  1.9 43.1 %copy-start = (s32[4]{0:T(128)S(1)}, s32[4]{0:T(128)}, u32[]{:S(2)}) copy-start(s32[4]{0:T(128)} %pad_add_fusion.scal) | copy-start | bytes 52
  5.7 39.2 %collective-permute-start = (bf16[1152,768]{1,0:T(8,128)(2,1)}, bf16[1152,768]{1,0:T(8,128)(2,1)S(1)}, u32[]{:S(2)}, u32[]{:S(2)}) collective-permute-start(bf16[1152,768]{1,0:T(8,128)(2,1)} %get-tuple-element.14), channel_id=1, source_target_pairs={{0,1},{1,0},{2,3},{3,2},{4,5},{5,4},{6,7},{7,6},{8,9},{9,8},{10,11... | collective-permute-start | bytes 5308424 | tf_op jit(solution)/shard_map/ppermute | solution.py:258
  7.6 37.3 %all-to-all-start = ((bf16[16,8,768]{2,1,0:T(8,128)(2,1)}), bf16[16,8,768]{2,1,0:T(8,128)(2,1)S(1)}, u32[]{:S(2)}, u32[]{:S(2)}) async-start(bf16[16,8,768]{2,1,0:T(8,128)(2,1)} %bitcast.40), calls=%async_computation | async-start | bytes 393216 | tf_op jit(solution)/shard_map/all_to_all | solution.py:270
  22.4 22.5 %collective-permute-start.2 = (bf16[64,1536]{1,0:T(8,128)(2,1)}, bf16[64,1536]{1,0:T(8,128)(2,1)S(1)}, u32[]{:S(2)}, u32[]{:S(2)}) collective-permute-start(bf16[64,1536]{1,0:T(8,128)(2,1)} %get-tuple-element.16), channel_id=1, source_target_pairs={{0,4},{4,0},{8,12},{12,8},{16,20},{20,16},{24,28},{28,24},{1,5},{5... | collective-permute-start | bytes 589832 | tf_op jit(solution)/shard_map/ppermute | solution.py:273
  25.7 19.2 %collective-permute-start.1 = (bf16[16,768]{1,0:T(8,128)(2,1)}, bf16[16,768]{1,0:T(8,128)(2,1)S(1)}, u32[]{:S(2)}, u32[]{:S(2)}) collective-permute-start(bf16[16,768]{1,0:T(8,128)(2,1)} %get-tuple-element.15), channel_id=1, source_target_pairs={{0,2},{2,0},{1,3},{3,1},{4,6},{6,4},{5,7},{7,5},{8,10},{10,8},{9,1... | collective-permute-start | bytes 73736 | tf_op jit(solution)/shard_map/ppermute | solution.py:258
  44.9 0.9 copy-start.4
  44.9 1.3 copy-start.2
  94.3 2.8 %copy-start.1 = (bf16[16,136,768]{2,1,0:T(8,128)(2,1)}, bf16[16,136,768]{2,1,0:T(8,128)(2,1)S(1)}, u32[]{:S(2)}) copy-start(bf16[16,136,768]{2,1,0:T(8,128)(2,1)S(1)} %all_to_all.25.got) | copy-start | bytes 10027012
  94.5 6.1 %collective-permute-start.3 = (bf16[16,64,768]{2,1,0:T(8,128)(2,1)S(1)}, bf16[16,64,768]{2,1,0:T(8,128)(2,1)S(1)}, u32[]{:S(2)}, u32[]{:S(2)}) collective-permute-start(bf16[16,64,768]{2,1,0:T(8,128)(2,1)S(1)} %slice.8), channel_id=1, source_target_pairs={{0,1},{1,0},{2,3},{3,2},{4,5},{5,4},{6,7},{7,6},{8,9},{9,8},{10,11... | collective-permute-start | bytes 4718600 | tf_op jit(solution)/shard_map/ppermute | solution.py:258
  97.1 3.5 %collective-permute-start.4 = (bf16[128,768]{1,0:T(8,128)(2,1)S(1)}, bf16[128,768]{1,0:T(8,128)(2,1)S(1)}, u32[]{:S(2)}, u32[]{:S(2)}) collective-permute-start(bf16[128,768]{1,0:T(8,128)(2,1)S(1)} %get-tuple-element.24), channel_id=1, source_target_pairs={{0,1},{1,0},{2,3},{3,2},{4,5},{5,4},{6,7},{7,6},{8,9},{9,8},{10,11... | collective-permute-start | bytes 589832 | tf_op jit(solution)/shard_map/ppermute | solution.py:258
  100.6 0.7 copy-start.5
  100.6 1.2 copy-start.3
  118.1 4.1 %collective-permute-start.5 = (bf16[16,2,24,384]{3,2,1,0:T(8,128)(2,1)}, bf16[16,2,24,384]{3,2,1,0:T(8,128)(2,1)S(1)}, u32[]{:S(2)}, u32[]{:S(2)}) collective-permute-start(bf16[16,2,24,384]{3,2,1,0:T(8,128)(2,1)} %get-tuple-element.23), channel_id=1, source_target_pairs={{0,1},{1,0},{2,3},{3,2},{4,5},{5,4},{6,7},{7,6},{8,9},{9,8},{10,11... | collective-permute-start | bytes 1769480 | tf_op jit(solution)/shard_map/ppermute | solution.py:258

commit v6 on v5

--- a/solution.py
+++ b/solution.py
@@ -140,7 +140,7 @@
     return pltpu.CompilerParams(vmem_limit_bytes=mebibytes * 1024 * 1024)
 
 
-def prepare_kernel(scal, rows, w_in, w_qkv, w_out, own, ahead, even, tail, sems):
+def prepare_kernel(scal, rows, w_in, w_qkv, w_out, own, ahead, even, sems):
     count, zh, at = scal[0], scal[1], scal[3]
     moves = [
         (w_in, own.at[pl.ds(0, 384)]),
@@ -175,10 +175,10 @@
     start = pl.multiple_of(1024 + first // 16 * 16, 16)
     wide = own[pl.ds(start, 16), :].astype(F32)
     last = jnp.where(first % 16 > 0, wide[8:16], wide[0:8])
-    tail[...] = jnp.concatenate([last, last], axis=0).astype(BF)
-    far = jnp.concatenate([distant[:, :WIDTH], distant[:, WIDTH:]], axis=0)
+    sent = jnp.concatenate([eight, last], axis=0)
+    far = jnp.concatenate([distant[:, :WIDTH], distant[:, WIDTH:], jnp.zeros((8, WIDTH), F32)], axis=0)
     for half in range(2):
-        value = jnp.where(zh == half, far, eight)
+        value = jnp.where(zh == half, far, sent)
         ahead[half] = jnp.concatenate([value] * 8, axis=0).astype(BF)
 
 
@@ -187,28 +187,34 @@
         prepare_kernel,
         out_shape=(
             jax.ShapeDtypeStruct((PACK, WIDTH), BF),
-            jax.ShapeDtypeStruct((2, 64, WIDTH), BF),
+            jax.ShapeDtypeStruct((2, 128, WIDTH), BF),
             jax.ShapeDtypeStruct((TOK // 2, TILE), BF),
-            jax.ShapeDtypeStruct((16, WIDTH), BF),
         ),
         in_specs=[SMEM, VMEM] + [ANY] * 3,
-        out_specs=(VMEM,) * 4,
+        out_specs=(VMEM,) * 3,
         scratch_shapes=[pltpu.SemaphoreType.DMA((3,))],
         compiler_params=room(62),
         interpret=interpret,
     )(*operands)
 
 
-def split_kernel(scal, line, tail, payload):
+def split_kernel(scal, line, payload):
     zh = scal[1]
-    piece = line[1 - zh]
-    target = lax.broadcasted_iota(jnp.int32, (64, 64), 0)
-    source = lax.broadcasted_iota(jnp.int32, (64, 64), 1)
-    origin = (target & 31) // 4 * 8 + target // 32 * 4 + (target & 3)
-    pick = jnp.where(source == origin, F32(1), F32(0)).astype(BF)
-    ordered = dot(pick, line[zh], NN).astype(BF)
+    target = lax.broadcasted_iota(jnp.int32, (64, 128), 0)
+    source = lax.broadcasted_iota(jnp.int32, (64, 128), 1)
+    piece = target // 8 * 16 + (target & 7)
+    ordered = (target & 31) // 4 * 16 + target // 32 * 4 + (target & 3)
+    pick = [
+        jnp.where(source == origin, F32(1), F32(0)).astype(BF)
+        for origin in (piece, ordered, target + 8)
+    ]
     both = jnp.concatenate(
-        [piece.astype(F32), ordered.astype(F32), tail[...].astype(F32)[0:8]], axis=0
+        [
+            dot(pick[0], line[1 - zh], NN),
+            dot(pick[1], line[zh], NN),
+            dot(pick[2], line[1 - zh], NN)[0:8],
+        ],
+        axis=0,
     ).astype(BF)
     for i in range(16):
         payload[i] = both
@@ -218,7 +224,7 @@
     return pl.pallas_call(
         split_kernel,
         out_shape=jax.ShapeDtypeStruct((16, 136, WIDTH), BF),
-        in_specs=[SMEM, VMEM, VMEM],
+        in_specs=[SMEM, VMEM],
         out_specs=VMEM,
         compiler_params=room(16),
         interpret=interpret,
@@ -243,7 +249,7 @@
             pltpu.VMEM((WIDTH, TOK), BF),
             pltpu.SemaphoreType.DMA((18,)),
         ],
-        compiler_params=room(62),
+        compiler_params=room(40),
         interpret=interpret,
     )(*operands)
 
@@ -266,15 +272,12 @@
     zh, core = lax.axis_index("zh"), lax.axis_index("core")
     w_out = w_out.T
     scal = jnp.stack([count, zh, core, yx * 64 + zl * 8]).astype(jnp.int32)
-    own, ahead, even, tail = prepare_call(scal, rows, w_in, w_qkv.T, w_out)
-    line = lax.all_to_all(ahead.reshape(16, 8, WIDTH), Z, 0, 0, tiled=True)
+    own, ahead, even = prepare_call(scal, rows, w_in, w_qkv.T, w_out)
+    line = lax.all_to_all(ahead.reshape(16, 16, WIDTH), Z, 0, 0, tiled=True)
     mate = swap(own, "core")
-    tail = swap(tail, "zh")
     partner = lax.ppermute(even, "zl", [(i, i ^ 1) for i in range(8)])
-    line, mate, tail, partner = lax.optimization_barrier(
-        (line.reshape(2, 64, WIDTH), mate, tail, partner)
-    )
-    got = lax.all_to_all(split_call(scal, line, tail), YX, 0, 0, tiled=True)
+    line, mate, partner = lax.optimization_barrier((line.reshape(2, 128, WIDTH), mate, partner))
+    got = lax.all_to_all(split_call(scal, line), YX, 0, 0, tiled=True)
     over_rest = got[:, 128:].reshape(128, WIDTH)
     cross, cross_rest = swap(got[:, :64], "core"), swap(over_rest, "core")
     out, keep, send = layer_call(

time: 180 us -> 181 us (level)
  waiting for transfers between devices: 12.6 us -> 23.3 us
  starting transfers between devices: 36 us -> 26.6 us
  blocking collectives: 102 us -> 106 us
  local copies, waits for them, and re-layouts: 3.74 us -> 1.41 us
    ppermute x1, waiting for transfers between devices: 0.01 us -> 20.3 us  [shards(): partner = lax.ppermute(even, 'zl', [(i, i ^ 1) for i in range(8)])]
    ppermute x5 -> x4, waiting for transfers between devices: 12.6 us -> 2.99 us  [swap(): return lax.ppermute(value, axis, [(0, 1), (1, 0)])]
    ppermute x5 -> x4, starting transfers between devices: 17.9 us -> 8.49 us  [swap(): return lax.ppermute(value, axis, [(0, 1), (1, 0)])]
    all_to_all x1, blocking collectives: 26.4 us -> 30.1 us  [shards(): column = lax.all_to_all(column, Z, 0, 0, tiled=True)]
  transfers between devices with their start and end apart: 7 -> 6, of which waited for: 3 -> 3; matrix products, arithmetic and copies ran while one was open for 0% -> 0% of each run, Pallas kernels for 0% -> 0%
where the time goes in v6:
time: 181 us
  blocking collectives  106 us (59%)
  starting transfers between devices  26.6 us (15%)
  waiting for transfers between devices  23.3 us (13%)
  Pallas kernels  20.8 us (11%)
    all_to_all x1, blocking collectives, shards(): got = lax.all_to_all(split_call(scal, line), YX, 0, 0, tiled=True)  48.1 us
    all_to_all x1, blocking collectives, shards(): column = lax.all_to_all(column, Z, 0, 0, tiled=True)  30.1 us
    ppermute x1, waiting for transfers between devices, shards(): partner = lax.ppermute(even, 'zl', [(i, i ^ 1) for i in range(8)])  20.3 us
    pallas_call x1, Pallas kernels, layer_call(): pl.pallas_call(layer_kernel, out_shape=(jax.ShapeDtypeStruct((TOK, WIDTH)...  16.1 us
    all_to_all x1, blocking collectives, shards(): plane = lax.all_to_all(pair, YX, 0, 0, tiled=True)  15.7 us
    all_to_all x1, starting transfers between devices, shards(): line = lax.all_to_all(ahead.reshape(16, 16, WIDTH), Z, 0, 0, tiled=True)  14.8 us
    all_to_all x1, blocking collectives, spread(): lax.all_to_all(jnp.broadcast_to(block[None], (size,) + block.shape), axes...  12.5 us
    ppermute x4, starting transfers between devices, swap(): return lax.ppermute(value, axis, [(0, 1), (1, 0)])  8.49 us
  transfers between devices with their start and end apart: 6, of which 3 were waited for; matrix products, arithmetic and copies ran while one was open for 0% of the time, Pallas kernels for 0%

profile of v6, /device:TPU:64, one launch (start us, length us, event | category | flops | bytes accessed | tf_op | source)
XLA Modules:
  0.0 180.8 jit_solution(12928686208634741288)
XLA Ops:
  1.3 0.6 pad_add_fusion.scal
  1.8 0.0 copy-start.3
  1.8 3.8 %shard_map.77 = (bf16[1152,768]{1,0:T(8,128)(2,1)}, bf16[2,128,768]{2,1,0:T(8,128)(2,1)}, bf16[64,1536]{1,0:T(8,128)(2,1)}) custom-call(s32[4]{0:T(128)} %pad_add_fusion.scal, bf16[128,1536]{1,0:T(8,128)(2,1)} %bitcast.30, bf16[384,768]{1,0:T(8,128)(2,1)} %w_in.1, bf16[576,768]{1,0:T(8,128)(2,1)} %bitcast.40, bf16[192,768]{1,0:T(8,128)(2,1)} %bitcast.43), custom_call_target="tpu_custom_call" | custom-call | tf_op jit(solution)/shard_map/pallas_call | solution.py:186
  5.7 1.9 %collective-permute-start = (bf16[1152,768]{1,0:T(8,128)(2,1)}, bf16[1152,768]{1,0:T(8,128)(2,1)S(1)}, u32[]{:S(2)}, u32[]{:S(2)}) collective-permute-start(bf16[1152,768]{1,0:T(8,128)(2,1)} %get-tuple-element.12), channel_id=1, source_target_pairs={{0,1},{1,0},{2,3},{3,2},{4,5},{5,4},{6,7},{7,6},{8,9},{9,8},{10,11... | collective-permute-start | bytes 5308424 | tf_op jit(solution)/shard_map/ppermute | solution.py:264
  7.6 14.8 %all-to-all-start = ((bf16[16,16,768]{2,1,0:T(8,128)(2,1)}), bf16[16,16,768]{2,1,0:T(8,128)(2,1)S(1)}, u32[]{:S(2)}, u32[]{:S(2)}) async-start(bf16[16,16,768]{2,1,0:T(8,128)(2,1)} %bitcast.42), calls=%async_computation | async-start | bytes 786432 | tf_op jit(solution)/shard_map/all_to_all | solution.py:276
  22.4 3.4 %collective-permute-start.1 = (bf16[64,1536]{1,0:T(8,128)(2,1)}, bf16[64,1536]{1,0:T(8,128)(2,1)S(1)}, u32[]{:S(2)}, u32[]{:S(2)}) collective-permute-start(bf16[64,1536]{1,0:T(8,128)(2,1)} %get-tuple-element.13), channel_id=1, source_target_pairs={{0,4},{4,0},{8,12},{12,8},{16,20},{20,16},{24,28},{28,24},{1,5},{5... | collective-permute-start | bytes 589832 | tf_op jit(solution)/shard_map/ppermute | solution.py:278
  25.8 20.3 %collective-permute-done.1 = bf16[64,1536]{1,0:T(8,128)(2,1)S(1)} collective-permute-done((bf16[64,1536]{1,0:T(8,128)(2,1)}, bf16[64,1536]{1,0:T(8,128)(2,1)S(1)}, u32[]{:S(2)}, u32[]{:S(2)}) %collective-permute-start.1) | collective-permute-done | bytes 196640 | tf_op jit(solution)/shard_map/ppermute | solution.py:278
  46.1 0.0 all-to-all-done
  46.1 0.0 collective-permute-done
  46.1 0.0 copy-done.3
  46.1 0.9 shard_map.78
  47.0 48.1 %all_to_all.25.got = bf16[16,136,768]{2,1,0:T(8,128)(2,1)S(1)} all-to-all(bf16[16,136,768]{2,1,0:T(8,128)(2,1)S(1)} %shard_map.78), channel_id=1, replica_groups=mesh['y'=4,'x'=4,'zl'=8,'zh'=2,'core'=2] {'y','x'}, dimensions={0} | all-to-all | bytes 6684672 | tf_op jit(solution)/shard_map/all_to_all | solution.py:280
  95.1 0.0 copy-start
  95.1 0.0 copy-start.1
  95.1 0.1 slice.8
  95.3 2.1 %collective-permute-start.2 = (bf16[16,64,768]{2,1,0:T(8,128)(2,1)S(1)}, bf16[16,64,768]{2,1,0:T(8,128)(2,1)S(1)}, u32[]{:S(2)}, u32[]{:S(2)}) collective-permute-start(bf16[16,64,768]{2,1,0:T(8,128)(2,1)S(1)} %slice.8), channel_id=1, source_target_pairs={{0,1},{1,0},{2,3},{3,2},{4,5},{5,4},{6,7},{7,6},{8,9},{9,8},{10,11... | collective-permute-start | bytes 4718600 | tf_op jit(solution)/shard_map/ppermute | solution.py:264
  97.4 2.4 %collective-permute-start.3 = (bf16[128,768]{1,0:T(8,128)(2,1)S(1)}, bf16[128,768]{1,0:T(8,128)(2,1)S(1)}, u32[]{:S(2)}, u32[]{:S(2)}) collective-permute-start(bf16[128,768]{1,0:T(8,128)(2,1)S(1)} %get-tuple-element.20), channel_id=1, source_target_pairs={{0,1},{1,0},{2,3},{3,2},{4,5},{5,4},{6,7},{7,6},{8,9},{9,8},{10,11... | collective-permute-start | bytes 589832 | tf_op jit(solution)/shard_map/ppermute | solution.py:264
  99.8 1.2 collective-permute-done.3
  101.0 0.0 collective-permute-done.2.cross
  101.0 0.0 copy-done
  101.0 0.0 copy-done.1
  101.0 0.0 copy-done.2
  101.0 16.1 %shard_map.79 = (f32[128,768]{1,0:T(8,128)}, f32[16,2,24,384]{3,2,1,0:T(8,128)S(1)}, bf16[16,2,24,384]{3,2,1,0:T(8,128)(2,1)S(1)}) custom-call(s32[4]{0:T(128)S(1)} %copy-done.3, bf16[4,32,1536]{2,1,0:T(8,128)(2,1)S(1)} %bitcast.31, bf16[2,32,1536]{2,1,0:T(8,128)(2,1)S(1)} %bitcast.35, bf16[18,64,768]{2,1,0:T(8,128)(2,1)S(1)} %bitcast.28, ...), custom_call_target="tpu_custom_call" | custom-call | tf_op jit(solution)/shard_map/pallas_call | solution.py:237
  117.1 2.1 %collective-permute-start.4 = (bf16[16,2,24,384]{3,2,1,0:T(8,128)(2,1)S(1)}, bf16[16,2,24,384]{3,2,1,0:T(8,128)(2,1)S(1)}, u32[]{:S(2)}, u32[]{:S(2)}) collective-permute-start(bf16[16,2,24,384]{3,2,1,0:T(8,128)(2,1)S(1)} %get-tuple-element.19), channel_id=1, source_target_pairs={{0,1},{1,0},{2,3},{3,2},{4,5},{5,4},{6,7},{7,6},{8,9},{9,8},{10,11... | collective-permute-start | bytes 1769480 | tf_op jit(solution)/shard_map/ppermute | solution.py:264
  119.2 1.8 collective-permute-done.4
  121.0 0.1 add_convert_fusion
  121.1 15.7 %all_to_all.26 = bf16[16,2,24,384]{3,2,1,0:T(8,128)(2,1)S(1)} all-to-all(bf16[16,2,24,384]{3,2,1,0:T(8,128)(2,1)S(1)} %add_convert_fusion), channel_id=1, replica_groups=mesh['y'=4,'x'=4,'zl'=8,'zh'=2,'core'=2] {'y','x'}, dimensions={0} | all-to-all | bytes 1179648 | tf_op jit(solution)/shard_map/all_to_all | solution.py:296
  136.8 0.1 reduce_sum.24
  137.0 30.1 %all_to_all.27 = bf16[16,24,384]{2,1,0:T(8,128)(2,1)S(1)} all-to-all(bf16[16,24,384]{2,1,0:T(8,128)(2,1)S(1)} %bitcast.39), channel_id=1, replica_groups=mesh['y'=4,'x'=4,'zl'=8,'zh'=2,'core'=2] {'zh','zl'}, dimensions={0} | all-to-all | bytes 589824 | tf_op jit(solution)/shard_map/all_to_all | solution.py:299
  167.2 12.5 %all_to_all.28 = bf16[16,24,384]{2,1,0:T(8,128)(2,1)S(1)} all-to-all(bf16[16,24,384]{2,1,0:T(8,128)(2,1)S(1)} %broadcast_in_dim.8), channel_id=1, replica_groups=mesh['y'=4,'x'=4,'zl'=8,'zh'=2,'core'=2] {'y','x'}, dimensions={0} | all-to-all | bytes 589824 | tf_op jit(solution)/shard_map/all_to_all | solution.py:258
  179.7 0.3 copy.9
  180.0 0.9 copy.10
  (6 shorter events, 0.2 us)
Async XLA Ops:
  1.8 44.2 %copy-start.3 = (s32[4]{0:T(128)S(1)}, s32[4]{0:T(128)}, u32[]{:S(2)}) copy-start(s32[4]{0:T(128)} %pad_add_fusion.scal) | copy-start | bytes 52
  5.7 40.4 %collective-permute-start = (bf16[1152,768]{1,0:T(8,128)(2,1)}, bf16[1152,768]{1,0:T(8,128)(2,1)S(1)}, u32[]{:S(2)}, u32[]{:S(2)}) collective-permute-start(bf16[1152,768]{1,0:T(8,128)(2,1)} %get-tuple-element.12), channel_id=1, source_target_pairs={{0,1},{1,0},{2,3},{3,2},{4,5},{5,4},{6,7},{7,6},{8,9},{9,8},{10,11... | collective-permute-start | bytes 5308424 | tf_op jit(solution)/shard_map/ppermute | solution.py:264
  7.6 38.4 %all-to-all-start = ((bf16[16,16,768]{2,1,0:T(8,128)(2,1)}), bf16[16,16,768]{2,1,0:T(8,128)(2,1)S(1)}, u32[]{:S(2)}, u32[]{:S(2)}) async-start(bf16[16,16,768]{2,1,0:T(8,128)(2,1)} %bitcast.42), calls=%async_computation | async-start | bytes 786432 | tf_op jit(solution)/shard_map/all_to_all | solution.py:276
  22.4 23.7 %collective-permute-start.1 = (bf16[64,1536]{1,0:T(8,128)(2,1)}, bf16[64,1536]{1,0:T(8,128)(2,1)S(1)}, u32[]{:S(2)}, u32[]{:S(2)}) collective-permute-start(bf16[64,1536]{1,0:T(8,128)(2,1)} %get-tuple-element.13), channel_id=1, source_target_pairs={{0,4},{4,0},{8,12},{12,8},{16,20},{20,16},{24,28},{28,24},{1,5},{5... | collective-permute-start | bytes 589832 | tf_op jit(solution)/shard_map/ppermute | solution.py:278
  95.1 5.9 %copy-start = (bf16[1152,768]{1,0:T(8,128)(2,1)S(1)}, bf16[1152,768]{1,0:T(8,128)(2,1)}, u32[]{:S(2)}) copy-start(bf16[1152,768]{1,0:T(8,128)(2,1)} %get-tuple-element.12) | copy-start | bytes 5308420
  95.1 5.9 %copy-start.1 = (bf16[1,128,1536]{2,1,0:T(8,128)(2,1)S(1)}, bf16[1,128,1536]{2,1,0:T(8,128)(2,1)}, u32[]{:S(2)}) copy-start(bf16[1,128,1536]{2,1,0:T(8,128)(2,1)} %param.6) | copy-start | bytes 1179652
  95.1 5.9 %copy-start.2 = (bf16[1,128,768]{2,1,0:T(8,128)(2,1)S(1)}, bf16[1,128,768]{2,1,0:T(8,128)(2,1)}, u32[]{:S(2)}) copy-start(bf16[1,128,768]{2,1,0:T(8,128)(2,1)} %param.11) | copy-start | bytes 589828
  95.3 5.7 %collective-permute-start.2 = (bf16[16,64,768]{2,1,0:T(8,128)(2,1)S(1)}, bf16[16,64,768]{2,1,0:T(8,128)(2,1)S(1)}, u32[]{:S(2)}, u32[]{:S(2)}) collective-permute-start(bf16[16,64,768]{2,1,0:T(8,128)(2,1)S(1)} %slice.8), channel_id=1, source_target_pairs={{0,1},{1,0},{2,3},{3,2},{4,5},{5,4},{6,7},{7,6},{8,9},{9,8},{10,11... | collective-permute-start | bytes 4718600 | tf_op jit(solution)/shard_map/ppermute | solution.py:264
  97.4 3.6 %collective-permute-start.3 = (bf16[128,768]{1,0:T(8,128)(2,1)S(1)}, bf16[128,768]{1,0:T(8,128)(2,1)S(1)}, u32[]{:S(2)}, u32[]{:S(2)}) collective-permute-start(bf16[128,768]{1,0:T(8,128)(2,1)S(1)} %get-tuple-element.20), channel_id=1, source_target_pairs={{0,1},{1,0},{2,3},{3,2},{4,5},{5,4},{6,7},{7,6},{8,9},{9,8},{10,11... | collective-permute-start | bytes 589832 | tf_op jit(solution)/shard_map/ppermute | solution.py:264
  117.1 3.9 %collective-permute-start.4 = (bf16[16,2,24,384]{3,2,1,0:T(8,128)(2,1)S(1)}, bf16[16,2,24,384]{3,2,1,0:T(8,128)(2,1)S(1)}, u32[]{:S(2)}, u32[]{:S(2)}) collective-permute-start(bf16[16,2,24,384]{3,2,1,0:T(8,128)(2,1)S(1)} %get-tuple-element.19), channel_id=1, source_target_pairs={{0,1},{1,0},{2,3},{3,2},{4,5},{5,4},{6,7},{7,6},{8,9},{9,8},{10,11... | collective-permute-start | bytes 1769480 | tf_op jit(solution)/shard_map/ppermute | solution.py:264

commit v7 on v5

--- a/solution.py
+++ b/solution.py
@@ -90,24 +90,24 @@
     twice = jnp.where(lane & 1 == 0, F32(1), F32(0))
     for c in copies[:8]:
         c.wait()
-    keys = given[...].reshape(WIDTH, TILE)
-    hid[...] = dot(keys, win[...].reshape(TILE, WIDTH), NN).astype(BF)
+    keys = given.reshape(WIDTH, TILE)
+    hid[...] = dot(keys[...], win.reshape(TILE, WIDTH)[...], NN).astype(BF)
     bias = jnp.concatenate(
         [
             jnp.where(lane < count, twice, F32(LOW)),
-            key_bias(keys[TOK : TOK + 64]),
+            key_bias(keys[pl.ds(TOK, 64), :]),
             jnp.full((1, 64), LOW, F32),
-            key_bias(keys[256:]),
+            key_bias(keys[pl.ds(256, FAR), :]),
         ],
         axis=1,
     )
     for c in copies[8:12]:
         c.wait()
-    flat = wqkv[...].reshape(3 * WIDTH, WIDTH)
-    kv[...] = dot(flat[WIDTH:], hid[...], NT).astype(BF)
+    flat = wqkv.reshape(3 * WIDTH, WIDTH)
+    kv[...] = dot(flat[pl.ds(WIDTH, 2 * WIDTH), :], hid[...], NT).astype(BF)
     own_hid = hid[pl.ds(0, TOK), :]
     for h in range(HEADS):
-        q = dot(own_hid, flat[h * HEAD : (h + 1) * HEAD], NT).astype(BF)
+        q = dot(own_hid, flat[pl.ds(h * HEAD, HEAD), :], NT).astype(BF)
         s = dot(q, kv[pl.ds(h * HEAD, HEAD), :], NN) * F32(SCALE) + bias
         p = jnp.exp2(s - jnp.max(s, axis=1, keepdims=True))
         o = dot(p.astype(BF), kv[pl.ds(WIDTH + h * HEAD, HEAD), :], NT)
@@ -128,7 +128,7 @@
                     )
     for c in copies[12:]:
         c.wait()
-    out[...] = dot(wout[...].reshape(WIDTH, WIDTH), attn[...], NN).T
+    out[...] = dot(wout.reshape(WIDTH, WIDTH)[...], attn[...], NN).T
 
 
 ANY = pl.BlockSpec(memory_space=pl.ANY)
@@ -140,7 +140,7 @@
     return pltpu.CompilerParams(vmem_limit_bytes=mebibytes * 1024 * 1024)
 
 
-def prepare_kernel(scal, rows, w_in, w_qkv, w_out, own, ahead, even, tail, sems):
+def prepare_kernel(scal, rows, w_in, w_qkv, w_out, own, ahead, even, sems):
     count, zh, at = scal[0], scal[1], scal[3]
     moves = [
         (w_in, own.at[pl.ds(0, 384)]),
@@ -171,11 +171,6 @@
     start = pl.multiple_of(at // 16 * 16, 16)
     wide = own[pl.ds(start, 16), :].astype(F32)
     eight = jnp.where(at > start, wide[8:16], wide[0:8])
-    first = 8 * (at // 64)
-    start = pl.multiple_of(1024 + first // 16 * 16, 16)
-    wide = own[pl.ds(start, 16), :].astype(F32)
-    last = jnp.where(first % 16 > 0, wide[8:16], wide[0:8])
-    tail[...] = jnp.concatenate([last, last], axis=0).astype(BF)
     far = jnp.concatenate([distant[:, :WIDTH], distant[:, WIDTH:]], axis=0)
     for half in range(2):
         value = jnp.where(zh == half, far, eight)
@@ -189,27 +184,22 @@
             jax.ShapeDtypeStruct((PACK, WIDTH), BF),
             jax.ShapeDtypeStruct((2, 64, WIDTH), BF),
             jax.ShapeDtypeStruct((TOK // 2, TILE), BF),
-            jax.ShapeDtypeStruct((16, WIDTH), BF),
         ),
         in_specs=[SMEM, VMEM] + [ANY] * 3,
-        out_specs=(VMEM,) * 4,
+        out_specs=(VMEM,) * 3,
         scratch_shapes=[pltpu.SemaphoreType.DMA((3,))],
         compiler_params=room(62),
         interpret=interpret,
     )(*operands)
 
 
-def split_kernel(scal, line, tail, payload):
+def split_kernel(scal, line, payload):
     zh = scal[1]
-    piece = line[1 - zh]
     target = lax.broadcasted_iota(jnp.int32, (64, 64), 0)
     source = lax.broadcasted_iota(jnp.int32, (64, 64), 1)
     origin = (target & 31) // 4 * 8 + target // 32 * 4 + (target & 3)
     pick = jnp.where(source == origin, F32(1), F32(0)).astype(BF)
-    ordered = dot(pick, line[zh], NN).astype(BF)
-    both = jnp.concatenate(
-        [piece.astype(F32), ordered.astype(F32), tail[...].astype(F32)[0:8]], axis=0
-    ).astype(BF)
+    both = jnp.concatenate([line[1 - zh], dot(pick, line[zh], NN).astype(BF)], axis=0)
     for i in range(16):
         payload[i] = both
 
@@ -217,8 +207,8 @@
 def split_call(*operands, interpret=False):
     return pl.pallas_call(
         split_kernel,
-        out_shape=jax.ShapeDtypeStruct((16, 136, WIDTH), BF),
-        in_specs=[SMEM, VMEM, VMEM],
+        out_shape=jax.ShapeDtypeStruct((16, 128, WIDTH), BF),
+        in_specs=[SMEM, VMEM],
         out_specs=VMEM,
         compiler_params=room(16),
         interpret=interpret,
@@ -243,7 +233,7 @@
             pltpu.VMEM((WIDTH, TOK), BF),
             pltpu.SemaphoreType.DMA((18,)),
         ],
-        compiler_params=room(62),
+        compiler_params=room(40),
         interpret=interpret,
     )(*operands)
 
@@ -266,17 +256,16 @@
     zh, core = lax.axis_index("zh"), lax.axis_index("core")
     w_out = w_out.T
     scal = jnp.stack([count, zh, core, yx * 64 + zl * 8]).astype(jnp.int32)
-    own, ahead, even, tail = prepare_call(scal, rows, w_in, w_qkv.T, w_out)
+    own, ahead, even = prepare_call(scal, rows, w_in, w_qkv.T, w_out)
     line = lax.all_to_all(ahead.reshape(16, 8, WIDTH), Z, 0, 0, tiled=True)
     mate = swap(own, "core")
-    tail = swap(tail, "zh")
     partner = lax.ppermute(even, "zl", [(i, i ^ 1) for i in range(8)])
-    line, mate, tail, partner = lax.optimization_barrier(
-        (line.reshape(2, 64, WIDTH), mate, tail, partner)
-    )
-    got = lax.all_to_all(split_call(scal, line, tail), YX, 0, 0, tiled=True)
-    over_rest = got[:, 128:].reshape(128, WIDTH)
-    cross, cross_rest = swap(got[:, :64], "core"), swap(over_rest, "core")
+    line, mate, partner = lax.optimization_barrier((line.reshape(2, 64, WIDTH), mate, partner))
+    got = lax.all_to_all(split_call(scal, line), YX, 0, 0, tiled=True)
+    over_rest = swap(w_out[64:], "zh")
+    cross_rest = swap(over_rest, "core")
+    got, over_rest, cross_rest = lax.optimization_barrier((got, over_rest, cross_rest))
+    cross = swap(got[:, :64], "core")
     out, keep, send = layer_call(
         scal,
         rows.reshape(4, 32, TILE),

time: 180 us -> 184 us (1.022)
  blocking collectives: 102 us -> 58.9 us
  waiting for transfers between devices: 12.6 us -> 52.1 us
  starting transfers between devices: 36 us -> 42.8 us
  local copies, waits for them, and re-layouts: 3.74 us -> 6.88 us
    all_to_all x1 -> x0, blocking collectives: 48.1 us -> none  [shards(): got = lax.all_to_all(split_call(scal, line, tail), YX, 0, 0, tiled=True)]
    all_to_all x0 -> x1, waiting for transfers between devices: none -> 14.5 us  [shards(): got = lax.all_to_all(split_call(scal, line), YX, 0, 0, tiled=True)]
    ppermute x5, waiting for transfers between devices: 12.6 us -> 26 us  [swap(): return lax.ppermute(value, axis, [(0, 1), (1, 0)])]
    ppermute x1, waiting for transfers between devices: 0.01 us -> 11.5 us  [shards(): partner = lax.ppermute(even, 'zl', [(i, i ^ 1) for i in range(8)])]
    all_to_all x0 -> x1, starting transfers between devices: none -> 7.17 us  [shards(): got = lax.all_to_all(split_call(scal, line), YX, 0, 0, tiled=True)]
    unnamed x13 -> x29, local copies, waits for them, and re-layouts: 2.51 us -> 6.39 us
    all_to_all x1, blocking collectives: 26.4 us -> 29.9 us  [shards(): column = lax.all_to_all(column, Z, 0, 0, tiled=True)]
  transfers between devices with their start and end apart: 7 -> 8, of which waited for: 3 -> 6; matrix products, arithmetic and copies ran while one was open for 0% -> 0% of each run, Pallas kernels for 0% -> 0%
where the time goes in v7:
time: 184 us
  blocking collectives  58.9 us (32%)
  waiting for transfers between devices  52.1 us (28%)
  starting transfers between devices  42.8 us (23%)
  Pallas kernels  20.7 us (11%)
  local copies, waits for them, and re-layouts  6.88 us (4%)
    all_to_all x1, blocking collectives, shards(): column = lax.all_to_all(column, Z, 0, 0, tiled=True)  29.9 us
    ppermute x5, waiting for transfers between devices, swap(): return lax.ppermute(value, axis, [(0, 1), (1, 0)])  26 us
    ppermute x5, starting transfers between devices, swap(): return lax.ppermute(value, axis, [(0, 1), (1, 0)])  17.5 us
    all_to_all x1, blocking collectives, shards(): plane = lax.all_to_all(pair, YX, 0, 0, tiled=True)  16.8 us
    pallas_call x1, Pallas kernels, layer_call(): pl.pallas_call(layer_kernel, out_shape=(jax.ShapeDtypeStruct((TOK, WIDTH)...  16.1 us
    all_to_all x1, starting transfers between devices, shards(): line = lax.all_to_all(ahead.reshape(16, 8, WIDTH), Z, 0, 0, tiled=True)  14.8 us
    all_to_all x1, waiting for transfers between devices, shards(): got = lax.all_to_all(split_call(scal, line), YX, 0, 0, tiled=True)  14.5 us
    all_to_all x1, blocking collectives, spread(): lax.all_to_all(jnp.broadcast_to(block[None], (size,) + block.shape), axes...  12.3 us
  transfers between devices with their start and end apart: 8, of which 6 were waited for; matrix products, arithmetic and copies ran while one was open for 0% of the time, Pallas kernels for 0%

profile of v7, /device:TPU:64, one launch (start us, length us, event | category | flops | bytes accessed | tf_op | source)
XLA Modules:
  0.0 183.8 jit_solution(6900081149818281324)
XLA Ops:
  1.3 0.6 pad_add_fusion.scal
  1.9 3.8 %shard_map.77 = (bf16[1152,768]{1,0:T(8,128)(2,1)}, bf16[2,64,768]{2,1,0:T(8,128)(2,1)}, bf16[64,1536]{1,0:T(8,128)(2,1)}) custom-call(s32[4]{0:T(128)} %pad_add_fusion.scal, bf16[128,1536]{1,0:T(8,128)(2,1)} %bitcast.28, bf16[384,768]{1,0:T(8,128)(2,1)} %w_in.1, bf16[576,768]{1,0:T(8,128)(2,1)} %bitcast.38, bf16[192,768]{1,0:T(8,128)(2,1)} %bitcast.39), custom_call_target="tpu_custom_call" | custom-call | tf_op jit(solution)/shard_map/pallas_call | solution.py:181
  5.7 1.9 %collective-permute-start = (bf16[1152,768]{1,0:T(8,128)(2,1)}, bf16[1152,768]{1,0:T(8,128)(2,1)S(1)}, u32[]{:S(2)}, u32[]{:S(2)}) collective-permute-start(bf16[1152,768]{1,0:T(8,128)(2,1)} %get-tuple-element.15), channel_id=1, source_target_pairs={{0,1},{1,0},{2,3},{3,2},{4,5},{5,4},{6,7},{7,6},{8,9},{9,8},{10,11... | collective-permute-start | bytes 5308424 | tf_op jit(solution)/shard_map/ppermute | solution.py:248
  7.6 14.8 %all-to-all-start = ((bf16[16,8,768]{2,1,0:T(8,128)(2,1)}), bf16[16,8,768]{2,1,0:T(8,128)(2,1)S(1)}, u32[]{:S(2)}, u32[]{:S(2)}) async-start(bf16[16,8,768]{2,1,0:T(8,128)(2,1)} %bitcast.42), calls=%async_computation | async-start | bytes 393216 | tf_op jit(solution)/shard_map/all_to_all | solution.py:260
  22.4 3.4 %collective-permute-start.1 = (bf16[64,1536]{1,0:T(8,128)(2,1)}, bf16[64,1536]{1,0:T(8,128)(2,1)S(1)}, u32[]{:S(2)}, u32[]{:S(2)}) collective-permute-start(bf16[64,1536]{1,0:T(8,128)(2,1)} %get-tuple-element.16), channel_id=1, source_target_pairs={{0,4},{4,0},{8,12},{12,8},{16,20},{20,16},{24,28},{28,24},{1,5},{5... | collective-permute-start | bytes 589832 | tf_op jit(solution)/shard_map/ppermute | solution.py:262
  25.7 11.5 %collective-permute-done.1 = bf16[64,1536]{1,0:T(8,128)(2,1)S(1)} collective-permute-done((bf16[64,1536]{1,0:T(8,128)(2,1)}, bf16[64,1536]{1,0:T(8,128)(2,1)S(1)}, u32[]{:S(2)}, u32[]{:S(2)}) %collective-permute-start.1) | collective-permute-done | bytes 196640 | tf_op jit(solution)/shard_map/ppermute | solution.py:262
  37.3 0.7 copy-done.6
  38.0 0.9 shard_map.78
  38.9 0.4 copy-done.2
  39.2 1.7 copy-done
  40.9 7.2 %all-to-all-start.1 = ((bf16[16,128,768]{2,1,0:T(8,128)(2,1)}), bf16[16,128,768]{2,1,0:T(8,128)(2,1)S(1)}, u32[]{:S(2)}, u32[]{:S(2)}) async-start(bf16[16,128,768]{2,1,0:T(8,128)(2,1)} %copy-done), calls=%async_computation.1 | async-start | bytes 6291456 | tf_op jit(solution)/shard_map/all_to_all | solution.py:264
  48.1 9.6 %collective-permute-start.2 = (bf16[128,768]{1,0:T(8,128)(2,1)S(1)}, bf16[128,768]{1,0:T(8,128)(2,1)S(1)}, u32[]{:S(2)}, u32[]{:S(2)}) collective-permute-start(bf16[128,768]{1,0:T(8,128)(2,1)S(1)} %slice.8), channel_id=1, source_target_pairs={{0,2},{2,0},{1,3},{3,1},{4,6},{6,4},{5,7},{7,5},{8,10},{10,8},{9,1... | collective-permute-start | bytes 589832 | tf_op jit(solution)/shard_map/ppermute | solution.py:248
  57.7 20.0 %collective-permute-done.2 = bf16[128,768]{1,0:T(8,128)(2,1)S(1)} collective-permute-done((bf16[128,768]{1,0:T(8,128)(2,1)S(1)}, bf16[128,768]{1,0:T(8,128)(2,1)S(1)}, u32[]{:S(2)}, u32[]{:S(2)}) %collective-permute-start.2) | collective-permute-done | bytes 196640 | tf_op jit(solution)/shard_map/ppermute | solution.py:248
  77.7 1.9 %collective-permute-start.3 = (bf16[128,768]{1,0:T(8,128)(2,1)S(1)}, bf16[128,768]{1,0:T(8,128)(2,1)S(1)}, u32[]{:S(2)}, u32[]{:S(2)}) collective-permute-start(bf16[128,768]{1,0:T(8,128)(2,1)S(1)} %collective-permute-done.2), channel_id=1, source_target_pairs={{0,1},{1,0},{2,3},{3,2},{4,5},{5,4},{6,7},{7,6},{8,9},{9,8},{10,11... | collective-permute-start | bytes 589832 | tf_op jit(solution)/shard_map/ppermute | solution.py:248
  79.6 0.7 copy-done.8
  80.3 0.7 collective-permute-done.3
  81.0 0.7 copy-done.10
  81.7 14.5 %all-to-all-done.1.got = bf16[16,128,768]{2,1,0:T(8,128)(2,1)S(1)} async-done(((bf16[16,128,768]{2,1,0:T(8,128)(2,1)}), bf16[16,128,768]{2,1,0:T(8,128)(2,1)S(1)}, u32[]{:S(2)}, u32[]{:S(2)}) %all-to-all-start.1) | async-done | bytes 3145760 | tf_op jit(solution)/shard_map/all_to_all | solution.py:264
  96.3 0.1 slice.7
  96.4 2.1 %collective-permute-start.4 = (bf16[16,64,768]{2,1,0:T(8,128)(2,1)S(1)}, bf16[16,64,768]{2,1,0:T(8,128)(2,1)S(1)}, u32[]{:S(2)}, u32[]{:S(2)}) collective-permute-start(bf16[16,64,768]{2,1,0:T(8,128)(2,1)S(1)} %slice.7), channel_id=1, source_target_pairs={{0,1},{1,0},{2,3},{3,2},{4,5},{5,4},{6,7},{7,6},{8,9},{9,8},{10,11... | collective-permute-start | bytes 4718600 | tf_op jit(solution)/shard_map/ppermute | solution.py:248
  98.4 3.4 %collective-permute-done.4.cross = bf16[16,64,768]{2,1,0:T(8,128)(2,1)S(1)} collective-permute-done((bf16[16,64,768]{2,1,0:T(8,128)(2,1)S(1)}, bf16[16,64,768]{2,1,0:T(8,128)(2,1)S(1)}, u32[]{:S(2)}, u32[]{:S(2)}) %collective-permute-start.4) | collective-permute-done | bytes 1572896 | tf_op jit(solution)/shard_map/ppermute | solution.py:248
  101.9 1.5 copy-done.3
  103.3 16.1 %shard_map.79 = (f32[128,768]{1,0:T(8,128)}, f32[16,2,24,384]{3,2,1,0:T(8,128)S(1)}, bf16[16,2,24,384]{3,2,1,0:T(8,128)(2,1)S(1)}) custom-call(s32[4]{0:T(128)S(1)} %copy-done.12, bf16[4,32,1536]{2,1,0:T(8,128)(2,1)S(1)} %bitcast.29, bf16[2,32,1536]{2,1,0:T(8,128)(2,1)S(1)} %bitcast.32, bf16[18,64,768]{2,1,0:T(8,128)(2,1)S(1)} %bitcast.26, ...), custom_call_target="tpu_custom_call" | custom-call | tf_op jit(solution)/shard_map/pallas_call | solution.py:221
  119.4 2.0 %collective-permute-start.5 = (bf16[16,2,24,384]{3,2,1,0:T(8,128)(2,1)S(1)}, bf16[16,2,24,384]{3,2,1,0:T(8,128)(2,1)S(1)}, u32[]{:S(2)}, u32[]{:S(2)}) collective-permute-start(bf16[16,2,24,384]{3,2,1,0:T(8,128)(2,1)S(1)} %get-tuple-element.25), channel_id=1, source_target_pairs={{0,1},{1,0},{2,3},{3,2},{4,5},{5,4},{6,7},{7,6},{8,9},{9,8},{10,11... | collective-permute-start | bytes 1769480 | tf_op jit(solution)/shard_map/ppermute | solution.py:248
  121.5 1.9 %collective-permute-done.5 = bf16[16,2,24,384]{3,2,1,0:T(8,128)(2,1)S(1)} collective-permute-done((bf16[16,2,24,384]{3,2,1,0:T(8,128)(2,1)S(1)}, bf16[16,2,24,384]{3,2,1,0:T(8,128)(2,1)S(1)}, u32[]{:S(2)}, u32[]{:S(2)}) %collective-permute-start.5) | collective-permute-done | bytes 589856 | tf_op jit(solution)/shard_map/ppermute | solution.py:248
  123.3 0.1 add_convert_fusion
  123.4 16.8 %all_to_all.25 = bf16[16,2,24,384]{3,2,1,0:T(8,128)(2,1)S(1)} all-to-all(bf16[16,2,24,384]{3,2,1,0:T(8,128)(2,1)S(1)} %add_convert_fusion), channel_id=1, replica_groups=mesh['y'=4,'x'=4,'zl'=8,'zh'=2,'core'=2] {'y','x'}, dimensions={0} | all-to-all | bytes 1179648 | tf_op jit(solution)/shard_map/all_to_all | solution.py:282
  140.2 0.1 reduce_sum.24
  140.3 29.9 %all_to_all.26 = bf16[16,24,384]{2,1,0:T(8,128)(2,1)S(1)} all-to-all(bf16[16,24,384]{2,1,0:T(8,128)(2,1)S(1)} %bitcast.37), channel_id=1, replica_groups=mesh['y'=4,'x'=4,'zl'=8,'zh'=2,'core'=2] {'zh','zl'}, dimensions={0} | all-to-all | bytes 589824 | tf_op jit(solution)/shard_map/all_to_all | solution.py:285
  170.3 12.3 %all_to_all.27 = bf16[16,24,384]{2,1,0:T(8,128)(2,1)S(1)} all-to-all(bf16[16,24,384]{2,1,0:T(8,128)(2,1)S(1)} %broadcast_in_dim.8), channel_id=1, replica_groups=mesh['y'=4,'x'=4,'zl'=8,'zh'=2,'core'=2] {'y','x'}, dimensions={0} | all-to-all | bytes 589824 | tf_op jit(solution)/shard_map/all_to_all | solution.py:242
  182.6 0.3 copy.9
  182.9 0.9 copy.10
  (29 shorter events, 0.2 us)
Async XLA Ops:
  1.9 36.1 %copy-start.12 = (s32[4]{0:T(128)S(1)}, s32[4]{0:T(128)}, u32[]{:S(2)}) copy-start(s32[4]{0:T(128)} %pad_add_fusion.scal) | copy-start | bytes 52
  5.7 32.3 %collective-permute-start = (bf16[1152,768]{1,0:T(8,128)(2,1)}, bf16[1152,768]{1,0:T(8,128)(2,1)S(1)}, u32[]{:S(2)}, u32[]{:S(2)}) collective-permute-start(bf16[1152,768]{1,0:T(8,128)(2,1)} %get-tuple-element.15), channel_id=1, source_target_pairs={{0,1},{1,0},{2,3},{3,2},{4,5},{5,4},{6,7},{7,6},{8,9},{9,8},{10,11... | collective-permute-start | bytes 5308424 | tf_op jit(solution)/shard_map/ppermute | solution.py:248
  7.6 30.4 %all-to-all-start = ((bf16[16,8,768]{2,1,0:T(8,128)(2,1)}), bf16[16,8,768]{2,1,0:T(8,128)(2,1)S(1)}, u32[]{:S(2)}, u32[]{:S(2)}) async-start(bf16[16,8,768]{2,1,0:T(8,128)(2,1)} %bitcast.42), calls=%async_computation | async-start | bytes 393216 | tf_op jit(solution)/shard_map/all_to_all | solution.py:260
  22.4 14.9 %collective-permute-start.1 = (bf16[64,1536]{1,0:T(8,128)(2,1)}, bf16[64,1536]{1,0:T(8,128)(2,1)S(1)}, u32[]{:S(2)}, u32[]{:S(2)}) collective-permute-start(bf16[64,1536]{1,0:T(8,128)(2,1)} %get-tuple-element.16), channel_id=1, source_target_pairs={{0,4},{4,0},{8,12},{12,8},{16,20},{20,16},{24,28},{28,24},{1,5},{5... | collective-permute-start | bytes 589832 | tf_op jit(solution)/shard_map/ppermute | solution.py:262
  37.3 0.7 copy-start.6
  38.0 1.3 copy-start.2
  39.2 1.7 copy-start
  40.9 7.2 %copy-start.13 = (bf16[768,192]{0,1:T(8,128)(2,1)S(1)}, bf16[768,192]{0,1:T(8,128)(2,1)}, u32[]{:S(2)}) copy-start(bf16[768,192]{0,1:T(8,128)(2,1)} %param.10) | copy-start | bytes 884740
  40.9 55.4 %all-to-all-start.1 = ((bf16[16,128,768]{2,1,0:T(8,128)(2,1)}), bf16[16,128,768]{2,1,0:T(8,128)(2,1)S(1)}, u32[]{:S(2)}, u32[]{:S(2)}) async-start(bf16[16,128,768]{2,1,0:T(8,128)(2,1)} %copy-done), calls=%async_computation.1 | async-start | bytes 6291456 | tf_op jit(solution)/shard_map/all_to_all | solution.py:264
  48.1 53.7 %copy-start.4 = (bf16[1,128,1536]{2,1,0:T(8,128)(2,1)S(1)}, bf16[1,128,1536]{2,1,0:T(8,128)(2,1)}, u32[]{:S(2)}) copy-start(bf16[1,128,1536]{2,1,0:T(8,128)(2,1)} %param.6) | copy-start | bytes 1179652
  48.1 29.6 %collective-permute-start.2 = (bf16[128,768]{1,0:T(8,128)(2,1)S(1)}, bf16[128,768]{1,0:T(8,128)(2,1)S(1)}, u32[]{:S(2)}, u32[]{:S(2)}) collective-permute-start(bf16[128,768]{1,0:T(8,128)(2,1)S(1)} %slice.8), channel_id=1, source_target_pairs={{0,2},{2,0},{1,3},{3,1},{4,6},{6,4},{5,7},{7,5},{8,10},{10,8},{9,1... | collective-permute-start | bytes 589832 | tf_op jit(solution)/shard_map/ppermute | solution.py:248
  77.7 3.3 %collective-permute-start.3 = (bf16[128,768]{1,0:T(8,128)(2,1)S(1)}, bf16[128,768]{1,0:T(8,128)(2,1)S(1)}, u32[]{:S(2)}, u32[]{:S(2)}) collective-permute-start(bf16[128,768]{1,0:T(8,128)(2,1)S(1)} %collective-permute-done.2), channel_id=1, source_target_pairs={{0,1},{1,0},{2,3},{3,2},{4,5},{5,4},{6,7},{7,6},{8,9},{9,8},{10,11... | collective-permute-start | bytes 589832 | tf_op jit(solution)/shard_map/ppermute | solution.py:248
  79.6 0.7 copy-start.8
  81.0 0.7 copy-start.10
  96.2 5.6 %copy-start.1 = (bf16[1152,768]{1,0:T(8,128)(2,1)S(1)}, bf16[1152,768]{1,0:T(8,128)(2,1)}, u32[]{:S(2)}) copy-start(bf16[1152,768]{1,0:T(8,128)(2,1)} %get-tuple-element.15) | copy-start | bytes 5308420
  96.2 5.6 %copy-start.5 = (bf16[1,128,768]{2,1,0:T(8,128)(2,1)S(1)}, bf16[1,128,768]{2,1,0:T(8,128)(2,1)}, u32[]{:S(2)}) copy-start(bf16[1,128,768]{2,1,0:T(8,128)(2,1)} %param.11) | copy-start | bytes 589828
  96.2 5.6 %copy-start.7 = (bf16[64,1536]{1,0:T(8,128)(2,1)S(1)}, bf16[64,1536]{1,0:T(8,128)(2,1)}, u32[]{:S(2)}) copy-start(bf16[64,1536]{1,0:T(8,128)(2,1)} %copy-done.6) | copy-start | bytes 589828
  96.2 5.6 %copy-start.9 = (bf16[128,768]{1,0:T(8,128)(2,1)S(1)}, bf16[128,768]{1,0:T(8,128)(2,1)}, u32[]{:S(2)}) copy-start(bf16[128,768]{1,0:T(8,128)(2,1)} %copy-done.8) | copy-start | bytes 589828
  96.3 5.6 %copy-start.11 = (bf16[128,768]{1,0:T(8,128)(2,1)S(1)}, bf16[128,768]{1,0:T(8,128)(2,1)}, u32[]{:S(2)}) copy-start(bf16[128,768]{1,0:T(8,128)(2,1)} %copy-done.10) | copy-start | bytes 589828
  96.4 5.4 %collective-permute-start.4 = (bf16[16,64,768]{2,1,0:T(8,128)(2,1)S(1)}, bf16[16,64,768]{2,1,0:T(8,128)(2,1)S(1)}, u32[]{:S(2)}, u32[]{:S(2)}) collective-permute-start(bf16[16,64,768]{2,1,0:T(8,128)(2,1)S(1)} %slice.7), channel_id=1, source_target_pairs={{0,1},{1,0},{2,3},{3,2},{4,5},{5,4},{6,7},{7,6},{8,9},{9,8},{10,11... | collective-permute-start | bytes 4718600 | tf_op jit(solution)/shard_map/ppermute | solution.py:248
  101.9 1.5 copy-start.3
  119.4 3.9 %collective-permute-start.5 = (bf16[16,2,24,384]{3,2,1,0:T(8,128)(2,1)S(1)}, bf16[16,2,24,384]{3,2,1,0:T(8,128)(2,1)S(1)}, u32[]{:S(2)}, u32[]{:S(2)}) collective-permute-start(bf16[16,2,24,384]{3,2,1,0:T(8,128)(2,1)S(1)} %get-tuple-element.25), channel_id=1, source_target_pairs={{0,1},{1,0},{2,3},{3,2},{4,5},{5,4},{6,7},{7,6},{8,9},{9,8},{10,11... | collective-permute-start | bytes 1769480 | tf_op jit(solution)/shard_map/ppermute | solution.py:248

commit v8 on v7

--- a/solution.py
+++ b/solution.py
@@ -171,10 +171,19 @@
     start = pl.multiple_of(at // 16 * 16, 16)
     wide = own[pl.ds(start, 16), :].astype(F32)
     eight = jnp.where(at > start, wide[8:16], wide[0:8])
+    line = 1024 + at // 64 * 8 + at // 8 % 8
+    start = pl.multiple_of(line // 16 * 16, 16)
+    wide = own[pl.ds(start, 16), :].astype(F32)
+    single = lax.broadcasted_iota(jnp.int32, (16, WIDTH), 0) == line - start
+    ninth = jnp.sum(jnp.where(single, wide, F32(0)), axis=0, keepdims=True)
     far = jnp.concatenate([distant[:, :WIDTH], distant[:, WIDTH:]], axis=0)
+    spare = jnp.zeros((2, TOK), F32)
     for half in range(2):
         value = jnp.where(zh == half, far, eight)
-        ahead[half] = jnp.concatenate([value] * 8, axis=0).astype(BF)
+        lanes = [value[:, c * TOK : (c + 1) * TOK] for c in range(6)]
+        more = [ninth[:, c * TOK : (c + 1) * TOK] for c in range(6)]
+        block = jnp.concatenate(lanes + [jnp.concatenate(more + [spare], axis=0)], axis=0)
+        ahead[half] = jnp.concatenate([block] * 8, axis=0).astype(BF)
 
 
 def prepare_call(*operands, interpret=False):
@@ -182,7 +191,7 @@
         prepare_kernel,
         out_shape=(
             jax.ShapeDtypeStruct((PACK, WIDTH), BF),
-            jax.ShapeDtypeStruct((2, 64, WIDTH), BF),
+            jax.ShapeDtypeStruct((2, 448, TOK), BF),
             jax.ShapeDtypeStruct((TOK // 2, TILE), BF),
         ),
         in_specs=[SMEM, VMEM] + [ANY] * 3,
@@ -195,11 +204,29 @@
 
 def split_kernel(scal, line, payload):
     zh = scal[1]
-    target = lax.broadcasted_iota(jnp.int32, (64, 64), 0)
-    source = lax.broadcasted_iota(jnp.int32, (64, 64), 1)
-    origin = (target & 31) // 4 * 8 + target // 32 * 4 + (target & 3)
-    pick = jnp.where(source == origin, F32(1), F32(0)).astype(BF)
-    both = jnp.concatenate([line[1 - zh], dot(pick, line[zh], NN).astype(BF)], axis=0)
+    ours, theirs = line[zh], line[1 - zh]
+    target = lax.broadcasted_iota(jnp.int32, (64, 448), 0)
+    source = lax.broadcasted_iota(jnp.int32, (64, 448), 1)
+    piece = target // 8 * 56 + (target & 7)
+    ordered = (target & 31) // 4 * 56 + target // 32 * 4 + (target & 3)
+    rest = (target & 7) * 56 + 48
+    columns = []
+    for c in range(6):
+        picks = [
+            jnp.where(source == origin, F32(1), F32(0)).astype(BF)
+            for origin in (piece + 8 * c, ordered + 8 * c, rest + c)
+        ]
+        columns.append(
+            jnp.concatenate(
+                [
+                    dot(picks[0], theirs, NN),
+                    dot(picks[1], ours, NN),
+                    dot(picks[2], theirs, NN)[0:8],
+                ],
+                axis=0,
+            )
+        )
+    both = jnp.concatenate(columns, axis=1).astype(BF)
     for i in range(16):
         payload[i] = both
 
@@ -207,7 +234,7 @@
 def split_call(*operands, interpret=False):
     return pl.pallas_call(
         split_kernel,
-        out_shape=jax.ShapeDtypeStruct((16, 128, WIDTH), BF),
+        out_shape=jax.ShapeDtypeStruct((16, 136, WIDTH), BF),
         in_specs=[SMEM, VMEM],
         out_specs=VMEM,
         compiler_params=room(16),
@@ -257,15 +284,13 @@
     w_out = w_out.T
     scal = jnp.stack([count, zh, core, yx * 64 + zl * 8]).astype(jnp.int32)
     own, ahead, even = prepare_call(scal, rows, w_in, w_qkv.T, w_out)
-    line = lax.all_to_all(ahead.reshape(16, 8, WIDTH), Z, 0, 0, tiled=True)
+    line = lax.all_to_all(ahead.reshape(16, 56, TOK), Z, 0, 0, tiled=True)
     mate = swap(own, "core")
     partner = lax.ppermute(even, "zl", [(i, i ^ 1) for i in range(8)])
-    line, mate, partner = lax.optimization_barrier((line.reshape(2, 64, WIDTH), mate, partner))
+    line, mate, partner = lax.optimization_barrier((line.reshape(2, 448, TOK), mate, partner))
     got = lax.all_to_all(split_call(scal, line), YX, 0, 0, tiled=True)
-    over_rest = swap(w_out[64:], "zh")
-    cross_rest = swap(over_rest, "core")
-    got, over_rest, cross_rest = lax.optimization_barrier((got, over_rest, cross_rest))
-    cross = swap(got[:, :64], "core")
+    over_rest = got[:, 128:].reshape(128, WIDTH)
+    cross, cross_rest = swap(got[:, :64], "core"), swap(over_rest, "core")
     out, keep, send = layer_call(
         scal,
         rows.reshape(4, 32, TILE),

time: 184 us -> 175 us (0.951)
  blocking collectives: 58.9 us -> 107 us
  waiting for transfers between devices: 52.1 us -> 16 us
  starting transfers between devices: 42.8 us -> 26.6 us
  local copies, waits for them, and re-layouts: 6.88 us -> 1.41 us
    all_to_all x0 -> x1, blocking collectives: none -> 48.4 us  [shards(): got = lax.all_to_all(split_call(scal, line), YX, 0, 0, tiled=True)]
    ppermute x5 -> x4, waiting for transfers between devices: 26 us -> 2.98 us  [swap(): return lax.ppermute(value, axis, [(0, 1), (1, 0)])]
    all_to_all x2 -> x1, waiting for transfers between devices: 14.5 us -> 0.01 us  [shards(): line = lax.all_to_all(ahead.reshape(16, 56, TOK), Z, 0, 0, tiled=True)]
    ppermute x5 -> x4, starting transfers between devices: 17.5 us -> 8.5 us  [swap(): return lax.ppermute(value, axis, [(0, 1), (1, 0)])]
    all_to_all x2 -> x1, starting transfers between devices: 21.9 us -> 14.8 us  [shards(): line = lax.all_to_all(ahead.reshape(16, 56, TOK), Z, 0, 0, tiled=True)]
    unnamed x29 -> x9, local copies, waits for them, and re-layouts: 6.39 us -> 0.87 us
  transfers between devices with their start and end apart: 8 -> 6, of which waited for: 6 -> 3; matrix products, arithmetic and copies ran while one was open for 0% -> 0% of each run, Pallas kernels for 0% -> 0%
where the time goes in v8:
time: 175 us; the launch traced here: 174 us
  blocking collectives  107 us (61%)
  starting transfers between devices  26.6 us (15%)
  Pallas kernels  21 us (12%)
  waiting for transfers between devices  16 us (9%)
    all_to_all x1, blocking collectives, shards(): got = lax.all_to_all(split_call(scal, line), YX, 0, 0, tiled=True)  48.4 us
    all_to_all x1, blocking collectives, shards(): column = lax.all_to_all(column, Z, 0, 0, tiled=True)  30.2 us
    pallas_call x1, Pallas kernels, layer_call(): pl.pallas_call(layer_kernel, out_shape=(jax.ShapeDtypeStruct((TOK, WIDTH)...  16.1 us
    all_to_all x1, blocking collectives, shards(): plane = lax.all_to_all(pair, YX, 0, 0, tiled=True)  15.6 us
    all_to_all x1, starting transfers between devices, shards(): line = lax.all_to_all(ahead.reshape(16, 56, TOK), Z, 0, 0, tiled=True)  14.8 us
    ppermute x1, waiting for transfers between devices, shards(): partner = lax.ppermute(even, 'zl', [(i, i ^ 1) for i in range(8)])  13.1 us
    all_to_all x1, blocking collectives, spread(): lax.all_to_all(jnp.broadcast_to(block[None], (size,) + block.shape), axes...  12.4 us
    ppermute x4, starting transfers between devices, swap(): return lax.ppermute(value, axis, [(0, 1), (1, 0)])  8.5 us
  transfers between devices with their start and end apart: 6, of which 3 were waited for; matrix products, arithmetic and copies ran while one was open for 0% of the time, Pallas kernels for 0%

profile of v8, /device:TPU:64, one launch (start us, length us, event | category | flops | bytes accessed | tf_op | source)
XLA Modules:
  0.0 174.0 jit_solution(4366388393336142154)
XLA Ops:
  1.3 0.6 pad_add_fusion.scal
  1.8 0.0 copy-start.3
  1.8 3.8 %shard_map.77 = (bf16[1152,768]{1,0:T(8,128)(2,1)}, bf16[2,448,128]{2,1,0:T(8,128)(2,1)}, bf16[64,1536]{1,0:T(8,128)(2,1)}) custom-call(s32[4]{0:T(128)} %pad_add_fusion.scal, bf16[128,1536]{1,0:T(8,128)(2,1)} %bitcast.30, bf16[384,768]{1,0:T(8,128)(2,1)} %w_in.1, bf16[576,768]{1,0:T(8,128)(2,1)} %bitcast.40, bf16[192,768]{1,0:T(8,128)(2,1)} %bitcast.42), custom_call_target="tpu_custom_call" | custom-call | tf_op jit(solution)/shard_map/pallas_call | solution.py:190
  5.6 1.9 %collective-permute-start = (bf16[1152,768]{1,0:T(8,128)(2,1)}, bf16[1152,768]{1,0:T(8,128)(2,1)S(1)}, u32[]{:S(2)}, u32[]{:S(2)}) collective-permute-start(bf16[1152,768]{1,0:T(8,128)(2,1)} %get-tuple-element.12), channel_id=1, source_target_pairs={{0,1},{1,0},{2,3},{3,2},{4,5},{5,4},{6,7},{7,6},{8,9},{9,8},{10,11... | collective-permute-start | bytes 5308424 | tf_op jit(solution)/shard_map/ppermute | solution.py:275
  7.6 14.8 %all-to-all-start = ((bf16[16,56,128]{2,1,0:T(8,128)(2,1)}), bf16[16,56,128]{2,1,0:T(8,128)(2,1)S(1)}, u32[]{:S(2)}, u32[]{:S(2)}) async-start(bf16[16,56,128]{2,1,0:T(8,128)(2,1)} %bitcast.43), calls=%async_computation | async-start | bytes 458752 | tf_op jit(solution)/shard_map/all_to_all | solution.py:287
  22.3 3.4 %collective-permute-start.1 = (bf16[64,1536]{1,0:T(8,128)(2,1)}, bf16[64,1536]{1,0:T(8,128)(2,1)S(1)}, u32[]{:S(2)}, u32[]{:S(2)}) collective-permute-start(bf16[64,1536]{1,0:T(8,128)(2,1)} %get-tuple-element.13), channel_id=1, source_target_pairs={{0,4},{4,0},{8,12},{12,8},{16,20},{20,16},{24,28},{28,24},{1,5},{5... | collective-permute-start | bytes 589832 | tf_op jit(solution)/shard_map/ppermute | solution.py:289
  25.7 13.1 %collective-permute-done.1 = bf16[64,1536]{1,0:T(8,128)(2,1)S(1)} collective-permute-done((bf16[64,1536]{1,0:T(8,128)(2,1)}, bf16[64,1536]{1,0:T(8,128)(2,1)S(1)}, u32[]{:S(2)}, u32[]{:S(2)}) %collective-permute-start.1) | collective-permute-done | bytes 196640 | tf_op jit(solution)/shard_map/ppermute | solution.py:289
  38.8 0.0 all-to-all-done
  38.8 0.0 collective-permute-done
  38.8 0.0 copy-done.3
  38.8 1.2 shard_map.78
  39.9 48.4 %all_to_all.25.got = bf16[16,136,768]{2,1,0:T(8,128)(2,1)S(1)} all-to-all(bf16[16,136,768]{2,1,0:T(8,128)(2,1)S(1)} %shard_map.78), channel_id=1, replica_groups=mesh['y'=4,'x'=4,'zl'=8,'zh'=2,'core'=2] {'y','x'}, dimensions={0} | all-to-all | bytes 6684672 | tf_op jit(solution)/shard_map/all_to_all | solution.py:291
  88.4 0.0 copy-start
  88.4 0.0 copy-start.1
  88.4 0.1 slice.8
  88.5 2.1 %collective-permute-start.2 = (bf16[16,64,768]{2,1,0:T(8,128)(2,1)S(1)}, bf16[16,64,768]{2,1,0:T(8,128)(2,1)S(1)}, u32[]{:S(2)}, u32[]{:S(2)}) collective-permute-start(bf16[16,64,768]{2,1,0:T(8,128)(2,1)S(1)} %slice.8), channel_id=1, source_target_pairs={{0,1},{1,0},{2,3},{3,2},{4,5},{5,4},{6,7},{7,6},{8,9},{9,8},{10,11... | collective-permute-start | bytes 4718600 | tf_op jit(solution)/shard_map/ppermute | solution.py:275
  90.6 2.4 %collective-permute-start.3 = (bf16[128,768]{1,0:T(8,128)(2,1)S(1)}, bf16[128,768]{1,0:T(8,128)(2,1)S(1)}, u32[]{:S(2)}, u32[]{:S(2)}) collective-permute-start(bf16[128,768]{1,0:T(8,128)(2,1)S(1)} %get-tuple-element.20), channel_id=1, source_target_pairs={{0,1},{1,0},{2,3},{3,2},{4,5},{5,4},{6,7},{7,6},{8,9},{9,8},{10,11... | collective-permute-start | bytes 589832 | tf_op jit(solution)/shard_map/ppermute | solution.py:275
  93.0 1.2 collective-permute-done.3
  94.2 0.0 collective-permute-done.2.cross
  94.2 0.0 copy-done
  94.2 0.0 copy-done.1
  94.2 0.0 copy-done.2
  94.3 16.1 %shard_map.79 = (f32[128,768]{1,0:T(8,128)}, f32[16,2,24,384]{3,2,1,0:T(8,128)S(1)}, bf16[16,2,24,384]{3,2,1,0:T(8,128)(2,1)S(1)}) custom-call(s32[4]{0:T(128)S(1)} %copy-done.3, bf16[4,32,1536]{2,1,0:T(8,128)(2,1)S(1)} %bitcast.31, bf16[2,32,1536]{2,1,0:T(8,128)(2,1)S(1)} %bitcast.35, bf16[18,64,768]{2,1,0:T(8,128)(2,1)S(1)} %bitcast.28, ...), custom_call_target="tpu_custom_call" | custom-call | tf_op jit(solution)/shard_map/pallas_call | solution.py:248
  110.3 2.1 %collective-permute-start.4 = (bf16[16,2,24,384]{3,2,1,0:T(8,128)(2,1)S(1)}, bf16[16,2,24,384]{3,2,1,0:T(8,128)(2,1)S(1)}, u32[]{:S(2)}, u32[]{:S(2)}) collective-permute-start(bf16[16,2,24,384]{3,2,1,0:T(8,128)(2,1)S(1)} %get-tuple-element.19), channel_id=1, source_target_pairs={{0,1},{1,0},{2,3},{3,2},{4,5},{5,4},{6,7},{7,6},{8,9},{9,8},{10,11... | collective-permute-start | bytes 1769480 | tf_op jit(solution)/shard_map/ppermute | solution.py:275
  112.5 1.8 %collective-permute-done.4 = bf16[16,2,24,384]{3,2,1,0:T(8,128)(2,1)S(1)} collective-permute-done((bf16[16,2,24,384]{3,2,1,0:T(8,128)(2,1)S(1)}, bf16[16,2,24,384]{3,2,1,0:T(8,128)(2,1)S(1)}, u32[]{:S(2)}, u32[]{:S(2)}) %collective-permute-start.4) | collective-permute-done | bytes 589856 | tf_op jit(solution)/shard_map/ppermute | solution.py:275
  114.2 0.1 add_convert_fusion
  114.4 15.6 %all_to_all.26 = bf16[16,2,24,384]{3,2,1,0:T(8,128)(2,1)S(1)} all-to-all(bf16[16,2,24,384]{3,2,1,0:T(8,128)(2,1)S(1)} %add_convert_fusion), channel_id=1, replica_groups=mesh['y'=4,'x'=4,'zl'=8,'zh'=2,'core'=2] {'y','x'}, dimensions={0} | all-to-all | bytes 1179648 | tf_op jit(solution)/shard_map/all_to_all | solution.py:307
  130.0 0.1 reduce_sum.24
  130.1 30.2 %all_to_all.27 = bf16[16,24,384]{2,1,0:T(8,128)(2,1)S(1)} all-to-all(bf16[16,24,384]{2,1,0:T(8,128)(2,1)S(1)} %bitcast.39), channel_id=1, replica_groups=mesh['y'=4,'x'=4,'zl'=8,'zh'=2,'core'=2] {'zh','zl'}, dimensions={0} | all-to-all | bytes 589824 | tf_op jit(solution)/shard_map/all_to_all | solution.py:310
  160.4 12.4 %all_to_all.28 = bf16[16,24,384]{2,1,0:T(8,128)(2,1)S(1)} all-to-all(bf16[16,24,384]{2,1,0:T(8,128)(2,1)S(1)} %broadcast_in_dim.8), channel_id=1, replica_groups=mesh['y'=4,'x'=4,'zl'=8,'zh'=2,'core'=2] {'y','x'}, dimensions={0} | all-to-all | bytes 589824 | tf_op jit(solution)/shard_map/all_to_all | solution.py:269
  172.8 0.3 copy.9
  173.1 0.9 copy.10
  (6 shorter events, 0.2 us)
Async XLA Ops:
  1.8 36.9 %copy-start.3 = (s32[4]{0:T(128)S(1)}, s32[4]{0:T(128)}, u32[]{:S(2)}) copy-start(s32[4]{0:T(128)} %pad_add_fusion.scal) | copy-start | bytes 52
  5.6 33.1 %collective-permute-start = (bf16[1152,768]{1,0:T(8,128)(2,1)}, bf16[1152,768]{1,0:T(8,128)(2,1)S(1)}, u32[]{:S(2)}, u32[]{:S(2)}) collective-permute-start(bf16[1152,768]{1,0:T(8,128)(2,1)} %get-tuple-element.12), channel_id=1, source_target_pairs={{0,1},{1,0},{2,3},{3,2},{4,5},{5,4},{6,7},{7,6},{8,9},{9,8},{10,11... | collective-permute-start | bytes 5308424 | tf_op jit(solution)/shard_map/ppermute | solution.py:275
  7.6 31.2 %all-to-all-start = ((bf16[16,56,128]{2,1,0:T(8,128)(2,1)}), bf16[16,56,128]{2,1,0:T(8,128)(2,1)S(1)}, u32[]{:S(2)}, u32[]{:S(2)}) async-start(bf16[16,56,128]{2,1,0:T(8,128)(2,1)} %bitcast.43), calls=%async_computation | async-start | bytes 458752 | tf_op jit(solution)/shard_map/all_to_all | solution.py:287
  22.3 16.4 %collective-permute-start.1 = (bf16[64,1536]{1,0:T(8,128)(2,1)}, bf16[64,1536]{1,0:T(8,128)(2,1)S(1)}, u32[]{:S(2)}, u32[]{:S(2)}) collective-permute-start(bf16[64,1536]{1,0:T(8,128)(2,1)} %get-tuple-element.13), channel_id=1, source_target_pairs={{0,4},{4,0},{8,12},{12,8},{16,20},{20,16},{24,28},{28,24},{1,5},{5... | collective-permute-start | bytes 589832 | tf_op jit(solution)/shard_map/ppermute | solution.py:289
  88.4 5.9 %copy-start = (bf16[1152,768]{1,0:T(8,128)(2,1)S(1)}, bf16[1152,768]{1,0:T(8,128)(2,1)}, u32[]{:S(2)}) copy-start(bf16[1152,768]{1,0:T(8,128)(2,1)} %get-tuple-element.12) | copy-start | bytes 5308420
  88.4 5.9 %copy-start.1 = (bf16[1,128,1536]{2,1,0:T(8,128)(2,1)S(1)}, bf16[1,128,1536]{2,1,0:T(8,128)(2,1)}, u32[]{:S(2)}) copy-start(bf16[1,128,1536]{2,1,0:T(8,128)(2,1)} %param.6) | copy-start | bytes 1179652
  88.4 5.9 %copy-start.2 = (bf16[1,128,768]{2,1,0:T(8,128)(2,1)S(1)}, bf16[1,128,768]{2,1,0:T(8,128)(2,1)}, u32[]{:S(2)}) copy-start(bf16[1,128,768]{2,1,0:T(8,128)(2,1)} %param.11) | copy-start | bytes 589828
  88.5 5.7 %collective-permute-start.2 = (bf16[16,64,768]{2,1,0:T(8,128)(2,1)S(1)}, bf16[16,64,768]{2,1,0:T(8,128)(2,1)S(1)}, u32[]{:S(2)}, u32[]{:S(2)}) collective-permute-start(bf16[16,64,768]{2,1,0:T(8,128)(2,1)S(1)} %slice.8), channel_id=1, source_target_pairs={{0,1},{1,0},{2,3},{3,2},{4,5},{5,4},{6,7},{7,6},{8,9},{9,8},{10,11... | collective-permute-start | bytes 4718600 | tf_op jit(solution)/shard_map/ppermute | solution.py:275
  90.6 3.6 %collective-permute-start.3 = (bf16[128,768]{1,0:T(8,128)(2,1)S(1)}, bf16[128,768]{1,0:T(8,128)(2,1)S(1)}, u32[]{:S(2)}, u32[]{:S(2)}) collective-permute-start(bf16[128,768]{1,0:T(8,128)(2,1)S(1)} %get-tuple-element.20), channel_id=1, source_target_pairs={{0,1},{1,0},{2,3},{3,2},{4,5},{5,4},{6,7},{7,6},{8,9},{9,8},{10,11... | collective-permute-start | bytes 589832 | tf_op jit(solution)/shard_map/ppermute | solution.py:275
  110.3 3.9 %collective-permute-start.4 = (bf16[16,2,24,384]{3,2,1,0:T(8,128)(2,1)S(1)}, bf16[16,2,24,384]{3,2,1,0:T(8,128)(2,1)S(1)}, u32[]{:S(2)}, u32[]{:S(2)}) collective-permute-start(bf16[16,2,24,384]{3,2,1,0:T(8,128)(2,1)S(1)} %get-tuple-element.19), channel_id=1, source_target_pairs={{0,1},{1,0},{2,3},{3,2},{4,5},{5,4},{6,7},{7,6},{8,9},{9,8},{10,11... | collective-permute-start | bytes 1769480 | tf_op jit(solution)/shard_map/ppermute | solution.py:275

commit v9 on v8

--- a/solution.py
+++ b/solution.py
@@ -35,10 +35,53 @@
     return jnp.where(dot(pick, block[:, :TOK], NT)[0:1] > MARK / 2, F32(LOW), F32(0))
 
 
+def begin_kernel(scal, rows, partner, own, mate, got, partial, last, bias, given, win, sems):
+    count, zh, core = scal[0], scal[1], scal[2]
+    moves = [
+        (own.at[pl.ds(0, 6)], win.at[0]),
+        (mate.at[pl.ds(0, 6)], win.at[1]),
+        (got.at[pl.ds(0, 6), pl.ds(0, 64)], win.at[2]),
+        (rows, given.at[pl.ds(0, 4)]),
+        (partner, given.at[pl.ds(4, 2)]),
+        (got.at[:, pl.ds(64, 32)], given.at[pl.ds(8, 16), :, pl.ds(0, WIDTH)]),
+        (got.at[:, pl.ds(96, 32)], given.at[pl.ds(8, 16), :, pl.ds(WIDTH, WIDTH)]),
+    ]
+    copies = [pltpu.make_async_copy(s, d, sems.at[i]) for i, (s, d) in enumerate(moves)]
+    for c in copies:
+        c.start()
+    given[pl.ds(6, 2)] = jnp.zeros((2, 32, TILE), BF)
+    for c in copies:
+        c.wait()
+
+    def columns(shard):
+        start = pl.multiple_of(shard * 384, 384)
+        return given[:, :, pl.ds(start, 384)].reshape(WIDTH, 384)
+
+    shards_here = (zh * 2 + core, zh * 2 + 1 - core, (1 - zh) * 2 + core)
+    parts = [
+        dot(columns(s), win[i].reshape(384, WIDTH), NN) for i, s in enumerate(shards_here)
+    ]
+    partial[...] = parts[0] + parts[1] + parts[2]
+    last[...] = columns((1 - zh) * 2 + 1 - core)
+    lane = lax.broadcasted_iota(jnp.int32, (1, TOK), 1)
+    twice = jnp.where(lane & 1 == 0, F32(1), F32(0))
+    keys = given.reshape(WIDTH, TILE)
+    bias[...] = jnp.concatenate(
+        [
+            jnp.where(lane < count, twice, F32(LOW)),
+            key_bias(keys[pl.ds(TOK, 64), :]),
+            jnp.full((1, 64), LOW, F32),
+            key_bias(keys[pl.ds(256, FAR), :]),
+        ],
+        axis=1,
+    )
+
+
 def layer_kernel(
     scal,
-    rows,
-    partner,
+    partial,
+    last,
+    key_bias_row,
     own,
     mate,
     got,
@@ -49,7 +92,6 @@
     out,
     keep,
     send,
-    given,
     win,
     wqkv,
     wout,
@@ -63,14 +105,7 @@
     over, over_other = (1 - zh) * 2 + core, (1 - zh) * 2 + 1 - core
     arrived = got.at[:, pl.ds(0, 64)]
     moves = [
-        (own.at[pl.ds(0, 6)], win.at[mine]),
-        (mate.at[pl.ds(0, 6)], win.at[other]),
-        (arrived.at[pl.ds(0, 6)], win.at[over]),
-        (cross.at[pl.ds(0, 6)], win.at[over_other]),
-        (rows, given.at[pl.ds(0, 4)]),
-        (partner, given.at[pl.ds(4, 2)]),
-        (got.at[:, pl.ds(64, 32)], given.at[pl.ds(8, 16), :, pl.ds(0, WIDTH)]),
-        (got.at[:, pl.ds(96, 32)], given.at[pl.ds(8, 16), :, pl.ds(WIDTH, WIDTH)]),
+        (cross.at[pl.ds(0, 6)], win),
         (own.at[pl.ds(6, 9)], wqkv.at[mine]),
         (mate.at[pl.ds(6, 9)], wqkv.at[other]),
         (arrived.at[pl.ds(6, 9)], wqkv.at[over]),
@@ -85,23 +120,11 @@
     copies = [pltpu.make_async_copy(s, d, sems.at[i]) for i, (s, d) in enumerate(moves)]
     for c in copies:
         c.start()
-    given[pl.ds(6, 2)] = jnp.zeros((2, 32, TILE), BF)
-    lane = lax.broadcasted_iota(jnp.int32, (1, TOK), 1)
-    twice = jnp.where(lane & 1 == 0, F32(1), F32(0))
-    for c in copies[:8]:
-        c.wait()
-    keys = given.reshape(WIDTH, TILE)
-    hid[...] = dot(keys[...], win.reshape(TILE, WIDTH)[...], NN).astype(BF)
-    bias = jnp.concatenate(
-        [
-            jnp.where(lane < count, twice, F32(LOW)),
-            key_bias(keys[pl.ds(TOK, 64), :]),
-            jnp.full((1, 64), LOW, F32),
-            key_bias(keys[pl.ds(256, FAR), :]),
-        ],
-        axis=1,
-    )
-    for c in copies[8:12]:
+    copies[0].wait()
+    fourth = dot(last[...], win[...].reshape(384, WIDTH), NN)
+    hid[...] = (partial[...] + fourth).astype(BF)
+    bias = key_bias_row[...]
+    for c in copies[1:5]:
         c.wait()
     flat = wqkv.reshape(3 * WIDTH, WIDTH)
     kv[...] = dot(flat[pl.ds(WIDTH, 2 * WIDTH), :], hid[...], NT).astype(BF)
@@ -126,7 +149,7 @@
                     target[r * 2 + c, half] = part[r * 24 : r * 24 + 24, c * 384 : c * 384 + 384].astype(
                         target.dtype
                     )
-    for c in copies[12:]:
+    for c in copies[5:]:
         c.wait()
     out[...] = dot(wout.reshape(WIDTH, WIDTH)[...], attn[...], NN).T
 
@@ -140,7 +163,7 @@
     return pltpu.CompilerParams(vmem_limit_bytes=mebibytes * 1024 * 1024)
 
 
-def prepare_kernel(scal, rows, w_in, w_qkv, w_out, own, ahead, even, sems):
+def prepare_kernel(scal, rows, w_in, w_qkv, w_out, pack, ahead, even, own, sems):
     count, zh, at = scal[0], scal[1], scal[3]
     moves = [
         (w_in, own.at[pl.ds(0, 384)]),
@@ -168,6 +191,8 @@
     even[...] = (dot(pick, rows[...], NN) + marks).astype(BF)
     for c in copies:
         c.wait()
+    back = pltpu.make_async_copy(own, pack, sems.at[3])
+    back.start()
     start = pl.multiple_of(at // 16 * 16, 16)
     wide = own[pl.ds(start, 16), :].astype(F32)
     eight = jnp.where(at > start, wide[8:16], wide[0:8])
@@ -184,6 +209,7 @@
         more = [ninth[:, c * TOK : (c + 1) * TOK] for c in range(6)]
         block = jnp.concatenate(lanes + [jnp.concatenate(more + [spare], axis=0)], axis=0)
         ahead[half] = jnp.concatenate([block] * 8, axis=0).astype(BF)
+    back.wait()
 
 
 def prepare_call(*operands, interpret=False):
@@ -195,8 +221,8 @@
             jax.ShapeDtypeStruct((TOK // 2, TILE), BF),
         ),
         in_specs=[SMEM, VMEM] + [ANY] * 3,
-        out_specs=(VMEM,) * 3,
-        scratch_shapes=[pltpu.SemaphoreType.DMA((3,))],
+        out_specs=(ANY, VMEM, VMEM),
+        scratch_shapes=[pltpu.VMEM((PACK, WIDTH), BF), pltpu.SemaphoreType.DMA((4,))],
         compiler_params=room(62),
         interpret=interpret,
     )(*operands)
@@ -242,23 +268,42 @@
     )(*operands)
 
 
+def begin_call(*operands, interpret=False):
+    return pl.pallas_call(
+        begin_kernel,
+        out_shape=(
+            jax.ShapeDtypeStruct((WIDTH, WIDTH), F32),
+            jax.ShapeDtypeStruct((WIDTH, 384), BF),
+            jax.ShapeDtypeStruct((1, WIDTH), F32),
+        ),
+        in_specs=[SMEM] + [ANY] * 5,
+        out_specs=(VMEM,) * 3,
+        scratch_shapes=[
+            pltpu.VMEM((24, 32, TILE), BF),
+            pltpu.VMEM((3, 6, 64, WIDTH), BF),
+            pltpu.SemaphoreType.DMA((7,)),
+        ],
+        compiler_params=room(32),
+        interpret=interpret,
+    )(*operands)
+
+
 def layer_call(*operands, interpret=False):
     part = jax.ShapeDtypeStruct((16, 2, 24, 384), F32)
     sent = jax.ShapeDtypeStruct((16, 2, 24, 384), BF)
     return pl.pallas_call(
         layer_kernel,
         out_shape=(jax.ShapeDtypeStruct((TOK, WIDTH), F32), part, sent),
-        in_specs=[SMEM] + [ANY] * 8 + [VMEM],
+        in_specs=[SMEM] + [VMEM] * 3 + [ANY] * 6 + [VMEM],
         out_specs=(VMEM,) * 3,
         scratch_shapes=[
-            pltpu.VMEM((24, 32, TILE), BF),
-            pltpu.VMEM((4, 6, 64, WIDTH), BF),
+            pltpu.VMEM((6, 64, WIDTH), BF),
             pltpu.VMEM((4, 9, 64, WIDTH), BF),
             pltpu.VMEM((4, 3, 64, WIDTH), BF),
             pltpu.VMEM((WIDTH, WIDTH), BF),
             pltpu.VMEM((2 * WIDTH, WIDTH), BF),
             pltpu.VMEM((WIDTH, TOK), BF),
-            pltpu.SemaphoreType.DMA((18,)),
+            pltpu.SemaphoreType.DMA((11,)),
         ],
         compiler_params=room(40),
         interpret=interpret,
@@ -291,17 +336,13 @@
     got = lax.all_to_all(split_call(scal, line), YX, 0, 0, tiled=True)
     over_rest = got[:, 128:].reshape(128, WIDTH)
     cross, cross_rest = swap(got[:, :64], "core"), swap(over_rest, "core")
+    own, mate = own.reshape(18, 64, WIDTH), mate.reshape(18, 64, WIDTH)
+    state = begin_call(
+        scal, rows.reshape(4, 32, TILE), partner.reshape(2, 32, TILE), own, mate, got
+    )
+    over_rest, cross_rest = over_rest.reshape(2, 64, WIDTH), cross_rest.reshape(2, 64, WIDTH)
     out, keep, send = layer_call(
-        scal,
-        rows.reshape(4, 32, TILE),
-        partner.reshape(2, 32, TILE),
-        own.reshape(18, 64, WIDTH),
-        mate.reshape(18, 64, WIDTH),
-        got,
-        cross,
-        over_rest.reshape(2, 64, WIDTH),
-        cross_rest.reshape(2, 64, WIDTH),
-        cotangent[0],
+        scal, *state, own, mate, got, cross, over_rest, cross_rest, cotangent[0]
     )
     pair = (keep + swap(send, "core").astype(F32)).astype(BF)
     plane = lax.all_to_all(pair, YX, 0, 0, tiled=True)

time: 175 us -> 175 us (level)
  Pallas kernels: 21 us -> 22.8 us
    pallas_call x0 -> x1, Pallas kernels: none -> 3.53 us  [begin_call(): pl.pallas_call(begin_kernel, out_shape=(jax.ShapeDtypeStruct((WIDTH, WIDT...]
    pallas_call x1, Pallas kernels: 16.1 us -> 13.7 us  [layer_call(): pl.pallas_call(layer_kernel, out_shape=(jax.ShapeDtypeStruct((TOK, WIDTH)...]
  transfers between devices with their start and end apart: 6 -> 6, of which waited for: 3 -> 2; matrix products, arithmetic and copies ran while one was open for 0% -> 0% of each run, Pallas kernels for 0% -> 2%
where the time goes in v9:
time: 175 us
  blocking collectives  107 us (61%)
  starting transfers between devices  26.4 us (15%)
  Pallas kernels  22.8 us (13%)
  waiting for transfers between devices  15 us (9%)
    all_to_all x1, blocking collectives, shards(): got = lax.all_to_all(split_call(scal, line), YX, 0, 0, tiled=True)  48.4 us
    all_to_all x1, blocking collectives, shards(): column = lax.all_to_all(column, Z, 0, 0, tiled=True)  30.2 us
    all_to_all x1, blocking collectives, shards(): plane = lax.all_to_all(pair, YX, 0, 0, tiled=True)  15.6 us
    all_to_all x1, starting transfers between devices, shards(): line = lax.all_to_all(ahead.reshape(16, 56, TOK), Z, 0, 0, tiled=True)  14.8 us
    pallas_call x1, Pallas kernels, layer_call(): pl.pallas_call(layer_kernel, out_shape=(jax.ShapeDtypeStruct((TOK, WIDTH)...  13.7 us
    ppermute x1, waiting for transfers between devices, shards(): partner = lax.ppermute(even, 'zl', [(i, i ^ 1) for i in range(8)])  13.1 us
    all_to_all x1, blocking collectives, spread(): lax.all_to_all(jnp.broadcast_to(block[None], (size,) + block.shape), axes...  12.3 us
    ppermute x4, starting transfers between devices, swap(): return lax.ppermute(value, axis, [(0, 1), (1, 0)])  8.3 us
  transfers between devices with their start and end apart: 6, of which 2 were waited for; matrix products, arithmetic and copies ran while one was open for 0% of the time, Pallas kernels for 2%

profile of v9, /device:TPU:64, one launch (start us, length us, event | category | flops | bytes accessed | tf_op | source)
XLA Modules:
  0.0 174.5 jit_solution(1577438486865142099)
XLA Ops:
  1.3 0.6 pad_add_fusion.scal
  1.9 0.0 copy-start.3
  1.9 4.4 %shard_map.77 = (bf16[1152,768]{1,0:T(8,128)(2,1)}, bf16[2,448,128]{2,1,0:T(8,128)(2,1)}, bf16[64,1536]{1,0:T(8,128)(2,1)}) custom-call(s32[4]{0:T(128)} %pad_add_fusion.scal, bf16[128,1536]{1,0:T(8,128)(2,1)} %bitcast.32, bf16[384,768]{1,0:T(8,128)(2,1)} %w_in.1, bf16[576,768]{1,0:T(8,128)(2,1)} %bitcast.42, bf16[192,768]{1,0:T(8,128)(2,1)} %bitcast.44), custom_call_target="tpu_custom_call" | custom-call | tf_op jit(solution)/shard_map/pallas_call | solution.py:216
  6.3 1.9 %collective-permute-start = (bf16[1152,768]{1,0:T(8,128)(2,1)}, bf16[1152,768]{1,0:T(8,128)(2,1)S(1)}, u32[]{:S(2)}, u32[]{:S(2)}) collective-permute-start(bf16[1152,768]{1,0:T(8,128)(2,1)} %get-tuple-element.15), channel_id=1, source_target_pairs={{0,1},{1,0},{2,3},{3,2},{4,5},{5,4},{6,7},{7,6},{8,9},{9,8},{10,11... | collective-permute-start | bytes 5308424 | tf_op jit(solution)/shard_map/ppermute | solution.py:320
  8.3 14.8 %all-to-all-start = ((bf16[16,56,128]{2,1,0:T(8,128)(2,1)}), bf16[16,56,128]{2,1,0:T(8,128)(2,1)S(1)}, u32[]{:S(2)}, u32[]{:S(2)}) async-start(bf16[16,56,128]{2,1,0:T(8,128)(2,1)} %bitcast.45), calls=%async_computation | async-start | bytes 458752 | tf_op jit(solution)/shard_map/all_to_all | solution.py:332
  23.0 3.4 %collective-permute-start.1 = (bf16[64,1536]{1,0:T(8,128)(2,1)}, bf16[64,1536]{1,0:T(8,128)(2,1)S(1)}, u32[]{:S(2)}, u32[]{:S(2)}) collective-permute-start(bf16[64,1536]{1,0:T(8,128)(2,1)} %get-tuple-element.16), channel_id=1, source_target_pairs={{0,4},{4,0},{8,12},{12,8},{16,20},{20,16},{24,28},{28,24},{1,5},{5... | collective-permute-start | bytes 589832 | tf_op jit(solution)/shard_map/ppermute | solution.py:334
  26.4 13.1 %collective-permute-done.1 = bf16[64,1536]{1,0:T(8,128)(2,1)S(1)} collective-permute-done((bf16[64,1536]{1,0:T(8,128)(2,1)}, bf16[64,1536]{1,0:T(8,128)(2,1)S(1)}, u32[]{:S(2)}, u32[]{:S(2)}) %collective-permute-start.1) | collective-permute-done | bytes 196640 | tf_op jit(solution)/shard_map/ppermute | solution.py:334
  39.4 0.0 all-to-all-done
  39.4 0.0 collective-permute-done
  39.4 0.0 copy-done.3
  39.5 1.2 shard_map.78
  40.6 48.4 %all_to_all.25.got = bf16[16,136,768]{2,1,0:T(8,128)(2,1)S(1)} all-to-all(bf16[16,136,768]{2,1,0:T(8,128)(2,1)S(1)} %shard_map.78), channel_id=1, replica_groups=mesh['y'=4,'x'=4,'zl'=8,'zh'=2,'core'=2] {'y','x'}, dimensions={0} | all-to-all | bytes 6684672 | tf_op jit(solution)/shard_map/all_to_all | solution.py:336
  89.0 0.1 slice.8
  89.2 2.1 %collective-permute-start.2 = (bf16[16,64,768]{2,1,0:T(8,128)(2,1)S(1)}, bf16[16,64,768]{2,1,0:T(8,128)(2,1)S(1)}, u32[]{:S(2)}, u32[]{:S(2)}) collective-permute-start(bf16[16,64,768]{2,1,0:T(8,128)(2,1)S(1)} %slice.8), channel_id=1, source_target_pairs={{0,1},{1,0},{2,3},{3,2},{4,5},{5,4},{6,7},{7,6},{8,9},{9,8},{10,11... | collective-permute-start | bytes 4718600 | tf_op jit(solution)/shard_map/ppermute | solution.py:320
  91.3 2.4 %collective-permute-start.3 = (bf16[128,768]{1,0:T(8,128)(2,1)S(1)}, bf16[128,768]{1,0:T(8,128)(2,1)S(1)}, u32[]{:S(2)}, u32[]{:S(2)}) collective-permute-start(bf16[128,768]{1,0:T(8,128)(2,1)S(1)} %get-tuple-element.26), channel_id=1, source_target_pairs={{0,1},{1,0},{2,3},{3,2},{4,5},{5,4},{6,7},{7,6},{8,9},{9,8},{10,11... | collective-permute-start | bytes 589832 | tf_op jit(solution)/shard_map/ppermute | solution.py:320
  93.7 0.0 copy-done
  93.7 0.0 copy-done.1
  93.7 0.0 copy-start.2
  93.7 3.5 %shard_map.79 = (f32[768,768]{1,0:T(8,128)S(1)}, bf16[768,384]{1,0:T(8,128)(2,1)S(1)}, f32[1,768]{1,0:T(1,128)S(1)}) custom-call(s32[4]{0:T(128)S(1)} %copy-done.3, bf16[4,32,1536]{2,1,0:T(8,128)(2,1)S(1)} %bitcast.33, bf16[2,32,1536]{2,1,0:T(8,128)(2,1)S(1)} %bitcast.38, bf16[18,64,768]{2,1,0:T(8,128)(2,1)S(1)} %bitcast.28, ...), custom_call_target="tpu_custom_call" | custom-call | tf_op jit(solution)/shard_map/pallas_call | solution.py:272
  97.3 0.0 collective-permute-done.3
  97.3 0.0 collective-permute-done.2.cross
  97.3 0.0 copy-done.2
  97.3 13.7 %shard_map.80 = (f32[128,768]{1,0:T(8,128)}, f32[16,2,24,384]{3,2,1,0:T(8,128)S(1)}, bf16[16,2,24,384]{3,2,1,0:T(8,128)(2,1)S(1)}) custom-call(s32[4]{0:T(128)S(1)} %copy-done.3, f32[768,768]{1,0:T(8,128)S(1)} %get-tuple-element.20.partial, bf16[768,384]{1,0:T(8,128)(2,1)S(1)} %get-tuple-element.21.last, f32[1,768]{1,0:T(1,128)S(1)} %get-tuple-element.22.key_bias_row, ...), custom_call_target="tpu_custom_call" | custom-call | tf_op jit(solution)/shard_map/pallas_call | solution.py:294
  111.0 1.9 %collective-permute-start.4 = (bf16[16,2,24,384]{3,2,1,0:T(8,128)(2,1)S(1)}, bf16[16,2,24,384]{3,2,1,0:T(8,128)(2,1)S(1)}, u32[]{:S(2)}, u32[]{:S(2)}) collective-permute-start(bf16[16,2,24,384]{3,2,1,0:T(8,128)(2,1)S(1)} %get-tuple-element.25), channel_id=1, source_target_pairs={{0,1},{1,0},{2,3},{3,2},{4,5},{5,4},{6,7},{7,6},{8,9},{9,8},{10,11... | collective-permute-start | bytes 1769480 | tf_op jit(solution)/shard_map/ppermute | solution.py:320
  112.9 2.0 %collective-permute-done.4 = bf16[16,2,24,384]{3,2,1,0:T(8,128)(2,1)S(1)} collective-permute-done((bf16[16,2,24,384]{3,2,1,0:T(8,128)(2,1)S(1)}, bf16[16,2,24,384]{3,2,1,0:T(8,128)(2,1)S(1)}, u32[]{:S(2)}, u32[]{:S(2)}) %collective-permute-start.4) | collective-permute-done | bytes 589856 | tf_op jit(solution)/shard_map/ppermute | solution.py:320
  114.9 0.1 add_convert_fusion
  115.0 15.6 %all_to_all.26 = bf16[16,2,24,384]{3,2,1,0:T(8,128)(2,1)S(1)} all-to-all(bf16[16,2,24,384]{3,2,1,0:T(8,128)(2,1)S(1)} %add_convert_fusion), channel_id=1, replica_groups=mesh['y'=4,'x'=4,'zl'=8,'zh'=2,'core'=2] {'y','x'}, dimensions={0} | all-to-all | bytes 1179648 | tf_op jit(solution)/shard_map/all_to_all | solution.py:348
  130.6 0.1 reduce_sum.24
  130.7 30.2 %all_to_all.27 = bf16[16,24,384]{2,1,0:T(8,128)(2,1)S(1)} all-to-all(bf16[16,24,384]{2,1,0:T(8,128)(2,1)S(1)} %bitcast.41), channel_id=1, replica_groups=mesh['y'=4,'x'=4,'zl'=8,'zh'=2,'core'=2] {'zh','zl'}, dimensions={0} | all-to-all | bytes 589824 | tf_op jit(solution)/shard_map/all_to_all | solution.py:351
  161.0 12.3 %all_to_all.28 = bf16[16,24,384]{2,1,0:T(8,128)(2,1)S(1)} all-to-all(bf16[16,24,384]{2,1,0:T(8,128)(2,1)S(1)} %broadcast_in_dim.8), channel_id=1, replica_groups=mesh['y'=4,'x'=4,'zl'=8,'zh'=2,'core'=2] {'y','x'}, dimensions={0} | all-to-all | bytes 589824 | tf_op jit(solution)/shard_map/all_to_all | solution.py:314
  173.4 0.3 copy.9
  173.7 0.9 copy.10
  (7 shorter events, 0.2 us)
Async XLA Ops:
  1.9 37.6 %copy-start.3 = (s32[4]{0:T(128)S(1)}, s32[4]{0:T(128)}, u32[]{:S(2)}) copy-start(s32[4]{0:T(128)} %pad_add_fusion.scal) | copy-start | bytes 52
  6.3 33.1 %collective-permute-start = (bf16[1152,768]{1,0:T(8,128)(2,1)}, bf16[1152,768]{1,0:T(8,128)(2,1)S(1)}, u32[]{:S(2)}, u32[]{:S(2)}) collective-permute-start(bf16[1152,768]{1,0:T(8,128)(2,1)} %get-tuple-element.15), channel_id=1, source_target_pairs={{0,1},{1,0},{2,3},{3,2},{4,5},{5,4},{6,7},{7,6},{8,9},{9,8},{10,11... | collective-permute-start | bytes 5308424 | tf_op jit(solution)/shard_map/ppermute | solution.py:320
  8.3 31.2 %all-to-all-start = ((bf16[16,56,128]{2,1,0:T(8,128)(2,1)}), bf16[16,56,128]{2,1,0:T(8,128)(2,1)S(1)}, u32[]{:S(2)}, u32[]{:S(2)}) async-start(bf16[16,56,128]{2,1,0:T(8,128)(2,1)} %bitcast.45), calls=%async_computation | async-start | bytes 458752 | tf_op jit(solution)/shard_map/all_to_all | solution.py:332
  23.0 16.4 %collective-permute-start.1 = (bf16[64,1536]{1,0:T(8,128)(2,1)}, bf16[64,1536]{1,0:T(8,128)(2,1)S(1)}, u32[]{:S(2)}, u32[]{:S(2)}) collective-permute-start(bf16[64,1536]{1,0:T(8,128)(2,1)} %get-tuple-element.16), channel_id=1, source_target_pairs={{0,4},{4,0},{8,12},{12,8},{16,20},{20,16},{24,28},{28,24},{1,5},{5... | collective-permute-start | bytes 589832 | tf_op jit(solution)/shard_map/ppermute | solution.py:334
  89.0 4.7 %copy-start = (bf16[1152,768]{1,0:T(8,128)(2,1)S(1)}, bf16[1152,768]{1,0:T(8,128)(2,1)}, u32[]{:S(2)}) copy-start(bf16[1152,768]{1,0:T(8,128)(2,1)} %get-tuple-element.15) | copy-start | bytes 5308420
  89.0 4.7 %copy-start.1 = (bf16[1,128,1536]{2,1,0:T(8,128)(2,1)S(1)}, bf16[1,128,1536]{2,1,0:T(8,128)(2,1)}, u32[]{:S(2)}) copy-start(bf16[1,128,1536]{2,1,0:T(8,128)(2,1)} %param.6) | copy-start | bytes 1179652
  89.2 8.1 %collective-permute-start.2 = (bf16[16,64,768]{2,1,0:T(8,128)(2,1)S(1)}, bf16[16,64,768]{2,1,0:T(8,128)(2,1)S(1)}, u32[]{:S(2)}, u32[]{:S(2)}) collective-permute-start(bf16[16,64,768]{2,1,0:T(8,128)(2,1)S(1)} %slice.8), channel_id=1, source_target_pairs={{0,1},{1,0},{2,3},{3,2},{4,5},{5,4},{6,7},{7,6},{8,9},{9,8},{10,11... | collective-permute-start | bytes 4718600 | tf_op jit(solution)/shard_map/ppermute | solution.py:320
  91.3 6.0 %collective-permute-start.3 = (bf16[128,768]{1,0:T(8,128)(2,1)S(1)}, bf16[128,768]{1,0:T(8,128)(2,1)S(1)}, u32[]{:S(2)}, u32[]{:S(2)}) collective-permute-start(bf16[128,768]{1,0:T(8,128)(2,1)S(1)} %get-tuple-element.26), channel_id=1, source_target_pairs={{0,1},{1,0},{2,3},{3,2},{4,5},{5,4},{6,7},{7,6},{8,9},{9,8},{10,11... | collective-permute-start | bytes 589832 | tf_op jit(solution)/shard_map/ppermute | solution.py:320
  93.7 3.6 %copy-start.2 = (bf16[1,128,768]{2,1,0:T(8,128)(2,1)S(1)}, bf16[1,128,768]{2,1,0:T(8,128)(2,1)}, u32[]{:S(2)}) copy-start(bf16[1,128,768]{2,1,0:T(8,128)(2,1)} %param.11) | copy-start | bytes 589828
  111.0 3.9 %collective-permute-start.4 = (bf16[16,2,24,384]{3,2,1,0:T(8,128)(2,1)S(1)}, bf16[16,2,24,384]{3,2,1,0:T(8,128)(2,1)S(1)}, u32[]{:S(2)}, u32[]{:S(2)}) collective-permute-start(bf16[16,2,24,384]{3,2,1,0:T(8,128)(2,1)S(1)} %get-tuple-element.25), channel_id=1, source_target_pairs={{0,1},{1,0},{2,3},{3,2},{4,5},{5,4},{6,7},{7,6},{8,9},{9,8},{10,11... | collective-permute-start | bytes 1769480 | tf_op jit(solution)/shard_map/ppermute | solution.py:320

commit v10 on v9

--- a/solution.py
+++ b/solution.py
@@ -35,16 +35,16 @@
     return jnp.where(dot(pick, block[:, :TOK], NT)[0:1] > MARK / 2, F32(LOW), F32(0))
 
 
-def begin_kernel(scal, rows, partner, own, mate, got, partial, last, bias, given, win, sems):
+def begin_kernel(scal, rows, partner, own, mate, over, far, partial, last, bias, given, win, sems):
     count, zh, core = scal[0], scal[1], scal[2]
     moves = [
         (own.at[pl.ds(0, 6)], win.at[0]),
         (mate.at[pl.ds(0, 6)], win.at[1]),
-        (got.at[pl.ds(0, 6), pl.ds(0, 64)], win.at[2]),
+        (over.at[pl.ds(0, 6)], win.at[2]),
         (rows, given.at[pl.ds(0, 4)]),
         (partner, given.at[pl.ds(4, 2)]),
-        (got.at[:, pl.ds(64, 32)], given.at[pl.ds(8, 16), :, pl.ds(0, WIDTH)]),
-        (got.at[:, pl.ds(96, 32)], given.at[pl.ds(8, 16), :, pl.ds(WIDTH, WIDTH)]),
+        (far.at[:, pl.ds(0, 32)], given.at[pl.ds(8, 16), :, pl.ds(0, WIDTH)]),
+        (far.at[:, pl.ds(32, 32)], given.at[pl.ds(8, 16), :, pl.ds(WIDTH, WIDTH)]),
     ]
     copies = [pltpu.make_async_copy(s, d, sems.at[i]) for i, (s, d) in enumerate(moves)]
     for c in copies:
@@ -84,10 +84,8 @@
     key_bias_row,
     own,
     mate,
-    got,
+    over,
     cross,
-    over_rest,
-    cross_rest,
     cot,
     out,
     keep,
@@ -101,22 +99,11 @@
     sems,
 ):
     count, zh, core = scal[0], scal[1], scal[2]
-    mine, other = zh * 2 + core, zh * 2 + 1 - core
-    over, over_other = (1 - zh) * 2 + core, (1 - zh) * 2 + 1 - core
-    arrived = got.at[:, pl.ds(0, 64)]
-    moves = [
-        (cross.at[pl.ds(0, 6)], win),
-        (own.at[pl.ds(6, 9)], wqkv.at[mine]),
-        (mate.at[pl.ds(6, 9)], wqkv.at[other]),
-        (arrived.at[pl.ds(6, 9)], wqkv.at[over]),
-        (cross.at[pl.ds(6, 9)], wqkv.at[over_other]),
-        (own.at[pl.ds(15, 3)], wout.at[mine]),
-        (mate.at[pl.ds(15, 3)], wout.at[other]),
-        (arrived.at[15], wout.at[over, 0]),
-        (cross.at[15], wout.at[over_other, 0]),
-        (over_rest, wout.at[over, pl.ds(1, 2)]),
-        (cross_rest, wout.at[over_other, pl.ds(1, 2)]),
-    ]
+    places = (zh * 2 + core, zh * 2 + 1 - core, (1 - zh) * 2 + core, (1 - zh) * 2 + 1 - core)
+    packs = (own, mate, over, cross)
+    moves = [(cross.at[pl.ds(0, 6)], win)]
+    moves += [(p.at[pl.ds(6, 9)], wqkv.at[s]) for p, s in zip(packs, places)]
+    moves += [(p.at[pl.ds(15, 3)], wout.at[s]) for p, s in zip(packs, places)]
     copies = [pltpu.make_async_copy(s, d, sems.at[i]) for i, (s, d) in enumerate(moves)]
     for c in copies:
         c.start()
@@ -163,8 +150,8 @@
     return pltpu.CompilerParams(vmem_limit_bytes=mebibytes * 1024 * 1024)
 
 
-def prepare_kernel(scal, rows, w_in, w_qkv, w_out, pack, ahead, even, own, sems):
-    count, zh, at = scal[0], scal[1], scal[3]
+def prepare_kernel(scal, rows, w_in, w_qkv, w_out, own, ahead, even, sems):
+    count, zh, at, line = scal[0], scal[1], scal[3], scal[4]
     moves = [
         (w_in, own.at[pl.ds(0, 384)]),
         (w_qkv, own.at[pl.ds(384, 576)]),
@@ -191,12 +178,9 @@
     even[...] = (dot(pick, rows[...], NN) + marks).astype(BF)
     for c in copies:
         c.wait()
-    back = pltpu.make_async_copy(own, pack, sems.at[3])
-    back.start()
     start = pl.multiple_of(at // 16 * 16, 16)
     wide = own[pl.ds(start, 16), :].astype(F32)
     eight = jnp.where(at > start, wide[8:16], wide[0:8])
-    line = 1024 + at // 64 * 8 + at // 8 % 8
     start = pl.multiple_of(line // 16 * 16, 16)
     wide = own[pl.ds(start, 16), :].astype(F32)
     single = lax.broadcasted_iota(jnp.int32, (16, WIDTH), 0) == line - start
@@ -209,7 +193,6 @@
         more = [ninth[:, c * TOK : (c + 1) * TOK] for c in range(6)]
         block = jnp.concatenate(lanes + [jnp.concatenate(more + [spare], axis=0)], axis=0)
         ahead[half] = jnp.concatenate([block] * 8, axis=0).astype(BF)
-    back.wait()
 
 
 def prepare_call(*operands, interpret=False):
@@ -221,8 +204,8 @@
             jax.ShapeDtypeStruct((TOK // 2, TILE), BF),
         ),
         in_specs=[SMEM, VMEM] + [ANY] * 3,
-        out_specs=(ANY, VMEM, VMEM),
-        scratch_shapes=[pltpu.VMEM((PACK, WIDTH), BF), pltpu.SemaphoreType.DMA((4,))],
+        out_specs=(VMEM,) * 3,
+        scratch_shapes=[pltpu.SemaphoreType.DMA((3,))],
         compiler_params=room(62),
         interpret=interpret,
     )(*operands)
@@ -246,8 +229,8 @@
             jnp.concatenate(
                 [
                     dot(picks[0], theirs, NN),
+                    dot(picks[2], theirs, NN)[0:8],
                     dot(picks[1], ours, NN),
-                    dot(picks[2], theirs, NN)[0:8],
                 ],
                 axis=0,
             )
@@ -276,7 +259,7 @@
             jax.ShapeDtypeStruct((WIDTH, 384), BF),
             jax.ShapeDtypeStruct((1, WIDTH), F32),
         ),
-        in_specs=[SMEM] + [ANY] * 5,
+        in_specs=[SMEM] + [ANY] * 6,
         out_specs=(VMEM,) * 3,
         scratch_shapes=[
             pltpu.VMEM((24, 32, TILE), BF),
@@ -294,7 +277,7 @@
     return pl.pallas_call(
         layer_kernel,
         out_shape=(jax.ShapeDtypeStruct((TOK, WIDTH), F32), part, sent),
-        in_specs=[SMEM] + [VMEM] * 3 + [ANY] * 6 + [VMEM],
+        in_specs=[SMEM] + [VMEM] * 3 + [ANY] * 4 + [VMEM],
         out_specs=(VMEM,) * 3,
         scratch_shapes=[
             pltpu.VMEM((6, 64, WIDTH), BF),
@@ -303,7 +286,7 @@
             pltpu.VMEM((WIDTH, WIDTH), BF),
             pltpu.VMEM((2 * WIDTH, WIDTH), BF),
             pltpu.VMEM((WIDTH, TOK), BF),
-            pltpu.SemaphoreType.DMA((11,)),
+            pltpu.SemaphoreType.DMA((9,)),
         ],
         compiler_params=room(40),
         interpret=interpret,
@@ -327,23 +310,21 @@
     zl = lax.axis_index("zl")
     zh, core = lax.axis_index("zh"), lax.axis_index("core")
     w_out = w_out.T
-    scal = jnp.stack([count, zh, core, yx * 64 + zl * 8]).astype(jnp.int32)
+    piece = yx * 72
+    scal = jnp.stack([count, zh, core, piece + zl * 8, piece + 64 + zl]).astype(jnp.int32)
     own, ahead, even = prepare_call(scal, rows, w_in, w_qkv.T, w_out)
     line = lax.all_to_all(ahead.reshape(16, 56, TOK), Z, 0, 0, tiled=True)
     mate = swap(own, "core")
     partner = lax.ppermute(even, "zl", [(i, i ^ 1) for i in range(8)])
     line, mate, partner = lax.optimization_barrier((line.reshape(2, 448, TOK), mate, partner))
     got = lax.all_to_all(split_call(scal, line), YX, 0, 0, tiled=True)
-    over_rest = got[:, 128:].reshape(128, WIDTH)
-    cross, cross_rest = swap(got[:, :64], "core"), swap(over_rest, "core")
+    over, far = got[:, :72].reshape(18, 64, WIDTH), got[:, 72:]
+    cross = swap(over, "core")
     own, mate = own.reshape(18, 64, WIDTH), mate.reshape(18, 64, WIDTH)
     state = begin_call(
-        scal, rows.reshape(4, 32, TILE), partner.reshape(2, 32, TILE), own, mate, got
-    )
-    over_rest, cross_rest = over_rest.reshape(2, 64, WIDTH), cross_rest.reshape(2, 64, WIDTH)
-    out, keep, send = layer_call(
-        scal, *state, own, mate, got, cross, over_rest, cross_rest, cotangent[0]
-    )
+        scal, rows.reshape(4, 32, TILE), partner.reshape(2, 32, TILE), own, mate, over, far
+    )
+    out, keep, send = layer_call(scal, *state, own, mate, over, cross, cotangent[0])
     pair = (keep + swap(send, "core").astype(F32)).astype(BF)
     plane = lax.all_to_all(pair, YX, 0, 0, tiled=True)
     plane = jnp.sum(plane.astype(F32), axis=0).astype(BF)

time: 175 us -> 172 us (0.983)
  starting transfers between devices: 26.4 us -> 24.5 us
    ppermute x4 -> x3, starting transfers between devices: 8.3 us -> 6.37 us  [swap(): return lax.ppermute(value, axis, [(0, 1), (1, 0)])]
  transfers between devices with their start and end apart: 6 -> 5, of which waited for: 2 -> 2; matrix products, arithmetic and copies ran while one was open for 0% -> 0% of each run, Pallas kernels for 2% -> 2%
where the time goes in v10:
time: 172 us
  blocking collectives  107 us (62%)
  starting transfers between devices  24.5 us (14%)
  Pallas kernels  21.7 us (13%)
  waiting for transfers between devices  14.7 us (9%)
  local copies, waits for them, and re-layouts  2.18 us (1%)
    all_to_all x1, blocking collectives, shards(): got = lax.all_to_all(split_call(scal, line), YX, 0, 0, tiled=True)  48.4 us
    all_to_all x1, blocking collectives, shards(): column = lax.all_to_all(column, Z, 0, 0, tiled=True)  30.4 us
    all_to_all x1, blocking collectives, shards(): plane = lax.all_to_all(pair, YX, 0, 0, tiled=True)  15.8 us
    all_to_all x1, starting transfers between devices, shards(): line = lax.all_to_all(ahead.reshape(16, 56, TOK), Z, 0, 0, tiled=True)  14.8 us
    pallas_call x1, Pallas kernels, layer_call(): pl.pallas_call(layer_kernel, out_shape=(jax.ShapeDtypeStruct((TOK, WIDTH)...  13.1 us
    ppermute x1, waiting for transfers between devices, shards(): partner = lax.ppermute(even, 'zl', [(i, i ^ 1) for i in range(8)])  13.1 us
    all_to_all x1, blocking collectives, spread(): lax.all_to_all(jnp.broadcast_to(block[None], (size,) + block.shape), axes...  12.1 us
    ppermute x3, starting transfers between devices, swap(): return lax.ppermute(value, axis, [(0, 1), (1, 0)])  6.37 us
  transfers between devices with their start and end apart: 5, of which 2 were waited for; matrix products, arithmetic and copies ran while one was open for 0% of the time, Pallas kernels for 2%

profile of v10, /device:TPU:64, one launch (start us, length us, event | category | flops | bytes accessed | tf_op | source)
XLA Modules:
  0.0 171.6 jit_solution(2991479691033995408)
XLA Ops:
  1.3 0.7 stack.19.scal
  2.0 3.8 %shard_map.77 = (bf16[1152,768]{1,0:T(8,128)(2,1)}, bf16[2,448,128]{2,1,0:T(8,128)(2,1)}, bf16[64,1536]{1,0:T(8,128)(2,1)}) custom-call(s32[5]{0:T(128)} %stack.19.scal, bf16[128,1536]{1,0:T(8,128)(2,1)} %bitcast.33, bf16[384,768]{1,0:T(8,128)(2,1)} %w_in.1, bf16[576,768]{1,0:T(8,128)(2,1)} %bitcast.41, bf16[192,768]{1,0:T(8,128)(2,1)} %bitcast.43), custom_call_target="tpu_custom_call" | custom-call | tf_op jit(solution)/shard_map/pallas_call | solution.py:199
  5.8 1.9 %collective-permute-start = (bf16[1152,768]{1,0:T(8,128)(2,1)}, bf16[1152,768]{1,0:T(8,128)(2,1)S(1)}, u32[]{:S(2)}, u32[]{:S(2)}) collective-permute-start(bf16[1152,768]{1,0:T(8,128)(2,1)} %get-tuple-element.15), channel_id=1, source_target_pairs={{0,1},{1,0},{2,3},{3,2},{4,5},{5,4},{6,7},{7,6},{8,9},{9,8},{10,11... | collective-permute-start | bytes 5308424 | tf_op jit(solution)/shard_map/ppermute | solution.py:303
  7.7 14.8 %all-to-all-start = ((bf16[16,56,128]{2,1,0:T(8,128)(2,1)}), bf16[16,56,128]{2,1,0:T(8,128)(2,1)S(1)}, u32[]{:S(2)}, u32[]{:S(2)}) async-start(bf16[16,56,128]{2,1,0:T(8,128)(2,1)} %bitcast.44), calls=%async_computation | async-start | bytes 458752 | tf_op jit(solution)/shard_map/all_to_all | solution.py:316
  22.4 3.4 %collective-permute-start.1 = (bf16[64,1536]{1,0:T(8,128)(2,1)}, bf16[64,1536]{1,0:T(8,128)(2,1)S(1)}, u32[]{:S(2)}, u32[]{:S(2)}) collective-permute-start(bf16[64,1536]{1,0:T(8,128)(2,1)} %get-tuple-element.16), channel_id=1, source_target_pairs={{0,4},{4,0},{8,12},{12,8},{16,20},{20,16},{24,28},{28,24},{1,5},{5... | collective-permute-start | bytes 589832 | tf_op jit(solution)/shard_map/ppermute | solution.py:318
  25.8 13.1 %collective-permute-done.1 = bf16[64,1536]{1,0:T(8,128)(2,1)S(1)} collective-permute-done((bf16[64,1536]{1,0:T(8,128)(2,1)}, bf16[64,1536]{1,0:T(8,128)(2,1)S(1)}, u32[]{:S(2)}, u32[]{:S(2)}) %collective-permute-start.1) | collective-permute-done | bytes 196640 | tf_op jit(solution)/shard_map/ppermute | solution.py:318
  38.9 0.0 all-to-all-done
  38.9 0.0 collective-permute-done
  38.9 0.0 copy-done.3
  38.9 1.2 shard_map.78
  40.1 48.4 %all_to_all.25 = bf16[16,136,768]{2,1,0:T(8,128)(2,1)S(1)} all-to-all(bf16[16,136,768]{2,1,0:T(8,128)(2,1)S(1)} %shard_map.78), channel_id=1, replica_groups=mesh['y'=4,'x'=4,'zl'=8,'zh'=2,'core'=2] {'y','x'}, dimensions={0} | all-to-all | bytes 6684672 | tf_op jit(solution)/shard_map/all_to_all | solution.py:320
  88.5 0.1 slice.8
  88.6 0.0 copy-start
  88.6 0.0 copy-start.1
  88.6 2.1 %collective-permute-start.2 = (bf16[18,64,768]{2,1,0:T(8,128)(2,1)S(1)}, bf16[18,64,768]{2,1,0:T(8,128)(2,1)S(1)}, u32[]{:S(2)}, u32[]{:S(2)}) collective-permute-start(bf16[18,64,768]{2,1,0:T(8,128)(2,1)S(1)} %bitcast.26), channel_id=1, source_target_pairs={{0,1},{1,0},{2,3},{3,2},{4,5},{5,4},{6,7},{7,6},{8,9},{9,8},{10,11... | collective-permute-start | bytes 5308424 | tf_op jit(solution)/shard_map/ppermute | solution.py:303
  90.7 0.2 slice.9.far
  90.8 0.0 copy-done
  90.9 0.0 copy-done.1
  90.9 0.0 copy-start.2
  90.9 3.6 %shard_map.79 = (f32[768,768]{1,0:T(8,128)S(1)}, bf16[768,384]{1,0:T(8,128)(2,1)S(1)}, f32[1,768]{1,0:T(1,128)S(1)}) custom-call(s32[5]{0:T(128)S(1)} %copy-done.3, bf16[4,32,1536]{2,1,0:T(8,128)(2,1)S(1)} %bitcast.34, bf16[2,32,1536]{2,1,0:T(8,128)(2,1)S(1)} %bitcast.37, bf16[18,64,768]{2,1,0:T(8,128)(2,1)S(1)} %bitcast.29, ...), custom_call_target="tpu_custom_call" | custom-call | tf_op jit(solution)/shard_map/pallas_call | solution.py:255
  94.5 0.0 collective-permute-done.2.cross
  94.5 0.0 copy-done.2
  94.5 13.1 %shard_map.80 = (f32[128,768]{1,0:T(8,128)}, f32[16,2,24,384]{3,2,1,0:T(8,128)S(1)}, bf16[16,2,24,384]{3,2,1,0:T(8,128)(2,1)S(1)}) custom-call(s32[5]{0:T(128)S(1)} %copy-done.3, f32[768,768]{1,0:T(8,128)S(1)} %get-tuple-element.20.partial, bf16[768,384]{1,0:T(8,128)(2,1)S(1)} %get-tuple-element.21.last, f32[1,768]{1,0:T(1,128)S(1)} %get-tuple-element.22.key_bias_row, ...), custom_call_target="tpu_custom_call" | custom-call | tf_op jit(solution)/shard_map/pallas_call | solution.py:277
  107.6 2.4 %collective-permute-start.3 = (bf16[16,2,24,384]{3,2,1,0:T(8,128)(2,1)S(1)}, bf16[16,2,24,384]{3,2,1,0:T(8,128)(2,1)S(1)}, u32[]{:S(2)}, u32[]{:S(2)}) collective-permute-start(bf16[16,2,24,384]{3,2,1,0:T(8,128)(2,1)S(1)} %get-tuple-element.25), channel_id=1, source_target_pairs={{0,1},{1,0},{2,3},{3,2},{4,5},{5,4},{6,7},{7,6},{8,9},{9,8},{10,11... | collective-permute-start | bytes 1769480 | tf_op jit(solution)/shard_map/ppermute | solution.py:303
  110.0 1.6 collective-permute-done.3
  111.7 0.1 add_convert_fusion
  111.8 15.8 %all_to_all.26 = bf16[16,2,24,384]{3,2,1,0:T(8,128)(2,1)S(1)} all-to-all(bf16[16,2,24,384]{3,2,1,0:T(8,128)(2,1)S(1)} %add_convert_fusion), channel_id=1, replica_groups=mesh['y'=4,'x'=4,'zl'=8,'zh'=2,'core'=2] {'y','x'}, dimensions={0} | all-to-all | bytes 1179648 | tf_op jit(solution)/shard_map/all_to_all | solution.py:329
  127.6 0.1 reduce_sum.24
  127.7 30.4 %all_to_all.27 = bf16[16,24,384]{2,1,0:T(8,128)(2,1)S(1)} all-to-all(bf16[16,24,384]{2,1,0:T(8,128)(2,1)S(1)} %bitcast.40), channel_id=1, replica_groups=mesh['y'=4,'x'=4,'zl'=8,'zh'=2,'core'=2] {'zh','zl'}, dimensions={0} | all-to-all | bytes 589824 | tf_op jit(solution)/shard_map/all_to_all | solution.py:332
  158.2 12.1 %all_to_all.28 = bf16[16,24,384]{2,1,0:T(8,128)(2,1)S(1)} all-to-all(bf16[16,24,384]{2,1,0:T(8,128)(2,1)S(1)} %broadcast_in_dim.8), channel_id=1, replica_groups=mesh['y'=4,'x'=4,'zl'=8,'zh'=2,'core'=2] {'y','x'}, dimensions={0} | all-to-all | bytes 589824 | tf_op jit(solution)/shard_map/all_to_all | solution.py:297
  170.4 0.3 copy.9
  170.7 0.9 copy.10
  (5 shorter events, 0.1 us)
Async XLA Ops:
  2.0 36.9 %copy-start.3 = (s32[5]{0:T(128)S(1)}, s32[5]{0:T(128)}, u32[]{:S(2)}) copy-start(s32[5]{0:T(128)} %stack.19.scal) | copy-start | bytes 64
  5.8 33.1 %collective-permute-start = (bf16[1152,768]{1,0:T(8,128)(2,1)}, bf16[1152,768]{1,0:T(8,128)(2,1)S(1)}, u32[]{:S(2)}, u32[]{:S(2)}) collective-permute-start(bf16[1152,768]{1,0:T(8,128)(2,1)} %get-tuple-element.15), channel_id=1, source_target_pairs={{0,1},{1,0},{2,3},{3,2},{4,5},{5,4},{6,7},{7,6},{8,9},{9,8},{10,11... | collective-permute-start | bytes 5308424 | tf_op jit(solution)/shard_map/ppermute | solution.py:303
  7.7 31.2 %all-to-all-start = ((bf16[16,56,128]{2,1,0:T(8,128)(2,1)}), bf16[16,56,128]{2,1,0:T(8,128)(2,1)S(1)}, u32[]{:S(2)}, u32[]{:S(2)}) async-start(bf16[16,56,128]{2,1,0:T(8,128)(2,1)} %bitcast.44), calls=%async_computation | async-start | bytes 458752 | tf_op jit(solution)/shard_map/all_to_all | solution.py:316
  22.4 16.4 %collective-permute-start.1 = (bf16[64,1536]{1,0:T(8,128)(2,1)}, bf16[64,1536]{1,0:T(8,128)(2,1)S(1)}, u32[]{:S(2)}, u32[]{:S(2)}) collective-permute-start(bf16[64,1536]{1,0:T(8,128)(2,1)} %get-tuple-element.16), channel_id=1, source_target_pairs={{0,4},{4,0},{8,12},{12,8},{16,20},{20,16},{24,28},{28,24},{1,5},{5... | collective-permute-start | bytes 589832 | tf_op jit(solution)/shard_map/ppermute | solution.py:318
  88.6 2.3 %copy-start = (bf16[1152,768]{1,0:T(8,128)(2,1)S(1)}, bf16[1152,768]{1,0:T(8,128)(2,1)}, u32[]{:S(2)}) copy-start(bf16[1152,768]{1,0:T(8,128)(2,1)} %get-tuple-element.15) | copy-start | bytes 5308420
  88.6 2.3 %copy-start.1 = (bf16[1,128,1536]{2,1,0:T(8,128)(2,1)S(1)}, bf16[1,128,1536]{2,1,0:T(8,128)(2,1)}, u32[]{:S(2)}) copy-start(bf16[1,128,1536]{2,1,0:T(8,128)(2,1)} %param.6) | copy-start | bytes 1179652
  88.6 5.9 %collective-permute-start.2 = (bf16[18,64,768]{2,1,0:T(8,128)(2,1)S(1)}, bf16[18,64,768]{2,1,0:T(8,128)(2,1)S(1)}, u32[]{:S(2)}, u32[]{:S(2)}) collective-permute-start(bf16[18,64,768]{2,1,0:T(8,128)(2,1)S(1)} %bitcast.26), channel_id=1, source_target_pairs={{0,1},{1,0},{2,3},{3,2},{4,5},{5,4},{6,7},{7,6},{8,9},{9,8},{10,11... | collective-permute-start | bytes 5308424 | tf_op jit(solution)/shard_map/ppermute | solution.py:303
  90.9 3.6 %copy-start.2 = (bf16[1,128,768]{2,1,0:T(8,128)(2,1)S(1)}, bf16[1,128,768]{2,1,0:T(8,128)(2,1)}, u32[]{:S(2)}) copy-start(bf16[1,128,768]{2,1,0:T(8,128)(2,1)} %param.11) | copy-start | bytes 589828
  107.6 4.0 %collective-permute-start.3 = (bf16[16,2,24,384]{3,2,1,0:T(8,128)(2,1)S(1)}, bf16[16,2,24,384]{3,2,1,0:T(8,128)(2,1)S(1)}, u32[]{:S(2)}, u32[]{:S(2)}) collective-permute-start(bf16[16,2,24,384]{3,2,1,0:T(8,128)(2,1)S(1)} %get-tuple-element.25), channel_id=1, source_target_pairs={{0,1},{1,0},{2,3},{3,2},{4,5},{5,4},{6,7},{7,6},{8,9},{9,8},{10,11... | collective-permute-start | bytes 1769480 | tf_op jit(solution)/shard_map/ppermute | solution.py:303

commit v11 on v10

--- a/solution.py
+++ b/solution.py
@@ -331,8 +331,8 @@
     column = jnp.broadcast_to(plane[:, None], (2, 8, 24, 384)).reshape(16, 24, 384)
     column = lax.all_to_all(column, Z, 0, 0, tiled=True)
     total = jnp.sum(column.astype(F32), axis=0)
-    whole = spread(total.astype(BF), YX, 16).astype(F32)
-    grad = whole.reshape(8, 2, 24, 384).transpose(0, 2, 1, 3).reshape(192, WIDTH)
+    whole = spread(total.astype(BF), YX, 16).reshape(8, 2, 24, 384)
+    grad = jnp.concatenate([whole[:, 0], whole[:, 1]], axis=2).astype(F32).reshape(192, WIDTH)
     return (out[None], grad)
 
 

time: 172 us -> 172 us (level)
  no operation moved by 1% of the time
where the time goes in v11:
time: 172 us; the launch traced here: 171 us
  blocking collectives  107 us (62%)
  starting transfers between devices  24.5 us (14%)
  Pallas kernels  21.7 us (13%)
  waiting for transfers between devices  14.7 us (9%)
    all_to_all x1, blocking collectives, shards(): got = lax.all_to_all(split_call(scal, line), YX, 0, 0, tiled=True)  48.4 us
    all_to_all x1, blocking collectives, shards(): column = lax.all_to_all(column, Z, 0, 0, tiled=True)  30.4 us
    all_to_all x1, blocking collectives, shards(): plane = lax.all_to_all(pair, YX, 0, 0, tiled=True)  15.8 us
    all_to_all x1, starting transfers between devices, shards(): line = lax.all_to_all(ahead.reshape(16, 56, TOK), Z, 0, 0, tiled=True)  14.8 us
    pallas_call x1, Pallas kernels, layer_call(): pl.pallas_call(layer_kernel, out_shape=(jax.ShapeDtypeStruct((TOK, WIDTH)...  13.1 us
    ppermute x1, waiting for transfers between devices, shards(): partner = lax.ppermute(even, 'zl', [(i, i ^ 1) for i in range(8)])  13.1 us
    all_to_all x1, blocking collectives, spread(): lax.all_to_all(jnp.broadcast_to(block[None], (size,) + block.shape), axes...  12.1 us
    ppermute x3, starting transfers between devices, swap(): return lax.ppermute(value, axis, [(0, 1), (1, 0)])  6.37 us
  transfers between devices with their start and end apart: 5, of which 2 were waited for; matrix products, arithmetic and copies ran while one was open for 0% of the time, Pallas kernels for 2%

profile of v11, /device:TPU:64, one launch (start us, length us, event | category | flops | bytes accessed | tf_op | source)
XLA Modules:
  0.0 171.1 jit_solution(15468761650257337600)
XLA Ops:
  1.3 0.6 stack.19.scal
  1.9 0.0 copy-start.3
  1.9 3.8 %shard_map.77 = (bf16[1152,768]{1,0:T(8,128)(2,1)}, bf16[2,448,128]{2,1,0:T(8,128)(2,1)}, bf16[64,1536]{1,0:T(8,128)(2,1)}) custom-call(s32[5]{0:T(128)} %stack.19.scal, bf16[128,1536]{1,0:T(8,128)(2,1)} %bitcast.29, bf16[384,768]{1,0:T(8,128)(2,1)} %w_in.1, bf16[576,768]{1,0:T(8,128)(2,1)} %bitcast.36, bf16[192,768]{1,0:T(8,128)(2,1)} %bitcast.39), custom_call_target="tpu_custom_call" | custom-call | tf_op jit(solution)/shard_map/pallas_call | solution.py:199
  5.6 1.9 %collective-permute-start = (bf16[1152,768]{1,0:T(8,128)(2,1)}, bf16[1152,768]{1,0:T(8,128)(2,1)S(1)}, u32[]{:S(2)}, u32[]{:S(2)}) collective-permute-start(bf16[1152,768]{1,0:T(8,128)(2,1)} %get-tuple-element.15), channel_id=1, source_target_pairs={{0,1},{1,0},{2,3},{3,2},{4,5},{5,4},{6,7},{7,6},{8,9},{9,8},{10,11... | collective-permute-start | bytes 5308424 | tf_op jit(solution)/shard_map/ppermute | solution.py:303
  7.6 14.8 %all-to-all-start = ((bf16[16,56,128]{2,1,0:T(8,128)(2,1)}), bf16[16,56,128]{2,1,0:T(8,128)(2,1)S(1)}, u32[]{:S(2)}, u32[]{:S(2)}) async-start(bf16[16,56,128]{2,1,0:T(8,128)(2,1)} %bitcast.40), calls=%async_computation | async-start | bytes 458752 | tf_op jit(solution)/shard_map/all_to_all | solution.py:316
  22.3 3.4 %collective-permute-start.1 = (bf16[64,1536]{1,0:T(8,128)(2,1)}, bf16[64,1536]{1,0:T(8,128)(2,1)S(1)}, u32[]{:S(2)}, u32[]{:S(2)}) collective-permute-start(bf16[64,1536]{1,0:T(8,128)(2,1)} %get-tuple-element.16), channel_id=1, source_target_pairs={{0,4},{4,0},{8,12},{12,8},{16,20},{20,16},{24,28},{28,24},{1,5},{5... | collective-permute-start | bytes 589832 | tf_op jit(solution)/shard_map/ppermute | solution.py:318
  25.7 13.1 %collective-permute-done.1 = bf16[64,1536]{1,0:T(8,128)(2,1)S(1)} collective-permute-done((bf16[64,1536]{1,0:T(8,128)(2,1)}, bf16[64,1536]{1,0:T(8,128)(2,1)S(1)}, u32[]{:S(2)}, u32[]{:S(2)}) %collective-permute-start.1) | collective-permute-done | bytes 196640 | tf_op jit(solution)/shard_map/ppermute | solution.py:318
  38.8 0.0 all-to-all-done
  38.8 0.0 collective-permute-done
  38.8 0.0 copy-done.3
  38.8 1.2 shard_map.78
  40.0 48.4 %all_to_all.25 = bf16[16,136,768]{2,1,0:T(8,128)(2,1)S(1)} all-to-all(bf16[16,136,768]{2,1,0:T(8,128)(2,1)S(1)} %shard_map.78), channel_id=1, replica_groups=mesh['y'=4,'x'=4,'zl'=8,'zh'=2,'core'=2] {'y','x'}, dimensions={0} | all-to-all | bytes 6684672 | tf_op jit(solution)/shard_map/all_to_all | solution.py:320
  88.4 0.1 slice.16
  88.5 0.0 copy-start
  88.5 0.0 copy-start.1
  88.5 2.1 %collective-permute-start.2 = (bf16[18,64,768]{2,1,0:T(8,128)(2,1)S(1)}, bf16[18,64,768]{2,1,0:T(8,128)(2,1)S(1)}, u32[]{:S(2)}, u32[]{:S(2)}) collective-permute-start(bf16[18,64,768]{2,1,0:T(8,128)(2,1)S(1)} %bitcast.22), channel_id=1, source_target_pairs={{0,1},{1,0},{2,3},{3,2},{4,5},{5,4},{6,7},{7,6},{8,9},{9,8},{10,11... | collective-permute-start | bytes 5308424 | tf_op jit(solution)/shard_map/ppermute | solution.py:303
  90.6 0.2 slice.17.far
  90.7 0.0 copy-done
  90.8 0.0 copy-done.1
  90.8 0.0 copy-start.2
  90.8 3.6 %shard_map.79 = (f32[768,768]{1,0:T(8,128)S(1)}, bf16[768,384]{1,0:T(8,128)(2,1)S(1)}, f32[1,768]{1,0:T(1,128)S(1)}) custom-call(s32[5]{0:T(128)S(1)} %copy-done.3, bf16[4,32,1536]{2,1,0:T(8,128)(2,1)S(1)} %bitcast.30, bf16[2,32,1536]{2,1,0:T(8,128)(2,1)S(1)} %bitcast.33, bf16[18,64,768]{2,1,0:T(8,128)(2,1)S(1)} %bitcast.25, ...), custom_call_target="tpu_custom_call" | custom-call | tf_op jit(solution)/shard_map/pallas_call | solution.py:255
  94.4 0.0 collective-permute-done.2.cross
  94.4 0.0 copy-done.2
  94.4 13.1 %shard_map.80 = (f32[128,768]{1,0:T(8,128)}, f32[16,2,24,384]{3,2,1,0:T(8,128)S(1)}, bf16[16,2,24,384]{3,2,1,0:T(8,128)(2,1)S(1)}) custom-call(s32[5]{0:T(128)S(1)} %copy-done.3, f32[768,768]{1,0:T(8,128)S(1)} %get-tuple-element.20.partial, bf16[768,384]{1,0:T(8,128)(2,1)S(1)} %get-tuple-element.21.last, f32[1,768]{1,0:T(1,128)S(1)} %get-tuple-element.22.key_bias_row, ...), custom_call_target="tpu_custom_call" | custom-call | tf_op jit(solution)/shard_map/pallas_call | solution.py:277
  107.5 2.4 %collective-permute-start.3 = (bf16[16,2,24,384]{3,2,1,0:T(8,128)(2,1)S(1)}, bf16[16,2,24,384]{3,2,1,0:T(8,128)(2,1)S(1)}, u32[]{:S(2)}, u32[]{:S(2)}) collective-permute-start(bf16[16,2,24,384]{3,2,1,0:T(8,128)(2,1)S(1)} %get-tuple-element.25), channel_id=1, source_target_pairs={{0,1},{1,0},{2,3},{3,2},{4,5},{5,4},{6,7},{7,6},{8,9},{9,8},{10,11... | collective-permute-start | bytes 1769480 | tf_op jit(solution)/shard_map/ppermute | solution.py:303
  109.9 1.6 collective-permute-done.3
  111.6 0.1 add_convert_fusion
  111.7 15.8 %all_to_all.26 = bf16[16,2,24,384]{3,2,1,0:T(8,128)(2,1)S(1)} all-to-all(bf16[16,2,24,384]{3,2,1,0:T(8,128)(2,1)S(1)} %add_convert_fusion), channel_id=1, replica_groups=mesh['y'=4,'x'=4,'zl'=8,'zh'=2,'core'=2] {'y','x'}, dimensions={0} | all-to-all | bytes 1179648 | tf_op jit(solution)/shard_map/all_to_all | solution.py:329
  127.5 0.1 reduce_sum.24
  127.6 30.4 %all_to_all.27 = bf16[16,24,384]{2,1,0:T(8,128)(2,1)S(1)} all-to-all(bf16[16,24,384]{2,1,0:T(8,128)(2,1)S(1)} %bitcast.35), channel_id=1, replica_groups=mesh['y'=4,'x'=4,'zl'=8,'zh'=2,'core'=2] {'zh','zl'}, dimensions={0} | all-to-all | bytes 589824 | tf_op jit(solution)/shard_map/all_to_all | solution.py:332
  158.1 12.1 %all_to_all.28 = bf16[16,24,384]{2,1,0:T(8,128)(2,1)S(1)} all-to-all(bf16[16,24,384]{2,1,0:T(8,128)(2,1)S(1)} %broadcast_in_dim.8), channel_id=1, replica_groups=mesh['y'=4,'x'=4,'zl'=8,'zh'=2,'core'=2] {'y','x'}, dimensions={0} | all-to-all | bytes 589824 | tf_op jit(solution)/shard_map/all_to_all | solution.py:297
  170.3 0.9 maximum_convert_fusion
  (4 shorter events, 0.1 us)
Async XLA Ops:
  1.9 36.9 %copy-start.3 = (s32[5]{0:T(128)S(1)}, s32[5]{0:T(128)}, u32[]{:S(2)}) copy-start(s32[5]{0:T(128)} %stack.19.scal) | copy-start | bytes 64
  5.6 33.1 %collective-permute-start = (bf16[1152,768]{1,0:T(8,128)(2,1)}, bf16[1152,768]{1,0:T(8,128)(2,1)S(1)}, u32[]{:S(2)}, u32[]{:S(2)}) collective-permute-start(bf16[1152,768]{1,0:T(8,128)(2,1)} %get-tuple-element.15), channel_id=1, source_target_pairs={{0,1},{1,0},{2,3},{3,2},{4,5},{5,4},{6,7},{7,6},{8,9},{9,8},{10,11... | collective-permute-start | bytes 5308424 | tf_op jit(solution)/shard_map/ppermute | solution.py:303
  7.6 31.2 %all-to-all-start = ((bf16[16,56,128]{2,1,0:T(8,128)(2,1)}), bf16[16,56,128]{2,1,0:T(8,128)(2,1)S(1)}, u32[]{:S(2)}, u32[]{:S(2)}) async-start(bf16[16,56,128]{2,1,0:T(8,128)(2,1)} %bitcast.40), calls=%async_computation | async-start | bytes 458752 | tf_op jit(solution)/shard_map/all_to_all | solution.py:316
  22.3 16.4 %collective-permute-start.1 = (bf16[64,1536]{1,0:T(8,128)(2,1)}, bf16[64,1536]{1,0:T(8,128)(2,1)S(1)}, u32[]{:S(2)}, u32[]{:S(2)}) collective-permute-start(bf16[64,1536]{1,0:T(8,128)(2,1)} %get-tuple-element.16), channel_id=1, source_target_pairs={{0,4},{4,0},{8,12},{12,8},{16,20},{20,16},{24,28},{28,24},{1,5},{5... | collective-permute-start | bytes 589832 | tf_op jit(solution)/shard_map/ppermute | solution.py:318
  88.5 2.3 %copy-start = (bf16[1152,768]{1,0:T(8,128)(2,1)S(1)}, bf16[1152,768]{1,0:T(8,128)(2,1)}, u32[]{:S(2)}) copy-start(bf16[1152,768]{1,0:T(8,128)(2,1)} %get-tuple-element.15) | copy-start | bytes 5308420
  88.5 2.3 %copy-start.1 = (bf16[1,128,1536]{2,1,0:T(8,128)(2,1)S(1)}, bf16[1,128,1536]{2,1,0:T(8,128)(2,1)}, u32[]{:S(2)}) copy-start(bf16[1,128,1536]{2,1,0:T(8,128)(2,1)} %param.6) | copy-start | bytes 1179652
  88.5 5.9 %collective-permute-start.2 = (bf16[18,64,768]{2,1,0:T(8,128)(2,1)S(1)}, bf16[18,64,768]{2,1,0:T(8,128)(2,1)S(1)}, u32[]{:S(2)}, u32[]{:S(2)}) collective-permute-start(bf16[18,64,768]{2,1,0:T(8,128)(2,1)S(1)} %bitcast.22), channel_id=1, source_target_pairs={{0,1},{1,0},{2,3},{3,2},{4,5},{5,4},{6,7},{7,6},{8,9},{9,8},{10,11... | collective-permute-start | bytes 5308424 | tf_op jit(solution)/shard_map/ppermute | solution.py:303
  90.8 3.6 %copy-start.2 = (bf16[1,128,768]{2,1,0:T(8,128)(2,1)S(1)}, bf16[1,128,768]{2,1,0:T(8,128)(2,1)}, u32[]{:S(2)}) copy-start(bf16[1,128,768]{2,1,0:T(8,128)(2,1)} %param.11) | copy-start | bytes 589828
  107.5 4.0 %collective-permute-start.3 = (bf16[16,2,24,384]{3,2,1,0:T(8,128)(2,1)S(1)}, bf16[16,2,24,384]{3,2,1,0:T(8,128)(2,1)S(1)}, u32[]{:S(2)}, u32[]{:S(2)}) collective-permute-start(bf16[16,2,24,384]{3,2,1,0:T(8,128)(2,1)S(1)} %get-tuple-element.25), channel_id=1, source_target_pairs={{0,1},{1,0},{2,3},{3,2},{4,5},{5,4},{6,7},{7,6},{8,9},{9,8},{10,11... | collective-permute-start | bytes 1769480 | tf_op jit(solution)/shard_map/ppermute | solution.py:303
